TPU v7x, 256 devices: a whole 4x4x8 slice. The times are simulated.
256 devices in a mesh: leaf: 256 (over z, x, y, core).
Axes of the slice: x: 4, y: 4, z: 8, core: 2. Of those that a mesh axis runs over, the one named last changes fastest.
Arguments:
- charges: bfloat16 [16, 2097152], P(None, 'leaf'), may hold values from -6 to 6
- points: bfloat16 [3, 2097152], P(None, 'leaf'), may hold values from 0 to 1
- leaf_basis: bfloat16 [2048, 1024, 128], P('leaf'), may hold values from -0.1875 to 0.1875
- transfer: float32 [4, 2, 128, 128], replicated, may hold values from -0.375 to 0.375
- coupling: float32 [4, 3, 128, 128], replicated, may hold values from -0.5 to 0.5
- near_list: int32 [2048, 5], P('leaf'), may hold values from 0 to 2047, as said below
- couple_flags: int32 [256, 4, 3], P('leaf'), may hold values from 0 to 1, as said below
Outputs:
- potential: bfloat16 [16, 2097152], P(None, 'leaf')
Inputs may be any that keep to these rules, and one draw needn't show every extreme that they name: `near_list`: entries of a row are distinct leaves within 32 of the row's leaf i; the first is i itself and the second lies exactly 32 away from i. `couple_flags`: at level t the flags are equal for all clusters c with equal c // 2^t.
All inputs are finite; a program needn't handle non-finite values.
Results may differ from a plain program's by a relative error of at most 0.0049.
Values may be sent and summed in bfloat16 or wider, within the bound.
No kernel may reach another device: no remote copies, remote signals or barrier semaphores. Data moves between devices by JAX's collectives and lax.ppermute only.
A program may use at most 64 MiB of HBM per device.

v0:
```python
import math

import jax
import jax.numpy as jnp
from jax import lax
from jax.sharding import PartitionSpec as P

smoothing_sq = 0.01


def passed_along(block, axis, distance):
    devices = range(lax.axis_size(axis))
    route = [(i - distance, i) for i in devices if i - distance in devices]
    return lax.ppermute(block, axis, route)


def from_partner(array, axis, apart):
    return lax.ppermute(array, axis, [(i, i ^ 1 << apart) for i in range(lax.axis_size(axis))])


def positions(raw, leaf_num, leaf_step):
    coords = raw.astype(jnp.float32)
    return jnp.stack([coords[0] + leaf_num * leaf_step, coords[1], coords[2]], axis=0)


def kernel_block(src_pos, tgt_pos):
    diff_x = src_pos[0][:, None] - tgt_pos[0][None, :]
    diff_y = src_pos[1][:, None] - tgt_pos[1][None, :]
    diff_z = src_pos[2][:, None] - tgt_pos[2][None, :]
    dist_sq = diff_x * diff_x + diff_y * diff_y + diff_z * diff_z
    return lax.rsqrt(dist_sq + smoothing_sq).astype(jnp.bfloat16)


def local(charges, points, leaf_basis, transfer, coupling, near_list, couple_flags):
    highest = lax.Precision.HIGHEST
    device_id = lax.axis_index("leaf")
    leaves_dev = leaf_basis.shape[0]
    leaf_rows = leaf_basis.shape[1]
    rhs_count = charges.shape[0]
    cluster_rows = leaves_dev * leaf_rows
    levels = transfer.shape[0]
    neighbours = near_list.shape[1]
    reach = 4
    leaf_step = 1.0 / (2.0 * reach * leaves_dev)
    pieces = {0: (charges, points)}
    for offset in range(-reach, reach + 1):
        if offset != 0:
            pieces[offset] = passed_along((charges, points), "leaf", -offset)
    window_vals = jnp.concatenate([pieces[o][0] for o in range(-reach, reach + 1)], axis=1)
    window_pos = jnp.concatenate([pieces[o][1] for o in range(-reach, reach + 1)], axis=1)
    base_leaf = (device_id - reach) * leaves_dev

    def near_leaf(a, accumulated):
        global_leaf = device_id * leaves_dev + a
        tgt_pos = positions(
            lax.dynamic_slice(points, (jnp.int32(0), a * leaf_rows), (3, leaf_rows)),
            global_leaf.astype(jnp.float32),
            leaf_step,
        )
        row_list = lax.dynamic_index_in_dim(near_list, a, 0, keepdims=False)
        near_sum = jnp.zeros((rhs_count, leaf_rows), jnp.float32)
        for k in range(neighbours):
            j = row_list[k]
            start = (j - base_leaf) * leaf_rows
            src_pos = positions(
                lax.dynamic_slice(window_pos, (jnp.int32(0), start), (3, leaf_rows)),
                j.astype(jnp.float32),
                leaf_step,
            )
            src_vals = lax.dynamic_slice(window_vals, (jnp.int32(0), start), (rhs_count, leaf_rows))
            near_sum = near_sum + jnp.dot(
                src_vals, kernel_block(src_pos, tgt_pos), preferred_element_type=jnp.float32
            )
        return lax.dynamic_update_slice(accumulated, near_sum, (jnp.int32(0), a * leaf_rows))

    near_field = lax.fori_loop(
        0, leaves_dev, near_leaf, jnp.zeros((rhs_count, cluster_rows), jnp.float32)
    )
    basis_rows = leaf_basis.reshape(cluster_rows, leaf_basis.shape[2])
    first_coef = jnp.dot(charges, basis_rows, preferred_element_type=jnp.float32)
    flag_vals = couple_flags[0].astype(jnp.float32)
    coupled_levels = []
    own_coef = first_coef
    sib_coef = from_partner(first_coef, "leaf", 0)
    for t in range(levels):
        child_side = device_id // 2**t % 2
        cousin_even, cousin_odd = from_partner((own_coef, sib_coef), "leaf", t + 1)
        partners = (sib_coef, cousin_even, cousin_odd)
        coupled = jnp.zeros(first_coef.shape, jnp.float32)
        for m in range(3):
            product = jnp.dot(
                partners[m], coupling[t, m], precision=highest, preferred_element_type=jnp.float32
            )
            coupled = coupled + flag_vals[t, m] * product
        coupled_levels.append(coupled)
        if t + 1 < levels:

            def merge_children(first_child, second_child):
                left_coef = jnp.where(child_side == 0, first_child, second_child)
                right_coef = jnp.where(child_side == 0, second_child, first_child)
                return jnp.dot(
                    left_coef, transfer[t, 0], precision=highest, preferred_element_type=jnp.float32
                ) + jnp.dot(
                    right_coef,
                    transfer[t, 1],
                    precision=highest,
                    preferred_element_type=jnp.float32,
                )

            own_coef, sib_coef = (
                merge_children(own_coef, sib_coef),
                merge_children(cousin_even, cousin_odd),
            )
    local_coef = coupled_levels[-1]
    for t in range(levels - 1, 0, -1):
        child_side = device_id // 2 ** (t - 1) % 2
        transfer_mat = lax.dynamic_index_in_dim(transfer[t - 1], child_side, 0, keepdims=False)
        local_coef = coupled_levels[t - 1] + lax.dot_general(
            local_coef,
            transfer_mat,
            (((1,), (1,)), ((), ())),
            precision=highest,
            preferred_element_type=jnp.float32,
        )
    local_bf = local_coef.astype(jnp.bfloat16)
    far_field = lax.dot_general(
        local_bf, basis_rows, (((1,), (1,)), ((), ())), preferred_element_type=jnp.float32
    )
    near_scale = 1.0 / math.sqrt(neighbours * leaf_rows)
    return (near_field * near_scale + far_field).astype(jnp.bfloat16)


def solution(mesh):
    return jax.shard_map(
        local,
        mesh=mesh,
        in_specs=(
            P(None, "leaf"),
            P(None, "leaf"),
            P("leaf", None, None),
            P(),
            P(),
            P("leaf", None),
            P("leaf", None, None),
        ),
        out_specs=P(None, "leaf"),
        check_vma=False,
    )
```

profile of v0, /device:TPU:127, one launch (start us, length us, event | category | flops | bytes accessed | tf_op | source)
XLA Modules:
  0.0 342.3 jit_solution(4331388721869198919)
XLA Ops:
  4.2 5.0 %collective-permute-start = (bf16[16,8192]{1,0:T(8,128)(2,1)S(1)}, bf16[16,8192]{1,0:T(8,128)(2,1)}, u32[]{:S(2)}, u32[]{:S(2)}) collective-permute-start(bf16[16,8192]{1,0:T(8,128)(2,1)S(1)} %copy-done.2), channel_id=1, source_target_pairs={{0,4},{1,5},{2,6},{3,7},{4,8},{5,9},{6,10},{7,11},{8,12},{9,13},{1... | collective-permute-start | bytes 786440 | tf_op jit(solution)/shard_map/ppermute | solution.py:14
  9.2 4.7 %collective-permute-start.1 = (bf16[16,8192]{1,0:T(8,128)(2,1)S(1)}, bf16[16,8192]{1,0:T(8,128)(2,1)}, u32[]{:S(2)}, u32[]{:S(2)}) collective-permute-start(bf16[16,8192]{1,0:T(8,128)(2,1)S(1)} %copy-done.2), channel_id=1, source_target_pairs={{0,3},{1,4},{2,5},{3,6},{4,7},{5,8},{6,9},{7,10},{8,11},{9,12},{10... | collective-permute-start | bytes 786440 | tf_op jit(solution)/shard_map/ppermute | solution.py:14
  14.0 3.6 %collective-permute-start.2 = (bf16[16,8192]{1,0:T(8,128)(2,1)S(1)}, bf16[16,8192]{1,0:T(8,128)(2,1)S(1)}, u32[]{:S(2)}, u32[]{:S(2)}) collective-permute-start(bf16[16,8192]{1,0:T(8,128)(2,1)S(1)} %copy-done.2), channel_id=1, source_target_pairs={{0,2},{1,3},{2,4},{3,5},{4,6},{5,7},{6,8},{7,9},{8,10},{9,11},{10,... | collective-permute-start | bytes 786440 | tf_op jit(solution)/shard_map/ppermute | solution.py:14
  51.8 8.5 %collective-permute-start.8 = (bf16[3,8192]{1,0:T(4,128)(2,1)}, bf16[3,8192]{1,0:T(4,128)(2,1)S(1)}, u32[]{:S(2)}, u32[]{:S(2)}) collective-permute-start(bf16[3,8192]{1,0:T(4,128)(2,1)} %param.10), channel_id=1, source_target_pairs={{0,4},{1,5},{2,6},{3,7},{4,8},{5,9},{6,10},{7,11},{8,12},{9,13},{1... | collective-permute-start | bytes 147464 | tf_op jit(solution)/shard_map/ppermute | solution.py:14
  68.2 10.1 %collective-permute-start.9 = (bf16[3,8192]{1,0:T(4,128)(2,1)S(1)}, bf16[3,8192]{1,0:T(4,128)(2,1)S(1)}, u32[]{:S(2)}, u32[]{:S(2)}) collective-permute-start(bf16[3,8192]{1,0:T(4,128)(2,1)S(1)} %copy-done.3), channel_id=1, source_target_pairs={{0,3},{1,4},{2,5},{3,6},{4,7},{5,8},{6,9},{7,10},{8,11},{9,12},{10... | collective-permute-start | bytes 147464 | tf_op jit(solution)/shard_map/ppermute | solution.py:14
  79.6 7.0 %collective-permute-start.10 = (bf16[3,8192]{1,0:T(4,128)(2,1)S(1)}, bf16[3,8192]{1,0:T(4,128)(2,1)S(1)}, u32[]{:S(2)}, u32[]{:S(2)}) collective-permute-start(bf16[3,8192]{1,0:T(4,128)(2,1)S(1)} %copy-done.3), channel_id=1, source_target_pairs={{0,2},{1,3},{2,4},{3,5},{4,6},{5,7},{6,8},{7,9},{8,10},{9,11},{10,... | collective-permute-start | bytes 147464 | tf_op jit(solution)/shard_map/ppermute | solution.py:14
  87.9 11.9 %collective-permute-start.11 = (bf16[3,8192]{1,0:T(4,128)(2,1)S(1)}, bf16[3,8192]{1,0:T(4,128)(2,1)S(1)}, u32[]{:S(2)}, u32[]{:S(2)}) collective-permute-start(bf16[3,8192]{1,0:T(4,128)(2,1)S(1)} %copy-done.3), channel_id=1, source_target_pairs={{0,1},{1,2},{2,3},{3,4},{4,5},{5,6},{6,7},{7,8},{8,9},{9,10},{10,1... | collective-permute-start | bytes 147464 | tf_op jit(solution)/shard_map/ppermute | solution.py:14
  104.4 8.4 %collective-permute-done.12 = bf16[3,8192]{1,0:T(4,128)(2,1)S(1)} collective-permute-done((bf16[3,8192]{1,0:T(4,128)(2,1)S(1)}, bf16[3,8192]{1,0:T(4,128)(2,1)S(1)}, u32[]{:S(2)}, u32[]{:S(2)}) %collective-permute-start.12) | collective-permute-done | bytes 49184 | tf_op jit(solution)/shard_map/ppermute | solution.py:14
  115.4 7.9 %collective-permute-done.13 = bf16[3,8192]{1,0:T(4,128)(2,1)S(1)} collective-permute-done((bf16[3,8192]{1,0:T(4,128)(2,1)S(1)}, bf16[3,8192]{1,0:T(4,128)(2,1)S(1)}, u32[]{:S(2)}, u32[]{:S(2)}) %collective-permute-start.13) | collective-permute-done | bytes 49184 | tf_op jit(solution)/shard_map/ppermute | solution.py:14
  125.8 8.7 %collective-permute-done.14 = bf16[3,8192]{1,0:T(4,128)(2,1)S(1)} collective-permute-done((bf16[3,8192]{1,0:T(4,128)(2,1)S(1)}, bf16[3,8192]{1,0:T(4,128)(2,1)S(1)}, u32[]{:S(2)}, u32[]{:S(2)}) %collective-permute-start.14) | collective-permute-done | bytes 49184 | tf_op jit(solution)/shard_map/ppermute | solution.py:14
  137.1 8.3 %collective-permute-done.15 = bf16[3,8192]{1,0:T(4,128)(2,1)S(1)} collective-permute-done((bf16[3,8192]{1,0:T(4,128)(2,1)S(1)}, bf16[3,8192]{1,0:T(4,128)(2,1)S(1)}, u32[]{:S(2)}, u32[]{:S(2)}) %collective-permute-start.15) | collective-permute-done | bytes 49184 | tf_op jit(solution)/shard_map/ppermute | solution.py:14
  155.9 3.3 collective-permute-done.4
  159.2 4.8 %collective-permute-done.5 = bf16[16,8192]{1,0:T(8,128)(2,1)S(1)} collective-permute-done((bf16[16,8192]{1,0:T(8,128)(2,1)S(1)}, bf16[16,8192]{1,0:T(8,128)(2,1)S(1)}, u32[]{:S(2)}, u32[]{:S(2)}) %collective-permute-start.5) | collective-permute-done | bytes 262176 | tf_op jit(solution)/shard_map/ppermute | solution.py:14
  164.1 5.1 %collective-permute-done.6 = bf16[16,8192]{1,0:T(8,128)(2,1)S(1)} collective-permute-done((bf16[16,8192]{1,0:T(8,128)(2,1)S(1)}, bf16[16,8192]{1,0:T(8,128)(2,1)S(1)}, u32[]{:S(2)}, u32[]{:S(2)}) %collective-permute-start.6) | collective-permute-done | bytes 262176 | tf_op jit(solution)/shard_map/ppermute | solution.py:14
  169.2 5.7 %collective-permute-done.7 = bf16[16,8192]{1,0:T(8,128)(2,1)S(1)} collective-permute-done((bf16[16,8192]{1,0:T(8,128)(2,1)S(1)}, bf16[16,8192]{1,0:T(8,128)(2,1)S(1)}, u32[]{:S(2)}, u32[]{:S(2)}) %collective-permute-start.7) | collective-permute-done | bytes 262176 | tf_op jit(solution)/shard_map/ppermute | solution.py:14
  176.4 165.2 %while.15 = (s32[]{:T(128)}, f32[16,8192]{1,0:T(8,128)S(1)}, s32[8,5]{1,0:T(8,128)}, s32[]{:T(128)}, bf16[16,73728]{1,0:T(8,128)(2,1)}, /*index=5*/bf16[3,73728]...) while((s32[]{:T(128)}, f32[16,8192]{1,0:T(8,128)S(1)}, ...), condition=%wide.region_1.2_spmd, body=%wide.region_0.1_spmd.sunk | while | flops 220291104 | bytes 1135349 | solution.py:76
  185.4 2.4 fusion.169
  188.5 2.4 fusion.170
  191.6 2.4 fusion.171
  194.6 2.4 fusion.172
  206.1 2.4 fusion.169
  209.1 2.4 fusion.170
  212.2 2.4 fusion.171
  215.2 2.4 fusion.172
  226.7 2.4 fusion.169
  232.9 2.4 fusion.171
  235.9 2.4 fusion.172
  256.5 2.4 fusion.172
  277.2 2.4 fusion.172
  297.8 2.4 fusion.172
  318.5 2.4 fusion.172
  339.1 2.4 fusion.172
  (196 shorter events, 149.1 us)
Async XLA Ops:
  0.0 1.6 copy-start
  0.0 4.2 %copy-start.2 = (bf16[16,8192]{1,0:T(8,128)(2,1)S(1)}, bf16[16,8192]{1,0:T(8,128)(2,1)}, u32[]{:S(2)}) copy-start(bf16[16,8192]{1,0:T(8,128)(2,1)} %param.9) | copy-start | bytes 786436
  0.0 17.6 %copy-start.5 = (s32[1,4,3]{1,0,2:T(1,128)S(1)}, s32[1,4,3]{1,0,2:T(1,128)}, u32[]{:S(2)}) copy-start(s32[1,4,3]{1,0,2:T(1,128)} %param.15) | copy-start | bytes 148
  0.0 18.3 %copy-start.1 = (f32[4,2,128,128]{3,2,1,0:T(8,128)S(1)}, f32[4,2,128,128]{3,2,1,0:T(8,128)}, u32[]{:S(2)}) copy-start(f32[4,2,128,128]{3,2,1,0:T(8,128)} %param.12) | copy-start | bytes 1572868
  2.9 17.3 %collective-permute-start.16 = (f32[16,128]{1,0:T(8,128)S(1)}, f32[16,128]{1,0:T(8,128)}, u32[]{:S(2)}, u32[]{:S(2)}) collective-permute-start(f32[16,128]{1,0:T(8,128)S(1)} %fusion.130), channel_id=1, source_target_pairs={{0,1},{1,0},{2,3},{3,2},{4,5},{5,4},{6,7},{7,6},{8,9},{9,8},{10,11... | collective-permute-start | bytes 24584 | tf_op jit(solution)/shard_map/ppermute | solution.py:18
  3.7 19.5 %collective-permute-start.17 = (f32[16,128]{1,0:T(8,128)S(1)}, f32[16,128]{1,0:T(8,128)S(1)}, u32[]{:S(2)}, u32[]{:S(2)}) collective-permute-start(f32[16,128]{1,0:T(8,128)S(1)} %fusion.130), channel_id=1, source_target_pairs={{0,2},{1,3},{2,0},{3,1},{4,6},{5,7},{6,4},{7,5},{8,10},{9,11},{10,... | collective-permute-start | bytes 24584 | tf_op jit(solution)/shard_map/ppermute | solution.py:18
  4.2 143.7 %collective-permute-start = (bf16[16,8192]{1,0:T(8,128)(2,1)S(1)}, bf16[16,8192]{1,0:T(8,128)(2,1)}, u32[]{:S(2)}, u32[]{:S(2)}) collective-permute-start(bf16[16,8192]{1,0:T(8,128)(2,1)S(1)} %copy-done.2), channel_id=1, source_target_pairs={{0,4},{1,5},{2,6},{3,7},{4,8},{5,9},{6,10},{7,11},{8,12},{9,13},{1... | collective-permute-start | bytes 786440 | tf_op jit(solution)/shard_map/ppermute | solution.py:14
  9.2 141.6 %collective-permute-start.1 = (bf16[16,8192]{1,0:T(8,128)(2,1)S(1)}, bf16[16,8192]{1,0:T(8,128)(2,1)}, u32[]{:S(2)}, u32[]{:S(2)}) collective-permute-start(bf16[16,8192]{1,0:T(8,128)(2,1)S(1)} %copy-done.2), channel_id=1, source_target_pairs={{0,3},{1,4},{2,5},{3,6},{4,7},{5,8},{6,9},{7,10},{8,11},{9,12},{10... | collective-permute-start | bytes 786440 | tf_op jit(solution)/shard_map/ppermute | solution.py:14
  14.0 139.7 %collective-permute-start.2 = (bf16[16,8192]{1,0:T(8,128)(2,1)S(1)}, bf16[16,8192]{1,0:T(8,128)(2,1)S(1)}, u32[]{:S(2)}, u32[]{:S(2)}) collective-permute-start(bf16[16,8192]{1,0:T(8,128)(2,1)S(1)} %copy-done.2), channel_id=1, source_target_pairs={{0,2},{1,3},{2,4},{3,5},{4,6},{5,7},{6,8},{7,9},{8,10},{9,11},{10,... | collective-permute-start | bytes 786440 | tf_op jit(solution)/shard_map/ppermute | solution.py:14
  20.2 135.6 %collective-permute-start.3 = (bf16[16,8192]{1,0:T(8,128)(2,1)S(1)}, bf16[16,8192]{1,0:T(8,128)(2,1)S(1)}, u32[]{:S(2)}, u32[]{:S(2)}) collective-permute-start(bf16[16,8192]{1,0:T(8,128)(2,1)S(1)} %copy-done.2), channel_id=1, source_target_pairs={{0,1},{1,2},{2,3},{3,4},{4,5},{5,6},{6,7},{7,8},{8,9},{9,10},{10,1... | collective-permute-start | bytes 786440 | tf_op jit(solution)/shard_map/ppermute | solution.py:14
  23.2 6.1 %collective-permute-start.18 = (f32[16,128]{1,0:T(8,128)}, f32[16,128]{1,0:T(8,128)S(1)}, u32[]{:S(2)}, u32[]{:S(2)}) collective-permute-start(f32[16,128]{1,0:T(8,128)} %collective-permute-done.16), channel_id=1, source_target_pairs={{0,2},{1,3},{2,0},{3,1},{4,6},{5,7},{6,4},{7,5},{8,10},{9,11},{10,... | collective-permute-start | bytes 24584 | tf_op jit(solution)/shard_map/ppermute | solution.py:18
  29.3 4.7 %collective-permute-start.19 = (f32[16,128]{1,0:T(8,128)S(1)}, f32[16,128]{1,0:T(8,128)S(1)}, u32[]{:S(2)}, u32[]{:S(2)}) collective-permute-start(f32[16,128]{1,0:T(8,128)S(1)} %convolution_add_fusion.4), channel_id=1, source_target_pairs={{0,4},{1,5},{2,6},{3,7},{4,0},{5,1},{6,2},{7,3},{8,12},{9,13},{10,... | collective-permute-start | bytes 24584 | tf_op jit(solution)/shard_map/ppermute | solution.py:18
  31.8 36.4 %copy-start.3 = (bf16[3,8192]{1,0:T(4,128)(2,1)S(1)}, bf16[3,8192]{1,0:T(4,128)(2,1)}, u32[]{:S(2)}) copy-start(bf16[3,8192]{1,0:T(4,128)(2,1)} %param.10) | copy-start | bytes 147460
  34.0 4.1 %collective-permute-start.20 = (f32[16,128]{1,0:T(8,128)S(1)}, f32[16,128]{1,0:T(8,128)S(1)}, u32[]{:S(2)}, u32[]{:S(2)}) collective-permute-start(f32[16,128]{1,0:T(8,128)S(1)} %convolution_add_fusion.5), channel_id=1, source_target_pairs={{0,4},{1,5},{2,6},{3,7},{4,0},{5,1},{6,2},{7,3},{8,12},{9,13},{10,... | collective-permute-start | bytes 24584 | tf_op jit(solution)/shard_map/ppermute | solution.py:18
  38.1 2.9 collective-permute-start.21
  41.0 2.6 collective-permute-start.22
  43.6 4.1 %collective-permute-start.23 = (f32[16,128]{1,0:T(8,128)S(1)}, f32[16,128]{1,0:T(8,128)S(1)}, u32[]{:S(2)}, u32[]{:S(2)}) collective-permute-start(f32[16,128]{1,0:T(8,128)S(1)} %convolution_add_fusion), channel_id=1, source_target_pairs={{0,16},{1,17},{2,18},{3,19},{4,20},{5,21},{6,22},{7,23},{8,24},{9,... | collective-permute-start | bytes 24584 | tf_op jit(solution)/shard_map/ppermute | solution.py:18
  47.7 4.0 %collective-permute-start.24 = (f32[16,128]{1,0:T(8,128)S(1)}, f32[16,128]{1,0:T(8,128)S(1)}, u32[]{:S(2)}, u32[]{:S(2)}) collective-permute-start(f32[16,128]{1,0:T(8,128)S(1)} %convolution_add_fusion.1), channel_id=1, source_target_pairs={{0,16},{1,17},{2,18},{3,19},{4,20},{5,21},{6,22},{7,23},{8,24},{9,... | collective-permute-start | bytes 24584 | tf_op jit(solution)/shard_map/ppermute | solution.py:18
  51.8 16.5 %collective-permute-start.8 = (bf16[3,8192]{1,0:T(4,128)(2,1)}, bf16[3,8192]{1,0:T(4,128)(2,1)S(1)}, u32[]{:S(2)}, u32[]{:S(2)}) collective-permute-start(bf16[3,8192]{1,0:T(4,128)(2,1)} %param.10), channel_id=1, source_target_pairs={{0,4},{1,5},{2,6},{3,7},{4,8},{5,9},{6,10},{7,11},{8,12},{9,13},{1... | collective-permute-start | bytes 147464 | tf_op jit(solution)/shard_map/ppermute | solution.py:14
  68.2 11.4 %collective-permute-start.9 = (bf16[3,8192]{1,0:T(4,128)(2,1)S(1)}, bf16[3,8192]{1,0:T(4,128)(2,1)S(1)}, u32[]{:S(2)}, u32[]{:S(2)}) collective-permute-start(bf16[3,8192]{1,0:T(4,128)(2,1)S(1)} %copy-done.3), channel_id=1, source_target_pairs={{0,3},{1,4},{2,5},{3,6},{4,7},{5,8},{6,9},{7,10},{8,11},{9,12},{10... | collective-permute-start | bytes 147464 | tf_op jit(solution)/shard_map/ppermute | solution.py:14
  79.6 8.3 %collective-permute-start.10 = (bf16[3,8192]{1,0:T(4,128)(2,1)S(1)}, bf16[3,8192]{1,0:T(4,128)(2,1)S(1)}, u32[]{:S(2)}, u32[]{:S(2)}) collective-permute-start(bf16[3,8192]{1,0:T(4,128)(2,1)S(1)} %copy-done.3), channel_id=1, source_target_pairs={{0,2},{1,3},{2,4},{3,5},{4,6},{5,7},{6,8},{7,9},{8,10},{9,11},{10,... | collective-permute-start | bytes 147464 | tf_op jit(solution)/shard_map/ppermute | solution.py:14
  87.9 13.3 %collective-permute-start.11 = (bf16[3,8192]{1,0:T(4,128)(2,1)S(1)}, bf16[3,8192]{1,0:T(4,128)(2,1)S(1)}, u32[]{:S(2)}, u32[]{:S(2)}) collective-permute-start(bf16[3,8192]{1,0:T(4,128)(2,1)S(1)} %copy-done.3), channel_id=1, source_target_pairs={{0,1},{1,2},{2,3},{3,4},{4,5},{5,6},{6,7},{7,8},{8,9},{9,10},{10,1... | collective-permute-start | bytes 147464 | tf_op jit(solution)/shard_map/ppermute | solution.py:14
  101.2 11.6 %collective-permute-start.12 = (bf16[3,8192]{1,0:T(4,128)(2,1)S(1)}, bf16[3,8192]{1,0:T(4,128)(2,1)S(1)}, u32[]{:S(2)}, u32[]{:S(2)}) collective-permute-start(bf16[3,8192]{1,0:T(4,128)(2,1)S(1)} %copy-done.3), channel_id=1, source_target_pairs={{1,0},{2,1},{3,2},{4,3},{5,4},{6,5},{7,6},{8,7},{9,8},{10,9},{11,1... | collective-permute-start | bytes 147464 | tf_op jit(solution)/shard_map/ppermute | solution.py:14
  112.8 10.4 %collective-permute-start.13 = (bf16[3,8192]{1,0:T(4,128)(2,1)S(1)}, bf16[3,8192]{1,0:T(4,128)(2,1)S(1)}, u32[]{:S(2)}, u32[]{:S(2)}) collective-permute-start(bf16[3,8192]{1,0:T(4,128)(2,1)S(1)} %copy-done.3), channel_id=1, source_target_pairs={{2,0},{3,1},{4,2},{5,3},{6,4},{7,5},{8,6},{9,7},{10,8},{11,9},{12,... | collective-permute-start | bytes 147464 | tf_op jit(solution)/shard_map/ppermute | solution.py:14
  123.2 11.3 %collective-permute-start.14 = (bf16[3,8192]{1,0:T(4,128)(2,1)S(1)}, bf16[3,8192]{1,0:T(4,128)(2,1)S(1)}, u32[]{:S(2)}, u32[]{:S(2)}) collective-permute-start(bf16[3,8192]{1,0:T(4,128)(2,1)S(1)} %copy-done.3), channel_id=1, source_target_pairs={{3,0},{4,1},{5,2},{6,3},{7,4},{8,5},{9,6},{10,7},{11,8},{12,9},{13... | collective-permute-start | bytes 147464 | tf_op jit(solution)/shard_map/ppermute | solution.py:14
  134.5 10.8 %collective-permute-start.15 = (bf16[3,8192]{1,0:T(4,128)(2,1)S(1)}, bf16[3,8192]{1,0:T(4,128)(2,1)S(1)}, u32[]{:S(2)}, u32[]{:S(2)}) collective-permute-start(bf16[3,8192]{1,0:T(4,128)(2,1)S(1)} %copy-done.3), channel_id=1, source_target_pairs={{4,0},{5,1},{6,2},{7,3},{8,4},{9,5},{10,6},{11,7},{12,8},{13,9},{1... | collective-permute-start | bytes 147464 | tf_op jit(solution)/shard_map/ppermute | solution.py:14
  145.4 13.9 %collective-permute-start.4 = (bf16[16,8192]{1,0:T(8,128)(2,1)S(1)}, bf16[16,8192]{1,0:T(8,128)(2,1)S(1)}, u32[]{:S(2)}, u32[]{:S(2)}) collective-permute-start(bf16[16,8192]{1,0:T(8,128)(2,1)S(1)} %copy-done.2), channel_id=1, source_target_pairs={{1,0},{2,1},{3,2},{4,3},{5,4},{6,5},{7,6},{8,7},{9,8},{10,9},{11,1... | collective-permute-start | bytes 786440 | tf_op jit(solution)/shard_map/ppermute | solution.py:14
  147.9 16.1 %collective-permute-start.5 = (bf16[16,8192]{1,0:T(8,128)(2,1)S(1)}, bf16[16,8192]{1,0:T(8,128)(2,1)S(1)}, u32[]{:S(2)}, u32[]{:S(2)}) collective-permute-start(bf16[16,8192]{1,0:T(8,128)(2,1)S(1)} %copy-done.2), channel_id=1, source_target_pairs={{2,0},{3,1},{4,2},{5,3},{6,4},{7,5},{8,6},{9,7},{10,8},{11,9},{12,... | collective-permute-start | bytes 786440 | tf_op jit(solution)/shard_map/ppermute | solution.py:14
  150.8 18.3 %collective-permute-start.6 = (bf16[16,8192]{1,0:T(8,128)(2,1)S(1)}, bf16[16,8192]{1,0:T(8,128)(2,1)S(1)}, u32[]{:S(2)}, u32[]{:S(2)}) collective-permute-start(bf16[16,8192]{1,0:T(8,128)(2,1)S(1)} %copy-done.2), channel_id=1, source_target_pairs={{3,0},{4,1},{5,2},{6,3},{7,4},{8,5},{9,6},{10,7},{11,8},{12,9},{13... | collective-permute-start | bytes 786440 | tf_op jit(solution)/shard_map/ppermute | solution.py:14
  153.7 21.2 %collective-permute-start.7 = (bf16[16,8192]{1,0:T(8,128)(2,1)S(1)}, bf16[16,8192]{1,0:T(8,128)(2,1)S(1)}, u32[]{:S(2)}, u32[]{:S(2)}) collective-permute-start(bf16[16,8192]{1,0:T(8,128)(2,1)S(1)} %copy-done.2), channel_id=1, source_target_pairs={{4,0},{5,1},{6,2},{7,3},{8,4},{9,5},{10,6},{11,7},{12,8},{13,9},{1... | collective-permute-start | bytes 786440 | tf_op jit(solution)/shard_map/ppermute | solution.py:14
  174.9 1.4 copy-start.4
where the time goes:
time: 348 us; the launch traced here: 342 us
  matrix products  121 us (35%)
  starting transfers between devices  79.7 us (23%)
  waiting for transfers between devices  57.9 us (17%)
  loops' own time  51.2 us (15%)
  local copies, waits for them, and re-layouts  24.3 us (7%)
  other arithmetic  7.73 us (2%)
    dot_general x40, matrix products, near_leaf(): jnp.dot(src_vals, kernel_block(src_pos, tgt_pos), preferred_element_type=...  96.2 us
    ppermute x16, starting transfers between devices, passed_along(): return lax.ppermute(block, axis, route)  68.3 us
    ppermute x16, waiting for transfers between devices, passed_along(): return lax.ppermute(block, axis, route)  54.2 us
    another operation x1, loops' own time, local(): lax.fori_loop(0, leaves_dev, near_leaf, jnp.zeros((rhs_count, cluster_row...  51.2 us
    dot_general x12, matrix products, local(): jnp.dot(partners[m], coupling[t, m], precision=highest, preferred_element...  19.7 us
    ppermute x9, starting transfers between devices, from_partner(): lax.ppermute(array, axis, [(i, i ^ 1 << apart) for i in range(lax.axis_si...  11.5 us
    unnamed x28, local copies, waits for them, and re-layouts  10.2 us
  transfers between devices with their start and end apart: 25, of which 15 were waited for; matrix products, arithmetic and copies ran while one was open for 10% of the time, Pallas kernels for 0%

commit v1 on v0

v1 whole, which is shorter than its diff:
```python
import functools
import math

import jax
import jax.numpy as jnp
from jax import lax
from jax.experimental import pallas as pl
from jax.experimental.pallas import tpu as pltpu
from jax.sharding import PartitionSpec as P

bf16 = jnp.bfloat16
f32 = jnp.float32
smoothing_sq = 0.01
LEAF = 1024
HALF = 512
LEAVES_DEV = 8
RHS = 16
RANK = 128
NB = 5
FEATS = 16
PAYLOAD = (19, 16, HALF)
VM = pl.BlockSpec(memory_space=pltpu.VMEM)
SM = pl.BlockSpec(memory_space=pltpu.SMEM)
ANY = pl.BlockSpec(memory_space=pl.ANY)


def params(mib):
    return pltpu.CompilerParams(vmem_limit_bytes=mib * 2**20)


def permuted(array, source_of):
    count = lax.axis_size("leaf")
    route = [(source_of(i), i) for i in range(count) if 0 <= source_of(i) < count]
    return lax.ppermute(array, "leaf", route)


def pack_kernel(charges, points, out, rows):
    for k in range(16):
        out[k] = charges[:, k * HALF : (k + 1) * HALF]
    for l in range(LEAVES_DEV):
        for h in range(2):
            start = l * LEAF + h * HALF
            part = points[:, start : start + HALF].astype(f32)
            for c in range(3):
                row = h * 24 + c * 8 + l
                rows[row : row + 1, :] = part[c : c + 1]
    for k in range(3):
        out[16 + k] = rows[k * 16 : (k + 1) * 16, :].astype(bf16)


def pack(charges, points):
    return pl.pallas_call(
        pack_kernel,
        out_shape=jax.ShapeDtypeStruct(PAYLOAD, bf16),
        in_specs=[VM, VM],
        out_specs=VM,
        scratch_shapes=[pltpu.VMEM((48, HALF), f32)],
        compiler_params=params(16),
        cost_estimate=pl.CostEstimate(flops=10**6, bytes_accessed=10**6, transcendentals=0),
    )(charges, points)


def coordinates(block):
    rows = jnp.concatenate([block[16], block[17], block[18]], axis=0).astype(f32)
    return jnp.concatenate([rows[:24], rows[24:]], axis=1)


def squared_norm_parts(block, first_leaf, extra):
    pts = coordinates(block)
    leaf = lax.broadcasted_iota(jnp.int32, (LEAVES_DEV, LEAF), 0) + first_leaf
    a = leaf.astype(f32) * (1.0 / 64.0)
    x, y, z = pts[0:8], pts[8:16], pts[16:24]
    full_x = x + a
    norm = full_x * full_x + y * y + z * z + extra
    high = norm.astype(bf16).astype(f32)
    rest = norm - high
    middle = rest.astype(bf16).astype(f32)
    return x, a, y, z, high, middle, rest - middle


def store_features(dst, base, rows, tmp):
    for f, row in enumerate(rows):
        tmp[:, f, :] = row
    for f in range(len(rows), FEATS):
        tmp[:, f, :] = jnp.zeros((LEAVES_DEV, LEAF), f32)
    for l in range(LEAVES_DEV):
        dst[base + l] = tmp[l].astype(bf16)


def source_features(block, first_leaf, dst, base, tmp):
    x, a, y, z, high, middle, low = squared_norm_parts(block, first_leaf, 0.0)
    one = jnp.ones_like(x)
    store_features(dst, base, [x, x, a, a, y, z, high, middle, low, one, one, one], tmp)


def target_features(block, dst, tmp):
    x, a, y, z, high, middle, low = squared_norm_parts(block, 0, smoothing_sq)
    one = jnp.ones_like(x)
    rows = [-2 * x, -2 * a, -2 * x, -2 * a, -2 * y, -2 * z, one, one, one, high, middle, low]
    store_features(dst, 0, rows, tmp)


def near_kernel(stage, shapes, *refs):
    (place, near_list), refs = refs[:2], refs[2:]
    pieces, refs = refs[: len(shapes)], refs[len(shapes) :]
    if stage == 0:
        (acc, tgt, vals, feats, tmp) = refs
    elif stage == 1:
        (tgt, acc_in, acc, vals, feats, tmp) = refs
    else:
        (tgt, acc_in, down, basis_hbm, out, vals, feats, tmp, acc, basis, sem) = refs
        fetch = pltpu.make_async_copy(basis_hbm, basis, sem)
        fetch.start()
    me, sign = place[0], place[1]
    offsets = ((0, 1), (-1, -2, 2, 3), (-3, -4, 4))[stage]
    slot = 0
    for piece, shape in zip(pieces, shapes):
        for part in range(shape[0]):
            block = piece.at[part]
            for l in range(LEAVES_DEV):
                vals[slot * 8 + l, :, :HALF] = block[2 * l]
                vals[slot * 8 + l, :, HALF:] = block[2 * l + 1]
            source_features(
                block, offsets[slot] * sign * LEAVES_DEV, feats, slot * LEAVES_DEV, tmp
            )
            slot += 1
    if stage == 0:
        target_features(pieces[0].at[0], tgt, tmp)
        acc[...] = jnp.zeros_like(acc)
    else:
        acc[...] = acc_in[...]

    def add_block(i, w):
        src = feats[w].astype(f32).T.astype(bf16)
        for t in range(0, LEAF, 512):
            dist_sq = jnp.dot(src, tgt[i, :, t : t + 512], preferred_element_type=f32)
            kernel_vals = lax.rsqrt(dist_sq).astype(bf16)
            acc[i, :, t : t + 512] += jnp.dot(
                vals[w], kernel_vals, preferred_element_type=f32
            )

    first = {0: 0, 1: 1, 2: 1}[stage]

    def item(it, carry):
        i, k = it // NB, it % NB
        j = near_list[i, k]
        off = (j // LEAVES_DEV - me) * sign
        index = jnp.int32(-1)
        for s, o in enumerate(offsets):
            index = jnp.where(off == o, s, index)

        @pl.when(index >= 0)
        def _():
            add_block(i, index * LEAVES_DEV + j % LEAVES_DEV)

        return carry

    lax.fori_loop(0, LEAVES_DEV * NB, item, 0)
    if stage == 2:
        fetch.wait()
        scale = 1.0 / math.sqrt(NB * LEAF)
        for l in range(LEAVES_DEV):
            far = lax.dot_general(
                down[...], basis[l], (((1,), (1,)), ((), ())), preferred_element_type=f32
            )
            out[:, l * LEAF : (l + 1) * LEAF] = (acc[l] * scale + far).astype(bf16)


def near_stage(stage, place, near_list, pieces, *more):
    shapes = [p.shape for p in pieces]
    slots = sum(s[0] for s in shapes)
    acc = jax.ShapeDtypeStruct((LEAVES_DEV, RHS, LEAF), f32)
    tgt = jax.ShapeDtypeStruct((LEAVES_DEV, FEATS, LEAF), bf16)
    scratch = [
        pltpu.VMEM((slots * 8, RHS, LEAF), bf16),
        pltpu.VMEM((slots * 8, FEATS, LEAF), bf16),
        pltpu.VMEM((LEAVES_DEV, FEATS, LEAF), f32),
    ]
    specs = [SM, SM] + [VM] * len(pieces)
    if stage == 0:
        out_shape, out_specs = (acc, tgt), (VM, VM)
    elif stage == 1:
        out_shape, out_specs = acc, VM
        specs += [VM, VM]
    else:
        out_shape, out_specs = jax.ShapeDtypeStruct((RHS, LEAVES_DEV * LEAF), bf16), VM
        specs += [VM, VM, VM, ANY]
        scratch += [
            pltpu.VMEM((LEAVES_DEV, RHS, LEAF), f32),
            pltpu.VMEM((LEAVES_DEV, LEAF, RANK), bf16),
            pltpu.SemaphoreType.DMA,
        ]
    return pl.pallas_call(
        functools.partial(near_kernel, stage, shapes),
        out_shape=out_shape,
        in_specs=specs,
        out_specs=out_specs,
        scratch_shapes=scratch,
        compiler_params=params(40),
        cost_estimate=pl.CostEstimate(
            flops=10**10, bytes_accessed=10**6, transcendentals=13 * 10**6
        ),
    )(place, near_list, *pieces, *more)


def tree_kernel(place, flags, coefs, transfer, coupling, out):
    me = place[0]

    def dot(a, b):
        return jnp.dot(a, b, precision=lax.Precision.HIGHEST, preferred_element_type=f32)

    levels = 4
    cur = [coefs[m] for m in range(32)]
    coupled = []
    for t in range(levels):
        total = jnp.zeros((RHS, RANK), f32)
        for m in range(3):
            flag = flags[t, m].astype(f32)
            total = total + flag * dot(cur[m + 1], coupling[t, m])
        coupled.append(total)
        if t + 1 < levels:
            right = ((me >> t) & 1) == 1
            even = jnp.concatenate(cur[0::2], axis=0)
            odd = jnp.concatenate(cur[1::2], axis=0)
            merged = dot(jnp.where(right, odd, even), transfer[t, 0]) + dot(
                jnp.where(right, even, odd), transfer[t, 1]
            )
            cur = [merged[m * RHS : (m + 1) * RHS] for m in range(len(cur) // 2)]
    local = coupled[-1]
    for t in range(levels - 1, 0, -1):
        right = ((me >> (t - 1)) & 1) == 1
        mat = jnp.where(right, transfer[t - 1, 1], transfer[t - 1, 0])
        local = coupled[t - 1] + lax.dot_general(
            local,
            mat,
            (((1,), (1,)), ((), ())),
            precision=lax.Precision.HIGHEST,
            preferred_element_type=f32,
        )
    out[...] = local.astype(bf16)


def tree(place, flags, coefs, transfer, coupling):
    return pl.pallas_call(
        tree_kernel,
        out_shape=jax.ShapeDtypeStruct((RHS, RANK), bf16),
        in_specs=[SM, SM, VM, VM, VM],
        out_specs=VM,
        compiler_params=params(16),
        cost_estimate=pl.CostEstimate(flops=10**9, bytes_accessed=10**6, transcendentals=0),
    )(place, flags, coefs, transfer, coupling)


def local(charges, points, leaf_basis, transfer, coupling, near_list, couple_flags):
    me = lax.axis_index("leaf")
    sign = 1 - 2 * (me % 2)
    place = jnp.stack([me, sign]).astype(jnp.int32)

    own = pack(charges, points)
    sib = permuted(own, lambda i: i ^ 1)
    pair = jnp.stack([own, sib])
    near1 = permuted(pair, lambda i: i - 1 if i % 2 == 0 else i + 1)
    far1 = permuted(near1, lambda i: i - 2 if i % 2 == 0 else i + 2)
    near2 = permuted(near1, lambda i: i ^ 1)
    far2 = permuted(far1[:1], lambda i: i ^ 1)

    coefs = jnp.dot(
        charges,
        leaf_basis.reshape(LEAVES_DEV * LEAF, RANK),
        preferred_element_type=f32,
    )[None]
    for step in range(5):
        coefs = jnp.concatenate([coefs, permuted(coefs, lambda i: i ^ (1 << step))])

    acc, tgt = near_stage(0, place, near_list, [pair])
    acc = near_stage(1, place, near_list, [near1, near2], tgt, acc)
    down = tree(place, couple_flags[0], coefs, transfer, coupling)
    return near_stage(2, place, near_list, [far1, far2], tgt, acc, down, leaf_basis)


def solution(mesh):
    return jax.shard_map(
        local,
        mesh=mesh,
        in_specs=(
            P(None, "leaf"),
            P(None, "leaf"),
            P("leaf", None, None),
            P(),
            P(),
            P("leaf", None),
            P("leaf", None, None),
        ),
        out_specs=P(None, "leaf"),
        check_vma=False,
    )
```

time: 348 us -> 92.1 us (0.26)
  the two profiles are of different devices: /device:TPU:127 before, /device:TPU:187 now
where the time goes in v1:
time: 92.1 us; the launch traced here: 92 us
  Pallas kernels  50.9 us (55%)
  starting transfers between devices  23.6 us (26%)
  waiting for transfers between devices  14.9 us (16%)
  matrix products  2.17 us (2%)
    pallas_call x3, Pallas kernels, near_stage(): pl.pallas_call(functools.partial(near_kernel, stage, shapes), out_shape=o...  47.5 us
    ppermute x10, starting transfers between devices, permuted(): return lax.ppermute(array, 'leaf', route)  23.6 us
    ppermute x10, waiting for transfers between devices, permuted(): return lax.ppermute(array, 'leaf', route)  14.9 us
    pallas_call x1, Pallas kernels, tree(): pl.pallas_call(tree_kernel, out_shape=jax.ShapeDtypeStruct((RHS, RANK), b...  3.35 us
    dot_general x1, matrix products, local(): jnp.dot(charges, leaf_basis.reshape(LEAVES_DEV * LEAF, RANK), preferred_e...  2.17 us
  transfers between devices with their start and end apart: 10, of which 4 were waited for; matrix products, arithmetic and copies ran while one was open for 0% of the time, Pallas kernels for 35%

profile of v1, /device:TPU:187, one launch (start us, length us, event | category | flops | bytes accessed | tf_op | source)
XLA Modules:
  0.0 92.0 jit_solution(8544109004345312917)
XLA Ops:
  0.0 0.0 copy-start.3
  0.0 0.0 copy-start.4
  0.0 2.2 %constant_dynamic-update-slice_fusion.4 = (f32[16,16,128]{2,1,0:T(8,128)S(1)}, f32[32,16,128]{2,1,0:T(8,128)S(1)}, f32[1,16,128]{2,1,0:T(8,128)S(1)}) fusion(bf16[16,8192]{1,0:T(8,128)(2,1)} %charges.1, bf16[8192,128]{1,0:T(8,128)(2,1)} %bitcast.10), kind=kOutput, calls=%fused_computation.8 | convolution fusion | flops 33554432 | bytes 2383872 | tf_op jit(solution)/shard_map/dot_general | solution.py:267
  2.2 0.8 collective-permute-start.5
  3.0 0.0 copy-done.2
  3.0 0.1 collective-permute-start
  3.1 0.7 collective-permute-done.5
  3.8 0.5 collective-permute-start.6
  4.3 2.1 %collective-permute-done.6 = f32[2,16,128]{2,1,0:T(8,128)S(1)} collective-permute-done((f32[2,16,128]{2,1,0:T(8,128)S(1)}, f32[2,16,128]{2,1,0:T(8,128)S(1)}, u32[]{:S(2)}, u32[]{:S(2)}) %collective-permute-start.6) | collective-permute-done | bytes 16416 | tf_op jit(solution)/shard_map/ppermute | solution.py:34
  6.4 1.0 %collective-permute-start.7 = (f32[4,16,128]{2,1,0:T(8,128)S(1)}, f32[4,16,128]{2,1,0:T(8,128)S(1)}, u32[]{:S(2)}, u32[]{:S(2)}) collective-permute-start(f32[4,16,128]{2,1,0:T(8,128)S(1)} %pad_maximum_fusion.2), channel_id=1, source_target_pairs={{4,0},{5,1},{6,2},{7,3},{0,4},{1,5},{2,6},{3,7},{12,8},{13,9},{14,... | collective-permute-start | bytes 98312 | tf_op jit(solution)/shard_map/ppermute | solution.py:34
  7.4 0.0 collective-permute-done
  7.4 0.1 pad_maximum_fusion.refs_2_
  7.4 6.4 %collective-permute-start.1 = (bf16[2,19,16,512]{3,2,1,0:T(8,128)(2,1)S(1)}, bf16[2,19,16,512]{3,2,1,0:T(8,128)(2,1)S(1)}, u32[]{:S(2)}, u32[]{:S(2)}) collective-permute-start(bf16[2,19,16,512]{3,2,1,0:T(8,128)(2,1)S(1)} %pad_maximum_fusion.refs_2_), channel_id=1, source_target_pairs={{2,1},{1,2},{4,3},{3,4},{6,5},{5,6},{8,7},{7,8},{10,9},{9,10},{12,... | collective-permute-start | bytes 1867784 | tf_op jit(solution)/shard_map/ppermute | solution.py:34
  13.8 0.0 collective-permute-done.7
  13.8 0.3 collective-permute-start.8
  14.2 9.5 %collective-permute-done.8 = f32[8,16,128]{2,1,0:T(8,128)S(1)} collective-permute-done((f32[8,16,128]{2,1,0:T(8,128)S(1)}, f32[8,16,128]{2,1,0:T(8,128)S(1)}, u32[]{:S(2)}, u32[]{:S(2)}) %collective-permute-start.8) | collective-permute-done | bytes 65568 | tf_op jit(solution)/shard_map/ppermute | solution.py:34
  23.7 2.7 %collective-permute-start.9 = (f32[16,16,128]{2,1,0:T(8,128)S(1)}, f32[16,16,128]{2,1,0:T(8,128)S(1)}, u32[]{:S(2)}, u32[]{:S(2)}) collective-permute-start(f32[16,16,128]{2,1,0:T(8,128)S(1)} %get-tuple-element.9), channel_id=1, source_target_pairs={{16,0},{17,1},{18,2},{19,3},{20,4},{21,5},{22,6},{23,7},{24,8},{25... | collective-permute-start | bytes 393224 | tf_op jit(solution)/shard_map/ppermute | solution.py:34
  26.4 0.1 copy.8
  26.5 0.1 pad_add_fusion.refs_0_.place
  26.6 2.5 %collective-permute-done.9 = f32[16,16,128]{2,1,0:T(8,128)S(1)} collective-permute-done((f32[16,16,128]{2,1,0:T(8,128)S(1)}, f32[16,16,128]{2,1,0:T(8,128)S(1)}, u32[]{:S(2)}, u32[]{:S(2)}) %collective-permute-start.9) | collective-permute-done | bytes 131104 | tf_op jit(solution)/shard_map/ppermute | solution.py:34
  29.2 3.4 %shard_map.76.refs_6_ = bf16[16,128]{1,0:T(8,128)(2,1)S(1)} custom-call(s32[2]{0:T(128)S(1)} %pad_add_fusion.refs_0_.place, s32[4,3]{1,0:T(4,128)S(1)} %bitcast.12, f32[32,16,128]{2,1,0:T(8,128)S(1)} %constant_dynamic-update-slice_fusion.5.coefs, f32[4,2,128,128]{3,2,1,0:T(8,128)S(1)} %copy-done.4, f32[4,3,128,128]{3,2,1,0:T(8,128)S(1)} %copy-done.3), custom_call_target="tpu_custom_call" | custom-call | flops 1000000000 | bytes 1000000 | tf_op jit(solution)/shard_map/pallas_call | solution.py:244
  32.5 0.0 collective-permute-done.1.refs_2_
  32.5 0.0 collective-permute-start.4
  32.6 1.9 %collective-permute-start.2 = (bf16[2,19,16,512]{3,2,1,0:T(8,128)(2,1)S(1)}, bf16[2,19,16,512]{3,2,1,0:T(8,128)(2,1)S(1)}, u32[]{:S(2)}, u32[]{:S(2)}) collective-permute-start(bf16[2,19,16,512]{3,2,1,0:T(8,128)(2,1)S(1)} %collective-permute-done.1.refs_2_), channel_id=1, source_target_pairs={{3,1},{0,2},{5,3},{2,4},{7,5},{4,6},{9,7},{6,8},{11,9},{8,10},{13,... | collective-permute-start | bytes 1867784 | tf_op jit(solution)/shard_map/ppermute | solution.py:34
  34.5 0.0 copy-done.5
  34.5 12.9 %shard_map.74 = (f32[8,16,1024]{2,1,0:T(8,128)S(1)}, bf16[8,16,1024]{2,1,0:T(8,128)(2,1)S(1)}) custom-call(s32[2]{0:T(128)S(1)} %pad_add_fusion.refs_0_.place, s32[8,5]{1,0:T(8,128)S(1)} %copy-done.5, bf16[2,19,16,512]{3,2,1,0:T(8,128)(2,1)S(1)} %pad_maximum_fusion.refs_2_), custom_call_target="tpu_custom_call" | custom-call | flops 10000000000 | bytes 1000000 | tf_op jit(solution)/shard_map/pallas_call | solution.py:193
  47.4 0.0 collective-permute-done.2.refs_2_
  47.4 9.9 %collective-permute-start.3 = (bf16[1,19,16,512]{3,2,1,0:T(8,128)(2,1)S(1)}, bf16[1,19,16,512]{3,2,1,0:T(8,128)(2,1)S(1)}, u32[]{:S(2)}, u32[]{:S(2)}) collective-permute-start(bf16[1,19,16,512]{3,2,1,0:T(8,128)(2,1)S(1)} %slice.4), channel_id=1, source_target_pairs={{1,0},{0,1},{3,2},{2,3},{5,4},{4,5},{7,6},{6,7},{9,8},{8,9},{11,10... | collective-permute-start | bytes 933896 | tf_op jit(solution)/shard_map/ppermute | solution.py:34
  57.4 0.0 collective-permute-done.4.refs_3_
  57.4 16.2 %shard_map.75.refs_5_ = f32[8,16,1024]{2,1,0:T(8,128)S(1)} custom-call(s32[2]{0:T(128)S(1)} %pad_add_fusion.refs_0_.place, s32[8,5]{1,0:T(8,128)S(1)} %copy-done.5, bf16[2,19,16,512]{3,2,1,0:T(8,128)(2,1)S(1)} %collective-permute-done.1.refs_2_, bf16[2,19,16,512]{3,2,1,0:T(8,128)(2,1)S(1)} %collective-permute-done.4.refs_3_, ...), custom_call_target="tpu_custom_call" | custom-call | flops 10000000000 | bytes 1000000 | tf_op jit(solution)/shard_map/pallas_call | solution.py:193
  73.6 0.0 collective-permute-done.3.refs_3_
  73.6 18.4 %shard_map.77 = bf16[16,8192]{1,0:T(8,128)(2,1)} custom-call(s32[2]{0:T(128)S(1)} %pad_add_fusion.refs_0_.place, s32[8,5]{1,0:T(8,128)S(1)} %copy-done.5, bf16[2,19,16,512]{3,2,1,0:T(8,128)(2,1)S(1)} %collective-permute-done.2.refs_2_, bf16[1,19,16,512]{3,2,1,0:T(8,128)(2,1)S(1)} %collective-permute-done.3.refs_3_, ...), custom_call_target="tpu_custom_call" | custom-call | flops 10000000000 | bytes 1000000 | tf_op jit(solution)/shard_map/pallas_call | solution.py:193
  (20 shorter events, 0.1 us)
Async XLA Ops:
  0.0 3.0 %copy-start.1 = (bf16[16,8192]{1,0:T(8,128)(2,1)S(1)}, bf16[16,8192]{1,0:T(8,128)(2,1)}, u32[]{:S(2)}) copy-start(bf16[16,8192]{1,0:T(8,128)(2,1)} %charges.1) | copy-start | bytes 786436
  0.0 3.0 %copy-start.2 = (bf16[3,8192]{1,0:T(4,128)(2,1)S(1)}, bf16[3,8192]{1,0:T(4,128)(2,1)}, u32[]{:S(2)}) copy-start(bf16[3,8192]{1,0:T(4,128)(2,1)} %points.1) | copy-start | bytes 147460
  0.0 26.4 %copy-start.6 = (s32[1,4,3]{1,0,2:T(1,128)S(1)}, s32[1,4,3]{1,0,2:T(1,128)}, u32[]{:S(2)}) copy-start(s32[1,4,3]{1,0,2:T(1,128)} %param.13) | copy-start | bytes 148
  0.0 29.2 %copy-start.3 = (f32[4,3,128,128]{3,2,1,0:T(8,128)S(1)}, f32[4,3,128,128]{3,2,1,0:T(8,128)}, u32[]{:S(2)}) copy-start(f32[4,3,128,128]{3,2,1,0:T(8,128)} %coupling.1) | copy-start | bytes 2359300
  0.0 29.2 %copy-start.4 = (f32[4,2,128,128]{3,2,1,0:T(8,128)S(1)}, f32[4,2,128,128]{3,2,1,0:T(8,128)}, u32[]{:S(2)}) copy-start(f32[4,2,128,128]{3,2,1,0:T(8,128)} %transfer.1) | copy-start | bytes 1572868
  2.2 1.6 %collective-permute-start.5 = (f32[1,16,128]{2,1,0:T(8,128)S(1)}, f32[1,16,128]{2,1,0:T(8,128)S(1)}, u32[]{:S(2)}, u32[]{:S(2)}) collective-permute-start(f32[1,16,128]{2,1,0:T(8,128)S(1)} %get-tuple-element.19), channel_id=1, source_target_pairs={{1,0},{0,1},{3,2},{2,3},{5,4},{4,5},{7,6},{6,7},{9,8},{8,9},{11,10... | collective-permute-start | bytes 24584 | tf_op jit(solution)/shard_map/ppermute | solution.py:34
  3.0 4.3 %collective-permute-start = (bf16[19,16,512]{2,1,0:T(8,128)(2,1)S(1)}, bf16[19,16,512]{2,1,0:T(8,128)(2,1)S(1)}, u32[]{:S(2)}, u32[]{:S(2)}) collective-permute-start(bf16[19,16,512]{2,1,0:T(8,128)(2,1)S(1)} %shard_map.73), channel_id=1, source_target_pairs={{1,0},{0,1},{3,2},{2,3},{5,4},{4,5},{7,6},{6,7},{9,8},{8,9},{11,10... | collective-permute-start | bytes 933896 | tf_op jit(solution)/shard_map/ppermute | solution.py:34
  3.8 2.6 %collective-permute-start.6 = (f32[2,16,128]{2,1,0:T(8,128)S(1)}, f32[2,16,128]{2,1,0:T(8,128)S(1)}, u32[]{:S(2)}, u32[]{:S(2)}) collective-permute-start(f32[2,16,128]{2,1,0:T(8,128)S(1)} %pad_maximum_fusion.3), channel_id=1, source_target_pairs={{2,0},{3,1},{0,2},{1,3},{6,4},{7,5},{4,6},{5,7},{10,8},{11,9},{8,1... | collective-permute-start | bytes 49160 | tf_op jit(solution)/shard_map/ppermute | solution.py:34
  6.4 7.4 %collective-permute-start.7 = (f32[4,16,128]{2,1,0:T(8,128)S(1)}, f32[4,16,128]{2,1,0:T(8,128)S(1)}, u32[]{:S(2)}, u32[]{:S(2)}) collective-permute-start(f32[4,16,128]{2,1,0:T(8,128)S(1)} %pad_maximum_fusion.2), channel_id=1, source_target_pairs={{4,0},{5,1},{6,2},{7,3},{0,4},{1,5},{2,6},{3,7},{12,8},{13,9},{14,... | collective-permute-start | bytes 98312 | tf_op jit(solution)/shard_map/ppermute | solution.py:34
  7.4 25.1 %collective-permute-start.1 = (bf16[2,19,16,512]{3,2,1,0:T(8,128)(2,1)S(1)}, bf16[2,19,16,512]{3,2,1,0:T(8,128)(2,1)S(1)}, u32[]{:S(2)}, u32[]{:S(2)}) collective-permute-start(bf16[2,19,16,512]{3,2,1,0:T(8,128)(2,1)S(1)} %pad_maximum_fusion.refs_2_), channel_id=1, source_target_pairs={{2,1},{1,2},{4,3},{3,4},{6,5},{5,6},{8,7},{7,8},{10,9},{9,10},{12,... | collective-permute-start | bytes 1867784 | tf_op jit(solution)/shard_map/ppermute | solution.py:34
  13.8 9.9 %collective-permute-start.8 = (f32[8,16,128]{2,1,0:T(8,128)S(1)}, f32[8,16,128]{2,1,0:T(8,128)S(1)}, u32[]{:S(2)}, u32[]{:S(2)}) collective-permute-start(f32[8,16,128]{2,1,0:T(8,128)S(1)} %pad_maximum_fusion.1), channel_id=1, source_target_pairs={{8,0},{9,1},{10,2},{11,3},{12,4},{13,5},{14,6},{15,7},{0,8},{1,9},... | collective-permute-start | bytes 196616 | tf_op jit(solution)/shard_map/ppermute | solution.py:34
  23.7 10.8 %copy-start.5 = (s32[8,5]{1,0:T(8,128)S(1)}, s32[8,5]{1,0:T(8,128)}, u32[]{:S(2)}) copy-start(s32[8,5]{1,0:T(8,128)} %refs_1_.5) | copy-start | bytes 484
  23.7 5.4 %collective-permute-start.9 = (f32[16,16,128]{2,1,0:T(8,128)S(1)}, f32[16,16,128]{2,1,0:T(8,128)S(1)}, u32[]{:S(2)}, u32[]{:S(2)}) collective-permute-start(f32[16,16,128]{2,1,0:T(8,128)S(1)} %get-tuple-element.9), channel_id=1, source_target_pairs={{16,0},{17,1},{18,2},{19,3},{20,4},{21,5},{22,6},{23,7},{24,8},{25... | collective-permute-start | bytes 393224 | tf_op jit(solution)/shard_map/ppermute | solution.py:34
  32.5 24.8 %collective-permute-start.4 = (bf16[2,19,16,512]{3,2,1,0:T(8,128)(2,1)S(1)}, bf16[2,19,16,512]{3,2,1,0:T(8,128)(2,1)S(1)}, u32[]{:S(2)}, u32[]{:S(2)}) collective-permute-start(bf16[2,19,16,512]{3,2,1,0:T(8,128)(2,1)S(1)} %collective-permute-done.1.refs_2_), channel_id=1, source_target_pairs={{1,0},{0,1},{3,2},{2,3},{5,4},{4,5},{7,6},{6,7},{9,8},{8,9},{11,10... | collective-permute-start | bytes 1867784 | tf_op jit(solution)/shard_map/ppermute | solution.py:34
  32.6 14.8 %collective-permute-start.2 = (bf16[2,19,16,512]{3,2,1,0:T(8,128)(2,1)S(1)}, bf16[2,19,16,512]{3,2,1,0:T(8,128)(2,1)S(1)}, u32[]{:S(2)}, u32[]{:S(2)}) collective-permute-start(bf16[2,19,16,512]{3,2,1,0:T(8,128)(2,1)S(1)} %collective-permute-done.1.refs_2_), channel_id=1, source_target_pairs={{3,1},{0,2},{5,3},{2,4},{7,5},{4,6},{9,7},{6,8},{11,9},{8,10},{13,... | collective-permute-start | bytes 1867784 | tf_op jit(solution)/shard_map/ppermute | solution.py:34
  47.4 26.1 %collective-permute-start.3 = (bf16[1,19,16,512]{3,2,1,0:T(8,128)(2,1)S(1)}, bf16[1,19,16,512]{3,2,1,0:T(8,128)(2,1)S(1)}, u32[]{:S(2)}, u32[]{:S(2)}) collective-permute-start(bf16[1,19,16,512]{3,2,1,0:T(8,128)(2,1)S(1)} %slice.4), channel_id=1, source_target_pairs={{1,0},{0,1},{3,2},{2,3},{5,4},{4,5},{7,6},{6,7},{9,8},{8,9},{11,10... | collective-permute-start | bytes 933896 | tf_op jit(solution)/shard_map/ppermute | solution.py:34
  57.4 16.2 %copy-start = (bf16[8,1024,128]{2,1,0:T(8,128)(2,1)S(1)}, bf16[8,1024,128]{2,1,0:T(8,128)(2,1)}, u32[]{:S(2)}) copy-start(bf16[8,1024,128]{2,1,0:T(8,128)(2,1)} %refs_7_.1) | copy-start | bytes 6291460

commit v2 on v1

--- a/solution.py
+++ b/solution.py
@@ -21,7 +21,9 @@
 PAYLOAD = (19, 16, HALF)
 VM = pl.BlockSpec(memory_space=pltpu.VMEM)
 SM = pl.BlockSpec(memory_space=pltpu.SMEM)
-ANY = pl.BlockSpec(memory_space=pl.ANY)
+SLOT_OFFSETS = (0, 1, -1, -2, 2, 3, -3, -4, 4)
+SELF = (2, 4, 6, 8)
+BUDGET = 11
 
 
 def params(mib):
@@ -100,107 +102,108 @@
     store_features(dst, 0, rows, tmp)
 
 
-def near_kernel(stage, shapes, *refs):
-    (place, near_list), refs = refs[:2], refs[2:]
-    pieces, refs = refs[: len(shapes)], refs[len(shapes) :]
-    if stage == 0:
-        (acc, tgt, vals, feats, tmp) = refs
-    elif stage == 1:
-        (tgt, acc_in, acc, vals, feats, tmp) = refs
-    else:
-        (tgt, acc_in, down, basis_hbm, out, vals, feats, tmp, acc, basis, sem) = refs
-        fetch = pltpu.make_async_copy(basis_hbm, basis, sem)
-        fetch.start()
-    me, sign = place[0], place[1]
-    offsets = ((0, 1), (-1, -2, 2, 3), (-3, -4, 4))[stage]
-    slot = 0
-    for piece, shape in zip(pieces, shapes):
-        for part in range(shape[0]):
-            block = piece.at[part]
-            for l in range(LEAVES_DEV):
-                vals[slot * 8 + l, :, :HALF] = block[2 * l]
-                vals[slot * 8 + l, :, HALF:] = block[2 * l + 1]
-            source_features(
-                block, offsets[slot] * sign * LEAVES_DEV, feats, slot * LEAVES_DEV, tmp
-            )
-            slot += 1
-    if stage == 0:
-        target_features(pieces[0].at[0], tgt, tmp)
-        acc[...] = jnp.zeros_like(acc)
-    else:
-        acc[...] = acc_in[...]
-
-    def add_block(i, w):
-        src = feats[w].astype(f32).T.astype(bf16)
-        for t in range(0, LEAF, 512):
-            dist_sq = jnp.dot(src, tgt[i, :, t : t + 512], preferred_element_type=f32)
-            kernel_vals = lax.rsqrt(dist_sq).astype(bf16)
-            acc[i, :, t : t + 512] += jnp.dot(
-                vals[w], kernel_vals, preferred_element_type=f32
-            )
-
-    first = {0: 0, 1: 1, 2: 1}[stage]
-
-    def item(it, carry):
-        i, k = it // NB, it % NB
-        j = near_list[i, k]
-        off = (j // LEAVES_DEV - me) * sign
-        index = jnp.int32(-1)
-        for s, o in enumerate(offsets):
-            index = jnp.where(off == o, s, index)
-
-        @pl.when(index >= 0)
+def load_cluster(block, slot, sign, vals, feats, tmp):
+    for l in range(LEAVES_DEV):
+        vals[slot * LEAVES_DEV + l, :, :HALF] = block[2 * l]
+        vals[slot * LEAVES_DEV + l, :, HALF:] = block[2 * l + 1]
+    first_leaf = SLOT_OFFSETS[slot] * LEAVES_DEV * sign
+    source_features(block, first_leaf, feats, slot * LEAVES_DEV, tmp)
+
+
+def add_block(i, w, tgt, vals, feats, acc):
+    src = feats[w].astype(f32).T.astype(bf16)
+    for t in range(0, LEAF, 512):
+        dist_sq = jnp.dot(src, tgt[i, :, t : t + 512], preferred_element_type=f32)
+        kernel_vals = lax.rsqrt(dist_sq).astype(bf16)
+        acc[i, :, t : t + 512] += jnp.dot(vals[w], kernel_vals, preferred_element_type=f32)
+
+
+def add_listed(part, work, tgt, vals, feats, acc):
+    def item(it, count):
+        i, k = it // (NB - 1), it % (NB - 1) + 1
+        w = work[i, k]
+        in_first = (w < 6 * LEAVES_DEV) & (count < BUDGET)
+
+        @pl.when(in_first if part == 1 else jnp.logical_not(in_first))
         def _():
-            add_block(i, index * LEAVES_DEV + j % LEAVES_DEV)
-
+            add_block(i, w, tgt, vals, feats, acc)
+
+        return count + in_first.astype(jnp.int32)
+
+    lax.fori_loop(0, LEAVES_DEV * (NB - 1), item, jnp.int32(0))
+
+
+def join(mine, theirs, joined):
+    n = mine.shape[0]
+    joined[:n] = mine[...]
+    joined[n:] = theirs[...]
+
+
+def first_kernel(place, pair, mine, theirs, acc, tgt, vals, feats, joined, tmp):
+    join(mine, theirs, joined)
+    acc[...] = jnp.zeros_like(acc)
+    target_features(pair.at[0], tgt, tmp)
+    for slot in range(2):
+        load_cluster(pair.at[slot], slot, place[1], vals, feats, tmp)
+    own_blocks(0, SELF[0], tgt, vals, feats, acc)
+
+
+def own_blocks(first, last, tgt, vals, feats, acc):
+    def one(i, carry):
+        add_block(i, i, tgt, vals, feats, acc)
         return carry
 
-    lax.fori_loop(0, LEAVES_DEV * NB, item, 0)
-    if stage == 2:
-        fetch.wait()
-        scale = 1.0 / math.sqrt(NB * LEAF)
-        for l in range(LEAVES_DEV):
-            far = lax.dot_general(
-                down[...], basis[l], (((1,), (1,)), ((), ())), preferred_element_type=f32
-            )
-            out[:, l * LEAF : (l + 1) * LEAF] = (acc[l] * scale + far).astype(bf16)
-
-
-def near_stage(stage, place, near_list, pieces, *more):
-    shapes = [p.shape for p in pieces]
-    slots = sum(s[0] for s in shapes)
-    acc = jax.ShapeDtypeStruct((LEAVES_DEV, RHS, LEAF), f32)
-    tgt = jax.ShapeDtypeStruct((LEAVES_DEV, FEATS, LEAF), bf16)
-    scratch = [
-        pltpu.VMEM((slots * 8, RHS, LEAF), bf16),
-        pltpu.VMEM((slots * 8, FEATS, LEAF), bf16),
-        pltpu.VMEM((LEAVES_DEV, FEATS, LEAF), f32),
-    ]
-    specs = [SM, SM] + [VM] * len(pieces)
-    if stage == 0:
-        out_shape, out_specs = (acc, tgt), (VM, VM)
-    elif stage == 1:
-        out_shape, out_specs = acc, VM
-        specs += [VM, VM]
-    else:
-        out_shape, out_specs = jax.ShapeDtypeStruct((RHS, LEAVES_DEV * LEAF), bf16), VM
-        specs += [VM, VM, VM, ANY]
-        scratch += [
-            pltpu.VMEM((LEAVES_DEV, RHS, LEAF), f32),
-            pltpu.VMEM((LEAVES_DEV, LEAF, RANK), bf16),
-            pltpu.SemaphoreType.DMA,
-        ]
+    lax.fori_loop(first, last, one, 0)
+
+
+def own_kernel(step, acc_in, tgt, vals, feats, mine, theirs, acc, joined):
+    join(mine, theirs, joined)
+    own_blocks(SELF[step - 1], SELF[step], tgt, vals, feats, acc)
+
+
+def near_kernel(place, work, near1, near2, tgt, mine, theirs, a_, v_, f_, acc, vals, feats, joined, tmp):
+    join(mine, theirs, joined)
+    for slot in range(2, 6):
+        piece = near1 if slot < 4 else near2
+        load_cluster(piece.at[slot % 2], slot, place[1], vals, feats, tmp)
+    add_listed(1, work, tgt, vals, feats, acc)
+
+
+def last_kernel(place, work, far1, far2, tgt, down, basis, a_, v_, f_, acc, vals, feats, out, tmp):
+    for slot in range(6, 9):
+        block = far1.at[slot - 6] if slot < 8 else far2.at[0]
+        load_cluster(block, slot, place[1], vals, feats, tmp)
+    add_listed(2, work, tgt, vals, feats, acc)
+    scale = 1.0 / math.sqrt(NB * LEAF)
+    for l in range(LEAVES_DEV):
+        far = lax.dot_general(
+            down[...], basis[l], (((1,), (1,)), ((), ())), preferred_element_type=f32
+        )
+        out[:, l * LEAF : (l + 1) * LEAF] = (acc[l] * scale + far).astype(bf16)
+
+
+ACC = jax.ShapeDtypeStruct((LEAVES_DEV, RHS, LEAF), f32)
+TGT = jax.ShapeDtypeStruct((LEAVES_DEV, FEATS, LEAF), bf16)
+VALS = jax.ShapeDtypeStruct((9 * LEAVES_DEV, RHS, LEAF), bf16)
+FEAT = jax.ShapeDtypeStruct((9 * LEAVES_DEV, FEATS, LEAF), bf16)
+TMP = pltpu.VMEM((LEAVES_DEV, FEATS, LEAF), f32)
+
+
+def staged(kernel, smem, inputs, state, outs, blocks, scratch=(TMP,)):
+    ins = len(smem) + len(inputs)
+    state_shapes = [jax.ShapeDtypeStruct(s.shape, s.dtype) for s in state]
     return pl.pallas_call(
-        functools.partial(near_kernel, stage, shapes),
-        out_shape=out_shape,
-        in_specs=specs,
-        out_specs=out_specs,
-        scratch_shapes=scratch,
+        kernel,
+        out_shape=tuple(state_shapes) + tuple(outs),
+        in_specs=[SM] * len(smem) + [VM] * (len(inputs) + len(state)),
+        out_specs=(VM,) * (len(state) + len(outs)),
+        scratch_shapes=list(scratch),
+        input_output_aliases={ins + n: n for n in range(len(state))},
         compiler_params=params(40),
         cost_estimate=pl.CostEstimate(
-            flops=10**10, bytes_accessed=10**6, transcendentals=13 * 10**6
+            flops=blocks * 10**9, bytes_accessed=10**6, transcendentals=blocks * 10**6
         ),
-    )(place, near_list, *pieces, *more)
+    )(*smem, *inputs, *state)
 
 
 def tree_kernel(place, flags, coefs, transfer, coupling, out):
@@ -251,31 +254,97 @@
     )(place, flags, coefs, transfer, coupling)
 
 
+def work_list(near_list, me, sign):
+    offset = (near_list // LEAVES_DEV - me) * sign
+    slot = jnp.zeros_like(offset)
+    for n, o in enumerate(SLOT_OFFSETS):
+        slot = jnp.where(offset == o, n, slot)
+    return slot * LEAVES_DEV + near_list % LEAVES_DEV
+
+
+def gate_kernel(*refs):
+    pass
+
+
+def gate(array, after):
+    anywhere = pl.BlockSpec(memory_space=pl.ANY)
+    return pl.pallas_call(
+        gate_kernel,
+        out_shape=jax.ShapeDtypeStruct(array.shape, array.dtype),
+        in_specs=[anywhere, anywhere],
+        out_specs=anywhere,
+        input_output_aliases={0: 0},
+    )(array, after)
+
+
+def joined_shape(n):
+    return jax.ShapeDtypeStruct((n, RHS, RANK), f32)
+
+
+def partner(coefs, step):
+    return permuted(coefs, lambda i: i ^ (1 << step))
+
+
 def local(charges, points, leaf_basis, transfer, coupling, near_list, couple_flags):
     me = lax.axis_index("leaf")
     sign = 1 - 2 * (me % 2)
     place = jnp.stack([me, sign]).astype(jnp.int32)
+    work = work_list(near_list, me, sign)
 
     own = pack(charges, points)
     sib = permuted(own, lambda i: i ^ 1)
     pair = jnp.stack([own, sib])
     near1 = permuted(pair, lambda i: i - 1 if i % 2 == 0 else i + 1)
-    far1 = permuted(near1, lambda i: i - 2 if i % 2 == 0 else i + 2)
-    near2 = permuted(near1, lambda i: i ^ 1)
-    far2 = permuted(far1[:1], lambda i: i ^ 1)
 
     coefs = jnp.dot(
         charges,
         leaf_basis.reshape(LEAVES_DEV * LEAF, RANK),
         preferred_element_type=f32,
     )[None]
-    for step in range(5):
-        coefs = jnp.concatenate([coefs, permuted(coefs, lambda i: i ^ (1 << step))])
-
-    acc, tgt = near_stage(0, place, near_list, [pair])
-    acc = near_stage(1, place, near_list, [near1, near2], tgt, acc)
+    recv = partner(coefs, 0)
+    following = partner(jnp.concatenate([coefs, recv]), 1)
+    acc, tgt, vals, feats, coefs = staged(
+        first_kernel, [place], [pair, coefs, recv], [], [ACC, TGT, VALS, FEAT, joined_shape(2)], 2
+    )
+    for step in range(1, 4):
+        recv = following
+        following = partner(jnp.concatenate([coefs, recv]), step + 1)
+
+        def own_step(t, v, f, c, r, a, acc, joined, step=step):
+            own_kernel(step, a, t, v, f, c, r, acc, joined)
+
+        acc, coefs = staged(
+            own_step,
+            [],
+            [tgt, vals, feats, coefs, recv],
+            [acc],
+            [joined_shape(2 ** (step + 1))],
+            2,
+            (),
+        )
+        if step == 2:
+            near1 = gate(near1, coefs)
+            near2 = permuted(near1, lambda i: i ^ 1)
+            far1 = permuted(near1, lambda i: i - 2 if i % 2 == 0 else i + 2)
+    acc, vals, feats, coefs = staged(
+        near_kernel,
+        [place, work],
+        [near1, near2, tgt, coefs, following],
+        [acc, vals, feats],
+        [joined_shape(32)],
+        BUDGET,
+    )
+    far1 = gate(far1, coefs)
+    far2 = permuted(far1[:1], lambda i: i ^ 1)
     down = tree(place, couple_flags[0], coefs, transfer, coupling)
-    return near_stage(2, place, near_list, [far1, far2], tgt, acc, down, leaf_basis)
+    return staged(
+        last_kernel,
+        [place, work],
+        [far1, far2, tgt, down, leaf_basis],
+        [acc, vals, feats],
+        [jax.ShapeDtypeStruct((RHS, LEAVES_DEV * LEAF), bf16)],
+        21,
+    )[-1]
 
 
 def solution(mesh):

time: 92.1 us -> 98.6 us (1.071)
  the two profiles are of different devices: /device:TPU:187 before, /device:TPU:127 now
where the time goes in v2:
time: 98.6 us; the launch traced here: 97.9 us
  Pallas kernels  50.2 us (51%)
  local copies, waits for them, and re-layouts  20 us (20%)
  starting transfers between devices  16.2 us (16%)
  waiting for transfers between devices  8.31 us (8%)
  matrix products  1.97 us (2%)
  other arithmetic  1.02 us (1%)
    pallas_call x6, Pallas kernels, staged(): pl.pallas_call(kernel, out_shape=tuple(state_shapes) + tuple(outs), in_sp...  46.8 us
    unnamed x55, local copies, waits for them, and re-layouts  18.1 us
    ppermute x10, starting transfers between devices, permuted(): return lax.ppermute(array, 'leaf', route)  16.2 us
    ppermute x10, waiting for transfers between devices, permuted(): return lax.ppermute(array, 'leaf', route)  8.31 us
    pallas_call x1, Pallas kernels, tree(): pl.pallas_call(tree_kernel, out_shape=jax.ShapeDtypeStruct((RHS, RANK), b...  3.35 us
  transfers between devices with their start and end apart: 10, of which 4 were waited for; matrix products, arithmetic and copies ran while one was open for 3% of the time, Pallas kernels for 26%

profile of v2, /device:TPU:127, one launch (start us, length us, event | category | flops | bytes accessed | tf_op | source)
XLA Modules:
  0.0 97.9 jit_solution(8022589535126056747)
XLA Ops:
  0.0 0.9 copy-done.3
  1.0 0.8 copy-done.10
  1.8 0.8 collective-permute-start
  2.6 2.0 %convolution_bitcast_fusion.mine = f32[1,16,128]{2,1,0:T(8,128)S(1)} fusion(bf16[16,8192]{1,0:T(8,128)(2,1)S(1)} %copy-done.3, bf16[8192,128]{1,0:T(8,128)(2,1)} %bitcast.10), kind=kOutput, calls=%fused_computation | convolution fusion | flops 33554432 | bytes 2367488 | tf_op jit(solution)/shard_map/dot_general | solution.py:299
  4.8 1.1 %collective-permute-done.2.theirs = f32[1,16,128]{2,1,0:T(8,128)S(1)} collective-permute-done((f32[1,16,128]{2,1,0:T(8,128)S(1)}, f32[1,16,128]{2,1,0:T(8,128)S(1)}, u32[]{:S(2)}, u32[]{:S(2)}) %collective-permute-start.2) | collective-permute-done | bytes 8224 | tf_op jit(solution)/shard_map/ppermute | solution.py:36
  6.4 5.5 %collective-permute-start.1 = (bf16[2,19,16,512]{3,2,1,0:T(8,128)(2,1)S(1)}, bf16[2,19,16,512]{3,2,1,0:T(8,128)(2,1)S(1)}, u32[]{:S(2)}, u32[]{:S(2)}) collective-permute-start(bf16[2,19,16,512]{3,2,1,0:T(8,128)(2,1)S(1)} %pad_maximum_fusion.pair), channel_id=1, source_target_pairs={{2,1},{1,2},{4,3},{3,4},{6,5},{5,6},{8,7},{7,8},{10,9},{9,10},{12,... | collective-permute-start | bytes 1867784 | tf_op jit(solution)/shard_map/ppermute | solution.py:36
  11.9 3.1 %shard_map.74 = (f32[8,16,1024]{2,1,0:T(8,128)S(1)}, bf16[8,16,1024]{2,1,0:T(8,128)(2,1)S(1)}, bf16[72,16,1024]{2,1,0:T(8,128)(2,1)S(1)}, bf16[72,16,1024]{2,1,0:T(8,128)(2,1)S(1)}, f32[2,16,128]{2,1,0:T(8,128)S(1)}) custom-call(s32[2]{0:T(128)S(1)} %pad_add_fusion.place, bf16[2,19,16,512]{3,2,1,0:T(8,128)(2,1)S(1)} %pad_maximum_fusion.pair, ...), custom_call_target="tpu_custom_call" | custom-call | flops 2000000000 | bytes 1000000 | tf_op jit(solution)/shard_map/pallas_call | solution.py:195
  15.1 2.1 %shard_map.75 = (f32[8,16,1024]{2,1,0:T(8,128)S(1)}, f32[4,16,128]{2,1,0:T(8,128)S(1)}) custom-call(bf16[8,16,1024]{2,1,0:T(8,128)(2,1)S(1)} %get-tuple-element.21.t.tgt, bf16[72,16,1024]{2,1,0:T(8,128)(2,1)S(1)} %get-tuple-element.22.v.v_, bf16[72,16,1024]{2,1,0:T(8,128)(2,1)S(1)} %get-tuple-element.23.f.f_, ...), custom_call_target="tpu_custom_call", output_to_operand_aliasing={{0}: (5, {})} | custom-call | flops 2000000000 | bytes 1000000 | tf_op jit(solution)/shard_map/pallas_call | solution.py:195
  17.2 2.9 %collective-permute-done.4.r = f32[4,16,128]{2,1,0:T(8,128)S(1)} collective-permute-done((f32[4,16,128]{2,1,0:T(8,128)S(1)}, f32[4,16,128]{2,1,0:T(8,128)S(1)}, u32[]{:S(2)}, u32[]{:S(2)}) %collective-permute-start.4) | collective-permute-done | bytes 32800 | tf_op jit(solution)/shard_map/ppermute | solution.py:36
  20.1 2.1 %shard_map.76 = (f32[8,16,1024]{2,1,0:T(8,128)S(1)}, f32[8,16,128]{2,1,0:T(8,128)S(1)}) custom-call(bf16[8,16,1024]{2,1,0:T(8,128)(2,1)S(1)} %get-tuple-element.21.t.tgt, bf16[72,16,1024]{2,1,0:T(8,128)(2,1)S(1)} %get-tuple-element.22.v.v_, bf16[72,16,1024]{2,1,0:T(8,128)(2,1)S(1)} %get-tuple-element.23.f.f_, ...), custom_call_target="tpu_custom_call", output_to_operand_aliasing={{0}: (5, {})} | custom-call | flops 2000000000 | bytes 1000000 | tf_op jit(solution)/shard_map/pallas_call | solution.py:195
  22.8 1.3 %collective-permute-done.1.refs_0_ = bf16[2,19,16,512]{3,2,1,0:T(8,128)(2,1)S(1)} collective-permute-done((bf16[2,19,16,512]{3,2,1,0:T(8,128)(2,1)S(1)}, bf16[2,19,16,512]{3,2,1,0:T(8,128)(2,1)S(1)}, u32[]{:S(2)}, u32[]{:S(2)}) %collective-permute-start.1) | collective-permute-done | bytes 622624 | tf_op jit(solution)/shard_map/ppermute | solution.py:36
  24.1 0.9 copy-done.4
  25.1 3.1 %collective-permute-done.7.r = f32[8,16,128]{2,1,0:T(8,128)S(1)} collective-permute-done((f32[8,16,128]{2,1,0:T(8,128)S(1)}, f32[8,16,128]{2,1,0:T(8,128)S(1)}, u32[]{:S(2)}, u32[]{:S(2)}) %collective-permute-start.7) | collective-permute-done | bytes 65568 | tf_op jit(solution)/shard_map/ppermute | solution.py:36
  28.1 0.8 pad_maximum_fusion.1
  29.6 0.8 copy-done.7
  30.5 1.7 %copy-done.14 = bf16[72,16,1024]{2,1,0:T(8,128)(2,1)S(1)} copy-done((bf16[72,16,1024]{2,1,0:T(8,128)(2,1)S(1)}, bf16[72,16,1024]{2,1,0:T(8,128)(2,1)}, u32[]{:S(2)}) %copy-start.14) | copy-done | bytes 2359320
  32.2 1.7 %copy-done.18 = bf16[72,16,1024]{2,1,0:T(8,128)(2,1)S(1)} copy-done((bf16[72,16,1024]{2,1,0:T(8,128)(2,1)S(1)}, bf16[72,16,1024]{2,1,0:T(8,128)(2,1)}, u32[]{:S(2)}) %copy-start.18) | copy-done | bytes 2359320
  33.8 2.1 %shard_map.78 = (f32[8,16,1024]{2,1,0:T(8,128)S(1)}, f32[16,16,128]{2,1,0:T(8,128)S(1)}) custom-call(bf16[8,16,1024]{2,1,0:T(8,128)(2,1)S(1)} %get-tuple-element.21.t.tgt, bf16[72,16,1024]{2,1,0:T(8,128)(2,1)S(1)} %copy-done.14, bf16[72,16,1024]{2,1,0:T(8,128)(2,1)S(1)} %copy-done.18, f32[8,16,128]{2,1,0:T(8,128)S(1)} %copy-done.7, ...), custom_call_target="tpu_custom_call", output_to_operand_aliasing={{0}: (5, {})} | custom-call | flops 2000000000 | bytes 1000000 | tf_op jit(solution)/shard_map/pallas_call | solution.py:195
  35.9 1.9 %collective-permute-start.5 = (bf16[2,19,16,512]{3,2,1,0:T(8,128)(2,1)S(1)}, bf16[2,19,16,512]{3,2,1,0:T(8,128)(2,1)S(1)}, u32[]{:S(2)}, u32[]{:S(2)}) collective-permute-start(bf16[2,19,16,512]{3,2,1,0:T(8,128)(2,1)S(1)} %copy-done.5), channel_id=1, source_target_pairs={{3,1},{0,2},{5,3},{2,4},{7,5},{4,6},{9,7},{6,8},{11,9},{8,10},{13,... | collective-permute-start | bytes 1867784 | tf_op jit(solution)/shard_map/ppermute | solution.py:36
  37.9 12.8 %shard_map.79 = (f32[8,16,1024]{2,1,0:T(8,128)S(1)}, bf16[72,16,1024]{2,1,0:T(8,128)(2,1)S(1)}, bf16[72,16,1024]{2,1,0:T(8,128)(2,1)S(1)}, f32[32,16,128]{2,1,0:T(8,128)S(1)}) custom-call(s32[2]{0:T(128)S(1)} %pad_add_fusion.place, s32[8,5]{1,0:T(8,128)S(1)} %fusion.2.work, ...), custom_call_target="tpu_custom_call", output_to_operand_aliasing={{0}: (7, {}), {1}: (8, {}), {2}: (9, {})} | custom-call | flops 11000000512 | bytes 1000000 | tf_op jit(solution)/shard_map/pallas_call | solution.py:195
  51.4 1.4 %copy-done.15 = bf16[72,16,1024]{2,1,0:T(8,128)(2,1)} copy-done((bf16[72,16,1024]{2,1,0:T(8,128)(2,1)}, bf16[72,16,1024]{2,1,0:T(8,128)(2,1)S(1)}, u32[]{:S(2)}) %copy-start.15) | copy-done | bytes 2359320
  52.9 1.4 %copy-done.19 = bf16[72,16,1024]{2,1,0:T(8,128)(2,1)} copy-done((bf16[72,16,1024]{2,1,0:T(8,128)(2,1)}, bf16[72,16,1024]{2,1,0:T(8,128)(2,1)S(1)}, u32[]{:S(2)}) %copy-start.19) | copy-done | bytes 2359320
  54.3 0.8 copy-done.21
  55.1 0.9 copy-done.1
  56.0 1.8 %slice.4 = bf16[1,19,16,512]{3,2,1,0:T(8,128)(2,1)} slice(bf16[2,19,16,512]{3,2,1,0:T(8,128)(2,1)} %shard_map.80.far1), slice={[0:1], [0:19], [0:16], [0:512]} | slice | bytes 622592 | tf_op jit(solution)/shard_map/slice | solution.py:338
  57.8 6.6 %collective-permute-start.9 = (bf16[1,19,16,512]{3,2,1,0:T(8,128)(2,1)}, bf16[1,19,16,512]{3,2,1,0:T(8,128)(2,1)}, u32[]{:S(2)}, u32[]{:S(2)}) collective-permute-start(bf16[1,19,16,512]{3,2,1,0:T(8,128)(2,1)} %slice.4), channel_id=1, source_target_pairs={{1,0},{0,1},{3,2},{2,3},{5,4},{4,5},{7,6},{6,7},{9,8},{8,9},{11,10... | collective-permute-start | bytes 933896 | tf_op jit(solution)/shard_map/ppermute | solution.py:36
  64.5 0.9 copy-done.9
  65.5 1.0 %copy-done.12 = f32[4,2,128,128]{3,2,1,0:T(8,128)S(1)} copy-done((f32[4,2,128,128]{3,2,1,0:T(8,128)S(1)}, f32[4,2,128,128]{3,2,1,0:T(8,128)}, u32[]{:S(2)}) %copy-start.12) | copy-done | bytes 524312
  66.5 3.3 %shard_map.81.down = bf16[16,128]{1,0:T(8,128)(2,1)S(1)} custom-call(s32[2]{0:T(128)S(1)} %pad_add_fusion.place, s32[4,3]{1,0:T(4,128)S(1)} %bitcast.12, f32[32,16,128]{2,1,0:T(8,128)S(1)} %copy-done.9, f32[4,2,128,128]{3,2,1,0:T(8,128)S(1)} %copy-done.12, f32[4,3,128,128]{3,2,1,0:T(8,128)S(1)} %copy-done.11), custom_call_target="tpu_custom_call" | custom-call | flops 1000000000 | bytes 1000000 | tf_op jit(solution)/shard_map/pallas_call | solution.py:247
  69.9 1.7 %copy-done.16 = bf16[72,16,1024]{2,1,0:T(8,128)(2,1)S(1)} copy-done((bf16[72,16,1024]{2,1,0:T(8,128)(2,1)S(1)}, bf16[72,16,1024]{2,1,0:T(8,128)(2,1)}, u32[]{:S(2)}) %copy-start.16) | copy-done | bytes 2359320
  71.6 1.7 %copy-done.20 = bf16[72,16,1024]{2,1,0:T(8,128)(2,1)S(1)} copy-done((bf16[72,16,1024]{2,1,0:T(8,128)(2,1)S(1)}, bf16[72,16,1024]{2,1,0:T(8,128)(2,1)}, u32[]{:S(2)}) %copy-start.20) | copy-done | bytes 2359320
  73.3 24.7 %shard_map.82 = (f32[8,16,1024]{2,1,0:T(8,128)S(1)}, bf16[72,16,1024]{2,1,0:T(8,128)(2,1)S(1)}, bf16[72,16,1024]{2,1,0:T(8,128)(2,1)S(1)}, bf16[16,8192]{1,0:T(8,128)(2,1)}) custom-call(s32[2]{0:T(128)S(1)} %pad_add_fusion.place, s32[8,5]{1,0:T(8,128)S(1)} %fusion.2.work, ...), custom_call_target="tpu_custom_call", output_to_operand_aliasing={{0}: (7, {}), {1}: (8, {}), {2}: (9, {})} | custom-call | flops 20999999488 | bytes 1000000 | tf_op jit(solution)/shard_map/pallas_call | solution.py:195
  (62 shorter events, 3.1 us)
Async XLA Ops:
  0.0 0.9 copy-start.3
  1.8 4.5 %collective-permute-start = (bf16[19,16,512]{2,1,0:T(8,128)(2,1)S(1)}, bf16[19,16,512]{2,1,0:T(8,128)(2,1)S(1)}, u32[]{:S(2)}, u32[]{:S(2)}) collective-permute-start(bf16[19,16,512]{2,1,0:T(8,128)(2,1)S(1)} %shard_map.73), channel_id=1, source_target_pairs={{1,0},{0,1},{3,2},{2,3},{5,4},{4,5},{7,6},{6,7},{9,8},{8,9},{11,10... | collective-permute-start | bytes 933896 | tf_op jit(solution)/shard_map/ppermute | solution.py:36
  4.6 1.3 %collective-permute-start.2 = (f32[1,16,128]{2,1,0:T(8,128)S(1)}, f32[1,16,128]{2,1,0:T(8,128)S(1)}, u32[]{:S(2)}, u32[]{:S(2)}) collective-permute-start(f32[1,16,128]{2,1,0:T(8,128)S(1)} %convolution_bitcast_fusion.mine), channel_id=1, source_target_pairs={{1,0},{0,1},{3,2},{2,3},{5,4},{4,5},{7,6},{6,7},{9,8},{8,9},{11,10... | collective-permute-start | bytes 24584 | tf_op jit(solution)/shard_map/ppermute | solution.py:36
  5.8 9.1 %collective-permute-start.3 = (f32[2,16,128]{2,1,0:T(8,128)S(1)}, f32[2,16,128]{2,1,0:T(8,128)S(1)}, u32[]{:S(2)}, u32[]{:S(2)}) collective-permute-start(f32[2,16,128]{2,1,0:T(8,128)S(1)} %pad_maximum_fusion.4), channel_id=1, source_target_pairs={{2,0},{3,1},{0,2},{1,3},{6,4},{7,5},{4,6},{5,7},{10,8},{11,9},{8,1... | collective-permute-start | bytes 49160 | tf_op jit(solution)/shard_map/ppermute | solution.py:36
  6.4 17.7 %collective-permute-start.1 = (bf16[2,19,16,512]{3,2,1,0:T(8,128)(2,1)S(1)}, bf16[2,19,16,512]{3,2,1,0:T(8,128)(2,1)S(1)}, u32[]{:S(2)}, u32[]{:S(2)}) collective-permute-start(bf16[2,19,16,512]{3,2,1,0:T(8,128)(2,1)S(1)} %pad_maximum_fusion.pair), channel_id=1, source_target_pairs={{2,1},{1,2},{4,3},{3,4},{6,5},{5,6},{8,7},{7,8},{10,9},{9,10},{12,... | collective-permute-start | bytes 1867784 | tf_op jit(solution)/shard_map/ppermute | solution.py:36
  15.0 5.1 %copy-start.13 = (bf16[72,16,1024]{2,1,0:T(8,128)(2,1)}, bf16[72,16,1024]{2,1,0:T(8,128)(2,1)S(1)}, u32[]{:S(2)}) copy-start(bf16[72,16,1024]{2,1,0:T(8,128)(2,1)S(1)} %get-tuple-element.22.v.v_) | copy-start | bytes 7077892
  15.0 5.1 %copy-start.17 = (bf16[72,16,1024]{2,1,0:T(8,128)(2,1)}, bf16[72,16,1024]{2,1,0:T(8,128)(2,1)S(1)}, u32[]{:S(2)}) copy-start(bf16[72,16,1024]{2,1,0:T(8,128)(2,1)S(1)} %get-tuple-element.23.f.f_) | copy-start | bytes 7077892
  15.0 22.9 %copy-start.23 = (bf16[8,16,1024]{2,1,0:T(8,128)(2,1)}, bf16[8,16,1024]{2,1,0:T(8,128)(2,1)S(1)}, u32[]{:S(2)}) copy-start(bf16[8,16,1024]{2,1,0:T(8,128)(2,1)S(1)} %get-tuple-element.21.t.tgt) | copy-start | bytes 786436
  15.0 5.1 %collective-permute-start.4 = (f32[4,16,128]{2,1,0:T(8,128)S(1)}, f32[4,16,128]{2,1,0:T(8,128)S(1)}, u32[]{:S(2)}, u32[]{:S(2)}) collective-permute-start(f32[4,16,128]{2,1,0:T(8,128)S(1)} %pad_maximum_fusion.3), channel_id=1, source_target_pairs={{4,0},{5,1},{6,2},{7,3},{0,4},{1,5},{2,6},{3,7},{12,8},{13,9},{14,... | collective-permute-start | bytes 98312 | tf_op jit(solution)/shard_map/ppermute | solution.py:36
  20.1 5.0 %copy-start.25 = (s32[8,5]{1,0:T(8,128)S(1)}, s32[8,5]{1,0:T(8,128)}, u32[]{:S(2)}) copy-start(s32[8,5]{1,0:T(8,128)} %param.12) | copy-start | bytes 484
  24.1 0.9 copy-start.4
  24.9 12.9 %collective-permute-start.6 = (bf16[2,19,16,512]{3,2,1,0:T(8,128)(2,1)}, bf16[2,19,16,512]{3,2,1,0:T(8,128)(2,1)S(1)}, u32[]{:S(2)}, u32[]{:S(2)}) collective-permute-start(bf16[2,19,16,512]{3,2,1,0:T(8,128)(2,1)} %shard_map.77.near1), channel_id=1, source_target_pairs={{1,0},{0,1},{3,2},{2,3},{5,4},{4,5},{7,6},{6,7},{9,8},{8,9},{11,10... | collective-permute-start | bytes 1867784 | tf_op jit(solution)/shard_map/ppermute | solution.py:36
  24.9 3.2 %collective-permute-start.7 = (f32[8,16,128]{2,1,0:T(8,128)S(1)}, f32[8,16,128]{2,1,0:T(8,128)S(1)}, u32[]{:S(2)}, u32[]{:S(2)}) collective-permute-start(f32[8,16,128]{2,1,0:T(8,128)S(1)} %pad_maximum_fusion.2), channel_id=1, source_target_pairs={{8,0},{9,1},{10,2},{11,3},{12,4},{13,5},{14,6},{15,7},{0,8},{1,9},... | collective-permute-start | bytes 196616 | tf_op jit(solution)/shard_map/ppermute | solution.py:36
  29.0 8.8 %collective-permute-start.8 = (f32[16,16,128]{2,1,0:T(8,128)S(1)}, f32[16,16,128]{2,1,0:T(8,128)S(1)}, u32[]{:S(2)}, u32[]{:S(2)}) collective-permute-start(f32[16,16,128]{2,1,0:T(8,128)S(1)} %pad_maximum_fusion.1), channel_id=1, source_target_pairs={{16,0},{17,1},{18,2},{19,3},{20,4},{21,5},{22,6},{23,7},{24,8},{25... | collective-permute-start | bytes 393224 | tf_op jit(solution)/shard_map/ppermute | solution.py:36
  30.5 1.7 %copy-start.14 = (bf16[72,16,1024]{2,1,0:T(8,128)(2,1)S(1)}, bf16[72,16,1024]{2,1,0:T(8,128)(2,1)}, u32[]{:S(2)}) copy-start(bf16[72,16,1024]{2,1,0:T(8,128)(2,1)} %copy-done.13) | copy-start | bytes 7077892
  32.2 1.7 %copy-start.18 = (bf16[72,16,1024]{2,1,0:T(8,128)(2,1)S(1)}, bf16[72,16,1024]{2,1,0:T(8,128)(2,1)}, u32[]{:S(2)}) copy-start(bf16[72,16,1024]{2,1,0:T(8,128)(2,1)} %copy-done.17) | copy-start | bytes 7077892
  33.8 2.1 %copy-start.5 = (bf16[2,19,16,512]{3,2,1,0:T(8,128)(2,1)S(1)}, bf16[2,19,16,512]{3,2,1,0:T(8,128)(2,1)}, u32[]{:S(2)}) copy-start(bf16[2,19,16,512]{3,2,1,0:T(8,128)(2,1)} %shard_map.77.near1) | copy-start | bytes 1867780
  35.9 19.2 %collective-permute-start.5 = (bf16[2,19,16,512]{3,2,1,0:T(8,128)(2,1)S(1)}, bf16[2,19,16,512]{3,2,1,0:T(8,128)(2,1)S(1)}, u32[]{:S(2)}, u32[]{:S(2)}) collective-permute-start(bf16[2,19,16,512]{3,2,1,0:T(8,128)(2,1)S(1)} %copy-done.5), channel_id=1, source_target_pairs={{3,1},{0,2},{5,3},{2,4},{7,5},{4,6},{9,7},{6,8},{11,9},{8,10},{13,... | collective-permute-start | bytes 1867784 | tf_op jit(solution)/shard_map/ppermute | solution.py:36
  37.9 26.6 %copy-start.26 = (s32[1,4,3]{1,0,2:T(1,128)S(1)}, s32[1,4,3]{1,0,2:T(1,128)}, u32[]{:S(2)}) copy-start(s32[1,4,3]{1,0,2:T(1,128)} %param.13) | copy-start | bytes 148
  37.9 26.6 %copy-start.11 = (f32[4,3,128,128]{3,2,1,0:T(8,128)S(1)}, f32[4,3,128,128]{3,2,1,0:T(8,128)}, u32[]{:S(2)}) copy-start(f32[4,3,128,128]{3,2,1,0:T(8,128)} %coupling.1) | copy-start | bytes 2359300
  51.4 1.4 %copy-start.15 = (bf16[72,16,1024]{2,1,0:T(8,128)(2,1)}, bf16[72,16,1024]{2,1,0:T(8,128)(2,1)S(1)}, u32[]{:S(2)}) copy-start(bf16[72,16,1024]{2,1,0:T(8,128)(2,1)S(1)} %get-tuple-element.34.v_) | copy-start | bytes 7077892
  52.9 1.4 %copy-start.19 = (bf16[72,16,1024]{2,1,0:T(8,128)(2,1)}, bf16[72,16,1024]{2,1,0:T(8,128)(2,1)S(1)}, u32[]{:S(2)}) copy-start(bf16[72,16,1024]{2,1,0:T(8,128)(2,1)S(1)} %get-tuple-element.35.f_) | copy-start | bytes 7077892
  55.1 0.9 copy-start.1
  56.0 13.9 %copy-start = (bf16[8,1024,128]{2,1,0:T(8,128)(2,1)S(1)}, bf16[8,1024,128]{2,1,0:T(8,128)(2,1)}, u32[]{:S(2)}) copy-start(bf16[8,1024,128]{2,1,0:T(8,128)(2,1)} %basis.1) | copy-start | bytes 6291460
  56.0 13.9 %copy-start.2 = (bf16[2,19,16,512]{3,2,1,0:T(8,128)(2,1)S(1)}, bf16[2,19,16,512]{3,2,1,0:T(8,128)(2,1)}, u32[]{:S(2)}) copy-start(bf16[2,19,16,512]{3,2,1,0:T(8,128)(2,1)} %shard_map.80.far1) | copy-start | bytes 1867780
  57.8 12.0 %collective-permute-start.9 = (bf16[1,19,16,512]{3,2,1,0:T(8,128)(2,1)}, bf16[1,19,16,512]{3,2,1,0:T(8,128)(2,1)}, u32[]{:S(2)}, u32[]{:S(2)}) collective-permute-start(bf16[1,19,16,512]{3,2,1,0:T(8,128)(2,1)} %slice.4), channel_id=1, source_target_pairs={{1,0},{0,1},{3,2},{2,3},{5,4},{4,5},{7,6},{6,7},{9,8},{8,9},{11,10... | collective-permute-start | bytes 933896 | tf_op jit(solution)/shard_map/ppermute | solution.py:36
  64.5 1.0 copy-start.9
  65.5 1.0 %copy-start.12 = (f32[4,2,128,128]{3,2,1,0:T(8,128)S(1)}, f32[4,2,128,128]{3,2,1,0:T(8,128)}, u32[]{:S(2)}) copy-start(f32[4,2,128,128]{3,2,1,0:T(8,128)} %transfer.1) | copy-start | bytes 1572868
  66.5 3.4 %copy-start.22 = (f32[8,16,1024]{2,1,0:T(8,128)S(1)}, f32[8,16,1024]{2,1,0:T(8,128)}, u32[]{:S(2)}) copy-start(f32[8,16,1024]{2,1,0:T(8,128)} %copy-done.21) | copy-start | bytes 1572868
  66.5 3.4 %copy-start.24 = (bf16[8,16,1024]{2,1,0:T(8,128)(2,1)S(1)}, bf16[8,16,1024]{2,1,0:T(8,128)(2,1)}, u32[]{:S(2)}) copy-start(bf16[8,16,1024]{2,1,0:T(8,128)(2,1)} %copy-done.23) | copy-start | bytes 786436
  69.9 1.7 %copy-start.16 = (bf16[72,16,1024]{2,1,0:T(8,128)(2,1)S(1)}, bf16[72,16,1024]{2,1,0:T(8,128)(2,1)}, u32[]{:S(2)}) copy-start(bf16[72,16,1024]{2,1,0:T(8,128)(2,1)} %copy-done.15) | copy-start | bytes 7077892
  71.6 1.7 %copy-start.20 = (bf16[72,16,1024]{2,1,0:T(8,128)(2,1)S(1)}, bf16[72,16,1024]{2,1,0:T(8,128)(2,1)}, u32[]{:S(2)}) copy-start(bf16[72,16,1024]{2,1,0:T(8,128)(2,1)} %copy-done.19) | copy-start | bytes 7077892
  (5 other events, 3.8 us)

commit v3 on v2

--- a/solution.py
+++ b/solution.py
@@ -22,7 +22,7 @@
 VM = pl.BlockSpec(memory_space=pltpu.VMEM)
 SM = pl.BlockSpec(memory_space=pltpu.SMEM)
 SLOT_OFFSETS = (0, 1, -1, -2, 2, 3, -3, -4, 4)
-SELF = (2, 4, 6, 8)
+SELF = (2, 5, 8)
 BUDGET = 11
 
 
@@ -36,9 +36,12 @@
     return lax.ppermute(array, "leaf", route)
 
 
-def pack_kernel(charges, points, out, rows):
-    for k in range(16):
-        out[k] = charges[:, k * HALF : (k + 1) * HALF]
+def pack_kernel(charges_hbm, points_hbm, out, charges, points, rows, sems):
+    get_points = pltpu.make_async_copy(points_hbm, points, sems.at[0])
+    get_charges = pltpu.make_async_copy(charges_hbm, charges, sems.at[1])
+    get_points.start()
+    get_charges.start()
+    get_points.wait()
     for l in range(LEAVES_DEV):
         for h in range(2):
             start = l * LEAF + h * HALF
@@ -48,16 +51,25 @@
                 rows[row : row + 1, :] = part[c : c + 1]
     for k in range(3):
         out[16 + k] = rows[k * 16 : (k + 1) * 16, :].astype(bf16)
+    get_charges.wait()
+    for k in range(16):
+        out[k] = charges[:, k * HALF : (k + 1) * HALF]
 
 
 def pack(charges, points):
+    anywhere = pl.BlockSpec(memory_space=pl.ANY)
     return pl.pallas_call(
         pack_kernel,
         out_shape=jax.ShapeDtypeStruct(PAYLOAD, bf16),
-        in_specs=[VM, VM],
+        in_specs=[anywhere, anywhere],
         out_specs=VM,
-        scratch_shapes=[pltpu.VMEM((48, HALF), f32)],
-        compiler_params=params(16),
+        scratch_shapes=[
+            pltpu.VMEM(charges.shape, bf16),
+            pltpu.VMEM(points.shape, bf16),
+            pltpu.VMEM((48, HALF), f32),
+            pltpu.SemaphoreType.DMA((2,)),
+        ],
+        compiler_params=params(4),
         cost_estimate=pl.CostEstimate(flops=10**6, bytes_accessed=10**6, transcendentals=0),
     )(charges, points)
 
@@ -169,10 +181,18 @@
     add_listed(1, work, tgt, vals, feats, acc)
 
 
-def last_kernel(place, work, far1, far2, tgt, down, basis, a_, v_, f_, acc, vals, feats, out, tmp):
-    for slot in range(6, 9):
-        block = far1.at[slot - 6] if slot < 8 else far2.at[0]
-        load_cluster(block, slot, place[1], vals, feats, tmp)
+def tree_kernel(
+    place, flags, far1, mine, theirs, transfer, coupling, v_, f_, vals, feats, down, tmp
+):
+    for slot in range(6, 8):
+        load_cluster(far1.at[slot - 6], slot, place[1], vals, feats, tmp)
+    n = mine.shape[0]
+    coefs = [mine[m] for m in range(n)] + [theirs[m] for m in range(n)]
+    down[...] = tree(place[0], flags, coefs, transfer, coupling)
+
+
+def last_kernel(place, work, far2, tgt, down, basis, a_, v_, f_, acc, vals, feats, out, tmp):
+    load_cluster(far2.at[0], 8, place[1], vals, feats, tmp)
     add_listed(2, work, tgt, vals, feats, acc)
     scale = 1.0 / math.sqrt(NB * LEAF)
     for l in range(LEAVES_DEV):
@@ -199,21 +219,19 @@
         out_specs=(VM,) * (len(state) + len(outs)),
         scratch_shapes=list(scratch),
         input_output_aliases={ins + n: n for n in range(len(state))},
-        compiler_params=params(40),
+        compiler_params=params(16),
         cost_estimate=pl.CostEstimate(
             flops=blocks * 10**9, bytes_accessed=10**6, transcendentals=blocks * 10**6
         ),
     )(*smem, *inputs, *state)
 
 
-def tree_kernel(place, flags, coefs, transfer, coupling, out):
-    me = place[0]
-
+def tree(me, flags, coefs, transfer, coupling):
     def dot(a, b):
         return jnp.dot(a, b, precision=lax.Precision.HIGHEST, preferred_element_type=f32)
 
     levels = 4
-    cur = [coefs[m] for m in range(32)]
+    cur = coefs
     coupled = []
     for t in range(levels):
         total = jnp.zeros((RHS, RANK), f32)
@@ -240,18 +258,7 @@
             precision=lax.Precision.HIGHEST,
             preferred_element_type=f32,
         )
-    out[...] = local.astype(bf16)
-
-
-def tree(place, flags, coefs, transfer, coupling):
-    return pl.pallas_call(
-        tree_kernel,
-        out_shape=jax.ShapeDtypeStruct((RHS, RANK), bf16),
-        in_specs=[SM, SM, VM, VM, VM],
-        out_specs=VM,
-        compiler_params=params(16),
-        cost_estimate=pl.CostEstimate(flops=10**9, bytes_accessed=10**6, transcendentals=0),
-    )(place, flags, coefs, transfer, coupling)
+    return local.astype(bf16)
 
 
 def work_list(near_list, me, sign):
@@ -267,13 +274,27 @@
 
 
 def gate(array, after):
-    anywhere = pl.BlockSpec(memory_space=pl.ANY)
     return pl.pallas_call(
         gate_kernel,
         out_shape=jax.ShapeDtypeStruct(array.shape, array.dtype),
-        in_specs=[anywhere, anywhere],
-        out_specs=anywhere,
+        in_specs=[VM, VM],
+        out_specs=VM,
         input_output_aliases={0: 0},
+        compiler_params=params(2),
+    )(array, after)
+
+
+def gate_copy_kernel(array, after, out):
+    out[0] = array[0]
+
+
+def gate_first(array, after):
+    return pl.pallas_call(
+        gate_copy_kernel,
+        out_shape=jax.ShapeDtypeStruct((1,) + array.shape[1:], array.dtype),
+        in_specs=[VM, VM],
+        out_specs=VM,
+        compiler_params=params(2),
     )(array, after)
 
 
@@ -306,7 +327,7 @@
     acc, tgt, vals, feats, coefs = staged(
         first_kernel, [place], [pair, coefs, recv], [], [ACC, TGT, VALS, FEAT, joined_shape(2)], 2
     )
-    for step in range(1, 4):
+    for step in range(1, 3):
         recv = following
         following = partner(jnp.concatenate([coefs, recv]), step + 1)
 
@@ -319,28 +340,36 @@
             [tgt, vals, feats, coefs, recv],
             [acc],
             [joined_shape(2 ** (step + 1))],
-            2,
+            3,
             (),
         )
-        if step == 2:
+        if step == 1:
             near1 = gate(near1, coefs)
             near2 = permuted(near1, lambda i: i ^ 1)
             far1 = permuted(near1, lambda i: i - 2 if i % 2 == 0 else i + 2)
+    recv = following
+    following = partner(jnp.concatenate([coefs, recv]), 4)
     acc, vals, feats, coefs = staged(
         near_kernel,
         [place, work],
-        [near1, near2, tgt, coefs, following],
+        [near1, near2, tgt, coefs, recv],
         [acc, vals, feats],
-        [joined_shape(32)],
+        [joined_shape(16)],
         BUDGET,
     )
-    far1 = gate(far1, coefs)
-    far2 = permuted(far1[:1], lambda i: i ^ 1)
-    down = tree(place, couple_flags[0], coefs, transfer, coupling)
+    far2 = permuted(gate_first(far1, coefs), lambda i: i ^ 1)
+    vals, feats, down = staged(
+        tree_kernel,
+        [place, couple_flags[0]],
+        [far1, coefs, following, transfer, coupling],
+        [vals, feats],
+        [jax.ShapeDtypeStruct((RHS, RANK), bf16)],
+        3,
+    )
     return staged(
         last_kernel,
         [place, work],
-        [far1, far2, tgt, down, leaf_basis],
+        [far2, tgt, down, leaf_basis],
         [acc, vals, feats],
         [jax.ShapeDtypeStruct((RHS, LEAVES_DEV * LEAF), bf16)],
         21,

time: 98.6 us -> 84 us (0.85)
  local copies, waits for them, and re-layouts: 20 us -> 8.12 us
  waiting for transfers between devices: 8.31 us -> 5.7 us
  starting transfers between devices: 16.2 us -> 17.4 us
    unnamed x55 -> x27, local copies, waits for them, and re-layouts: 18.1 us -> 8.12 us
    pallas_call x1, Pallas kernels: 3.35 us -> 0.02 us  [gate_first(): pl.pallas_call(gate_copy_kernel, out_shape=jax.ShapeDtypeStruct((1,) + ar...]
    pallas_call x6, Pallas kernels: 46.8 us -> 49.9 us  [staged(): pl.pallas_call(kernel, out_shape=tuple(state_shapes) + tuple(outs), in_sp...]
    ppermute x10, waiting for transfers between devices: 8.31 us -> 5.7 us  [permuted(): return lax.ppermute(array, 'leaf', route)]
    slice x1 -> x0, local copies, waits for them, and re-layouts: 1.85 us -> none  [local(): far2 = permuted(far1[:1], lambda i: i ^ 1)]
    ppermute x10, starting transfers between devices: 16.2 us -> 17.4 us  [permuted(): return lax.ppermute(array, 'leaf', route)]
  transfers between devices with their start and end apart: 10 -> 10, of which waited for: 4 -> 2; matrix products, arithmetic and copies ran while one was open for 3% -> 3% of each run, Pallas kernels for 26% -> 31%
where the time goes in v3:
time: 84 us; the launch traced here: 83.7 us
  Pallas kernels  50 us (60%)
  starting transfers between devices  17.4 us (21%)
  local copies, waits for them, and re-layouts  8.12 us (10%)
  waiting for transfers between devices  5.7 us (7%)
  matrix products  2.07 us (2%)
    pallas_call x6, Pallas kernels, staged(): pl.pallas_call(kernel, out_shape=tuple(state_shapes) + tuple(outs), in_sp...  49.9 us
    ppermute x10, starting transfers between devices, permuted(): return lax.ppermute(array, 'leaf', route)  17.4 us
    unnamed x27, local copies, waits for them, and re-layouts  8.12 us
    ppermute x10, waiting for transfers between devices, permuted(): return lax.ppermute(array, 'leaf', route)  5.7 us
    dot_general x1, matrix products, local(): jnp.dot(charges, leaf_basis.reshape(LEAVES_DEV * LEAF, RANK), preferred_e...  2.07 us
  transfers between devices with their start and end apart: 10, of which 2 were waited for; matrix products, arithmetic and copies ran while one was open for 3% of the time, Pallas kernels for 31%

profile of v3, /device:TPU:127, one launch (start us, length us, event | category | flops | bytes accessed | tf_op | source)
XLA Modules:
  0.0 83.7 jit_solution(15600059284731661407)
XLA Ops:
  0.0 0.9 %copy-done.1 = bf16[16,8192]{1,0:T(8,128)(2,1)S(1)} copy-done((bf16[16,8192]{1,0:T(8,128)(2,1)S(1)}, bf16[16,8192]{1,0:T(8,128)(2,1)}, u32[]{:S(2)}) %copy-start.1) | copy-done | bytes 262168
  1.0 0.8 %copy-done.2 = bf16[3,8192]{1,0:T(4,128)(2,1)S(1)} copy-done((bf16[3,8192]{1,0:T(4,128)(2,1)S(1)}, bf16[3,8192]{1,0:T(4,128)(2,1)}, u32[]{:S(2)}) %copy-start.2) | copy-done | bytes 49176
  1.8 0.1 shard_map.73
  1.9 0.8 collective-permute-start
  2.7 2.1 %convolution_bitcast_fusion.mine = f32[1,16,128]{2,1,0:T(8,128)S(1)} fusion(bf16[16,8192]{1,0:T(8,128)(2,1)} %charges_hbm.1, bf16[8192,128]{1,0:T(8,128)(2,1)} %bitcast.10), kind=kOutput, calls=%fused_computation | convolution fusion | flops 33554432 | bytes 2367488 | tf_op jit(solution)/shard_map/dot_general | solution.py:320
  4.8 0.1 collective-permute-start.2
  4.9 0.1 pad_add_fusion.place
  5.0 0.1 pad_maximum_fusion.pair
  5.0 4.7 %collective-permute-start.1 = (bf16[2,19,16,512]{3,2,1,0:T(8,128)(2,1)S(1)}, bf16[2,19,16,512]{3,2,1,0:T(8,128)(2,1)S(1)}, u32[]{:S(2)}, u32[]{:S(2)}) collective-permute-start(bf16[2,19,16,512]{3,2,1,0:T(8,128)(2,1)S(1)} %pad_maximum_fusion.pair), channel_id=1, source_target_pairs={{2,1},{1,2},{4,3},{3,4},{6,5},{5,6},{8,7},{7,8},{10,9},{9,10},{12,... | collective-permute-start | bytes 1867784 | tf_op jit(solution)/shard_map/ppermute | solution.py:36
  9.8 0.1 collective-permute-start.3
  9.9 3.1 %shard_map.74 = (f32[8,16,1024]{2,1,0:T(8,128)S(1)}, bf16[8,16,1024]{2,1,0:T(8,128)(2,1)S(1)}, bf16[72,16,1024]{2,1,0:T(8,128)(2,1)S(1)}, bf16[72,16,1024]{2,1,0:T(8,128)(2,1)S(1)}, f32[2,16,128]{2,1,0:T(8,128)S(1)}) custom-call(s32[2]{0:T(128)S(1)} %pad_add_fusion.place, bf16[2,19,16,512]{3,2,1,0:T(8,128)(2,1)S(1)} %pad_maximum_fusion.pair, ...), custom_call_target="tpu_custom_call" | custom-call | flops 2000000000 | bytes 1000000 | tf_op jit(solution)/shard_map/pallas_call | solution.py:215
  12.9 3.9 %collective-permute-done.3.r = f32[2,16,128]{2,1,0:T(8,128)S(1)} collective-permute-done((f32[2,16,128]{2,1,0:T(8,128)S(1)}, f32[2,16,128]{2,1,0:T(8,128)S(1)}, u32[]{:S(2)}, u32[]{:S(2)}) %collective-permute-start.3) | collective-permute-done | bytes 16416 | tf_op jit(solution)/shard_map/ppermute | solution.py:36
  16.9 1.0 %collective-permute-start.6 = (f32[4,16,128]{2,1,0:T(8,128)S(1)}, f32[4,16,128]{2,1,0:T(8,128)S(1)}, u32[]{:S(2)}, u32[]{:S(2)}) collective-permute-start(f32[4,16,128]{2,1,0:T(8,128)S(1)} %pad_maximum_fusion.3), channel_id=1, source_target_pairs={{4,0},{5,1},{6,2},{7,3},{0,4},{1,5},{2,6},{3,7},{12,8},{13,9},{14,... | collective-permute-start | bytes 98312 | tf_op jit(solution)/shard_map/ppermute | solution.py:36
  17.8 3.1 %shard_map.75 = (f32[8,16,1024]{2,1,0:T(8,128)S(1)}, f32[4,16,128]{2,1,0:T(8,128)S(1)}) custom-call(bf16[8,16,1024]{2,1,0:T(8,128)(2,1)S(1)} %get-tuple-element.22.t.tgt, bf16[72,16,1024]{2,1,0:T(8,128)(2,1)S(1)} %get-tuple-element.23.v.v_, bf16[72,16,1024]{2,1,0:T(8,128)(2,1)S(1)} %get-tuple-element.24.f.f_, ...), custom_call_target="tpu_custom_call", output_to_operand_aliasing={{0}: (5, {})} | custom-call | flops 3000000000 | bytes 1000000 | tf_op jit(solution)/shard_map/pallas_call | solution.py:215
  20.9 1.8 %collective-permute-done.1.refs_0_ = bf16[2,19,16,512]{3,2,1,0:T(8,128)(2,1)S(1)} collective-permute-done((bf16[2,19,16,512]{3,2,1,0:T(8,128)(2,1)S(1)}, bf16[2,19,16,512]{3,2,1,0:T(8,128)(2,1)S(1)}, u32[]{:S(2)}, u32[]{:S(2)}) %collective-permute-start.1) | collective-permute-done | bytes 622624 | tf_op jit(solution)/shard_map/ppermute | solution.py:36
  22.8 0.1 collective-permute-start.7
  22.9 3.1 %shard_map.77 = (f32[8,16,1024]{2,1,0:T(8,128)S(1)}, f32[8,16,128]{2,1,0:T(8,128)S(1)}) custom-call(bf16[8,16,1024]{2,1,0:T(8,128)(2,1)S(1)} %get-tuple-element.22.t.tgt, bf16[72,16,1024]{2,1,0:T(8,128)(2,1)S(1)} %get-tuple-element.23.v.v_, bf16[72,16,1024]{2,1,0:T(8,128)(2,1)S(1)} %get-tuple-element.24.f.f_, ...), custom_call_target="tpu_custom_call", output_to_operand_aliasing={{0}: (5, {})} | custom-call | flops 3000000000 | bytes 1000000 | tf_op jit(solution)/shard_map/pallas_call | solution.py:215
  26.0 0.1 collective-permute-start.9
  26.1 2.1 %collective-permute-start.4 = (bf16[2,19,16,512]{3,2,1,0:T(8,128)(2,1)S(1)}, bf16[2,19,16,512]{3,2,1,0:T(8,128)(2,1)S(1)}, u32[]{:S(2)}, u32[]{:S(2)}) collective-permute-start(bf16[2,19,16,512]{3,2,1,0:T(8,128)(2,1)S(1)} %shard_map.76.near1), channel_id=1, source_target_pairs={{3,1},{0,2},{5,3},{2,4},{7,5},{4,6},{9,7},{6,8},{11,9},{8,10},{13,... | collective-permute-start | bytes 1867784 | tf_op jit(solution)/shard_map/ppermute | solution.py:36
  28.3 0.0 copy-start.12
  28.3 0.0 copy-start.3
  28.3 0.0 copy-start.4
  28.3 12.8 %shard_map.78 = (f32[8,16,1024]{2,1,0:T(8,128)S(1)}, bf16[72,16,1024]{2,1,0:T(8,128)(2,1)S(1)}, bf16[72,16,1024]{2,1,0:T(8,128)(2,1)S(1)}, f32[16,16,128]{2,1,0:T(8,128)S(1)}) custom-call(s32[2]{0:T(128)S(1)} %pad_add_fusion.place, s32[8,5]{1,0:T(8,128)S(1)} %fusion.2.work, ...), custom_call_target="tpu_custom_call", output_to_operand_aliasing={{0}: (7, {}), {1}: (8, {}), {2}: (9, {})} | custom-call | flops 11000000512 | bytes 1000000 | tf_op jit(solution)/shard_map/pallas_call | solution.py:215
  41.2 1.4 %copy-done.5 = bf16[72,16,1024]{2,1,0:T(8,128)(2,1)} copy-done((bf16[72,16,1024]{2,1,0:T(8,128)(2,1)}, bf16[72,16,1024]{2,1,0:T(8,128)(2,1)S(1)}, u32[]{:S(2)}) %copy-start.5) | copy-done | bytes 2359320
  42.6 1.4 %copy-done.7 = bf16[72,16,1024]{2,1,0:T(8,128)(2,1)} copy-done((bf16[72,16,1024]{2,1,0:T(8,128)(2,1)}, bf16[72,16,1024]{2,1,0:T(8,128)(2,1)S(1)}, u32[]{:S(2)}) %copy-start.7) | copy-done | bytes 2359320
  44.1 8.5 %collective-permute-start.8 = (bf16[1,19,16,512]{3,2,1,0:T(8,128)(2,1)S(1)}, bf16[1,19,16,512]{3,2,1,0:T(8,128)(2,1)S(1)}, u32[]{:S(2)}, u32[]{:S(2)}) collective-permute-start(bf16[1,19,16,512]{3,2,1,0:T(8,128)(2,1)S(1)} %shard_map.79), channel_id=1, source_target_pairs={{1,0},{0,1},{3,2},{2,3},{5,4},{4,5},{7,6},{6,7},{9,8},{8,9},{11,10... | collective-permute-start | bytes 933896 | tf_op jit(solution)/shard_map/ppermute | solution.py:36
  52.5 0.1 copy.19
  52.6 1.7 %copy-done.6 = bf16[72,16,1024]{2,1,0:T(8,128)(2,1)S(1)} copy-done((bf16[72,16,1024]{2,1,0:T(8,128)(2,1)S(1)}, bf16[72,16,1024]{2,1,0:T(8,128)(2,1)}, u32[]{:S(2)}) %copy-start.6) | copy-done | bytes 2359320
  54.3 1.7 %copy-done.8 = bf16[72,16,1024]{2,1,0:T(8,128)(2,1)S(1)} copy-done((bf16[72,16,1024]{2,1,0:T(8,128)(2,1)S(1)}, bf16[72,16,1024]{2,1,0:T(8,128)(2,1)}, u32[]{:S(2)}) %copy-start.8) | copy-done | bytes 2359320
  56.0 3.6 %shard_map.80 = (bf16[72,16,1024]{2,1,0:T(8,128)(2,1)S(1)}, bf16[72,16,1024]{2,1,0:T(8,128)(2,1)S(1)}, bf16[16,128]{1,0:T(8,128)(2,1)S(1)}) custom-call(s32[2]{0:T(128)S(1)} %pad_add_fusion.place, s32[4,3]{1,0:T(4,128)S(1)} %bitcast.12, bf16[2,19,16,512]{3,2,1,0:T(8,128)(2,1)S(1)} %collective-permute-done.4.array.far1, ...), custom_call_target="tpu_custom_call", output_to_operand_aliasing={{0}: (7, {}), {1}: (8, {})} | custom-call | flops 3000000000 | bytes 1000000 | tf_op jit(solution)/shard_map/pallas_call | solution.py:215
  59.6 0.0 copy-done.10
  59.6 24.1 %shard_map.81 = (f32[8,16,1024]{2,1,0:T(8,128)S(1)}, bf16[72,16,1024]{2,1,0:T(8,128)(2,1)S(1)}, bf16[72,16,1024]{2,1,0:T(8,128)(2,1)S(1)}, bf16[16,8192]{1,0:T(8,128)(2,1)}) custom-call(s32[2]{0:T(128)S(1)} %pad_add_fusion.place, s32[8,5]{1,0:T(8,128)S(1)} %fusion.2.work, ...), custom_call_target="tpu_custom_call", output_to_operand_aliasing={{0}: (6, {}), {1}: (7, {}), {2}: (8, {})} | custom-call | flops 20999999488 | bytes 1000000 | tf_op jit(solution)/shard_map/pallas_call | solution.py:215
  (32 shorter events, 0.1 us)
Async XLA Ops:
  0.0 0.9 %copy-start.1 = (bf16[16,8192]{1,0:T(8,128)(2,1)S(1)}, bf16[16,8192]{1,0:T(8,128)(2,1)}, u32[]{:S(2)}) copy-start(bf16[16,8192]{1,0:T(8,128)(2,1)} %charges_hbm.1) | copy-start | bytes 786436
  1.0 0.8 %copy-start.2 = (bf16[3,8192]{1,0:T(4,128)(2,1)S(1)}, bf16[3,8192]{1,0:T(4,128)(2,1)}, u32[]{:S(2)}) copy-start(bf16[3,8192]{1,0:T(4,128)(2,1)} %points_hbm.1) | copy-start | bytes 147460
  1.9 3.0 %collective-permute-start = (bf16[19,16,512]{2,1,0:T(8,128)(2,1)S(1)}, bf16[19,16,512]{2,1,0:T(8,128)(2,1)S(1)}, u32[]{:S(2)}, u32[]{:S(2)}) collective-permute-start(bf16[19,16,512]{2,1,0:T(8,128)(2,1)S(1)} %shard_map.73), channel_id=1, source_target_pairs={{1,0},{0,1},{3,2},{2,3},{5,4},{4,5},{7,6},{6,7},{9,8},{8,9},{11,10... | collective-permute-start | bytes 933896 | tf_op jit(solution)/shard_map/ppermute | solution.py:36
  4.8 5.0 %collective-permute-start.2 = (f32[1,16,128]{2,1,0:T(8,128)S(1)}, f32[1,16,128]{2,1,0:T(8,128)S(1)}, u32[]{:S(2)}, u32[]{:S(2)}) collective-permute-start(f32[1,16,128]{2,1,0:T(8,128)S(1)} %convolution_bitcast_fusion.mine), channel_id=1, source_target_pairs={{1,0},{0,1},{3,2},{2,3},{5,4},{4,5},{7,6},{6,7},{9,8},{8,9},{11,10... | collective-permute-start | bytes 24584 | tf_op jit(solution)/shard_map/ppermute | solution.py:36
  5.0 17.7 %collective-permute-start.1 = (bf16[2,19,16,512]{3,2,1,0:T(8,128)(2,1)S(1)}, bf16[2,19,16,512]{3,2,1,0:T(8,128)(2,1)S(1)}, u32[]{:S(2)}, u32[]{:S(2)}) collective-permute-start(bf16[2,19,16,512]{3,2,1,0:T(8,128)(2,1)S(1)} %pad_maximum_fusion.pair), channel_id=1, source_target_pairs={{2,1},{1,2},{4,3},{3,4},{6,5},{5,6},{8,7},{7,8},{10,9},{9,10},{12,... | collective-permute-start | bytes 1867784 | tf_op jit(solution)/shard_map/ppermute | solution.py:36
  9.8 7.1 %collective-permute-start.3 = (f32[2,16,128]{2,1,0:T(8,128)S(1)}, f32[2,16,128]{2,1,0:T(8,128)S(1)}, u32[]{:S(2)}, u32[]{:S(2)}) collective-permute-start(f32[2,16,128]{2,1,0:T(8,128)S(1)} %pad_maximum_fusion.4), channel_id=1, source_target_pairs={{2,0},{3,1},{0,2},{1,3},{6,4},{7,5},{4,6},{5,7},{10,8},{11,9},{8,1... | collective-permute-start | bytes 49160 | tf_op jit(solution)/shard_map/ppermute | solution.py:36
  12.9 15.3 %copy-start.9 = (bf16[8,16,1024]{2,1,0:T(8,128)(2,1)}, bf16[8,16,1024]{2,1,0:T(8,128)(2,1)S(1)}, u32[]{:S(2)}) copy-start(bf16[8,16,1024]{2,1,0:T(8,128)(2,1)S(1)} %get-tuple-element.22.t.tgt) | copy-start | bytes 786436
  16.9 5.9 %collective-permute-start.6 = (f32[4,16,128]{2,1,0:T(8,128)S(1)}, f32[4,16,128]{2,1,0:T(8,128)S(1)}, u32[]{:S(2)}, u32[]{:S(2)}) collective-permute-start(f32[4,16,128]{2,1,0:T(8,128)S(1)} %pad_maximum_fusion.3), channel_id=1, source_target_pairs={{4,0},{5,1},{6,2},{7,3},{0,4},{1,5},{2,6},{3,7},{12,8},{13,9},{14,... | collective-permute-start | bytes 98312 | tf_op jit(solution)/shard_map/ppermute | solution.py:36
  17.8 4.9 %copy-start.11 = (s32[8,5]{1,0:T(8,128)S(1)}, s32[8,5]{1,0:T(8,128)}, u32[]{:S(2)}) copy-start(s32[8,5]{1,0:T(8,128)} %param.12) | copy-start | bytes 484
  22.7 5.6 %collective-permute-start.5 = (bf16[2,19,16,512]{3,2,1,0:T(8,128)(2,1)S(1)}, bf16[2,19,16,512]{3,2,1,0:T(8,128)(2,1)S(1)}, u32[]{:S(2)}, u32[]{:S(2)}) collective-permute-start(bf16[2,19,16,512]{3,2,1,0:T(8,128)(2,1)S(1)} %shard_map.76.near1), channel_id=1, source_target_pairs={{1,0},{0,1},{3,2},{2,3},{5,4},{4,5},{7,6},{6,7},{9,8},{8,9},{11,10... | collective-permute-start | bytes 1867784 | tf_op jit(solution)/shard_map/ppermute | solution.py:36
  22.8 3.2 %collective-permute-start.7 = (f32[8,16,128]{2,1,0:T(8,128)S(1)}, f32[8,16,128]{2,1,0:T(8,128)S(1)}, u32[]{:S(2)}, u32[]{:S(2)}) collective-permute-start(f32[8,16,128]{2,1,0:T(8,128)S(1)} %pad_maximum_fusion.2), channel_id=1, source_target_pairs={{8,0},{9,1},{10,2},{11,3},{12,4},{13,5},{14,6},{15,7},{0,8},{1,9},... | collective-permute-start | bytes 196616 | tf_op jit(solution)/shard_map/ppermute | solution.py:36
  26.0 26.6 %collective-permute-start.9 = (f32[16,16,128]{2,1,0:T(8,128)S(1)}, f32[16,16,128]{2,1,0:T(8,128)S(1)}, u32[]{:S(2)}, u32[]{:S(2)}) collective-permute-start(f32[16,16,128]{2,1,0:T(8,128)S(1)} %pad_maximum_fusion.1), channel_id=1, source_target_pairs={{16,0},{17,1},{18,2},{19,3},{20,4},{21,5},{22,6},{23,7},{24,8},{25... | collective-permute-start | bytes 393224 | tf_op jit(solution)/shard_map/ppermute | solution.py:36
  26.1 17.9 %collective-permute-start.4 = (bf16[2,19,16,512]{3,2,1,0:T(8,128)(2,1)S(1)}, bf16[2,19,16,512]{3,2,1,0:T(8,128)(2,1)S(1)}, u32[]{:S(2)}, u32[]{:S(2)}) collective-permute-start(bf16[2,19,16,512]{3,2,1,0:T(8,128)(2,1)S(1)} %shard_map.76.near1), channel_id=1, source_target_pairs={{3,1},{0,2},{5,3},{2,4},{7,5},{4,6},{9,7},{6,8},{11,9},{8,10},{13,... | collective-permute-start | bytes 1867784 | tf_op jit(solution)/shard_map/ppermute | solution.py:36
  28.3 24.2 %copy-start.12 = (s32[1,4,3]{1,0,2:T(1,128)S(1)}, s32[1,4,3]{1,0,2:T(1,128)}, u32[]{:S(2)}) copy-start(s32[1,4,3]{1,0,2:T(1,128)} %param.13) | copy-start | bytes 148
  28.3 24.3 %copy-start.3 = (f32[4,3,128,128]{3,2,1,0:T(8,128)S(1)}, f32[4,3,128,128]{3,2,1,0:T(8,128)}, u32[]{:S(2)}) copy-start(f32[4,3,128,128]{3,2,1,0:T(8,128)} %coupling.1) | copy-start | bytes 2359300
  28.3 24.3 %copy-start.4 = (f32[4,2,128,128]{3,2,1,0:T(8,128)S(1)}, f32[4,2,128,128]{3,2,1,0:T(8,128)}, u32[]{:S(2)}) copy-start(f32[4,2,128,128]{3,2,1,0:T(8,128)} %transfer.1) | copy-start | bytes 1572868
  41.1 1.4 %copy-start.5 = (bf16[72,16,1024]{2,1,0:T(8,128)(2,1)}, bf16[72,16,1024]{2,1,0:T(8,128)(2,1)S(1)}, u32[]{:S(2)}) copy-start(bf16[72,16,1024]{2,1,0:T(8,128)(2,1)S(1)} %get-tuple-element.32.v_) | copy-start | bytes 7077892
  42.6 1.4 %copy-start.7 = (bf16[72,16,1024]{2,1,0:T(8,128)(2,1)}, bf16[72,16,1024]{2,1,0:T(8,128)(2,1)S(1)}, u32[]{:S(2)}) copy-start(bf16[72,16,1024]{2,1,0:T(8,128)(2,1)S(1)} %get-tuple-element.33.f_) | copy-start | bytes 7077892
  44.1 15.5 %collective-permute-start.8 = (bf16[1,19,16,512]{3,2,1,0:T(8,128)(2,1)S(1)}, bf16[1,19,16,512]{3,2,1,0:T(8,128)(2,1)S(1)}, u32[]{:S(2)}, u32[]{:S(2)}) collective-permute-start(bf16[1,19,16,512]{3,2,1,0:T(8,128)(2,1)S(1)} %shard_map.79), channel_id=1, source_target_pairs={{1,0},{0,1},{3,2},{2,3},{5,4},{4,5},{7,6},{6,7},{9,8},{8,9},{11,10... | collective-permute-start | bytes 933896 | tf_op jit(solution)/shard_map/ppermute | solution.py:36
  52.6 1.7 %copy-start.6 = (bf16[72,16,1024]{2,1,0:T(8,128)(2,1)S(1)}, bf16[72,16,1024]{2,1,0:T(8,128)(2,1)}, u32[]{:S(2)}) copy-start(bf16[72,16,1024]{2,1,0:T(8,128)(2,1)} %copy-done.5) | copy-start | bytes 7077892
  54.3 1.7 %copy-start.8 = (bf16[72,16,1024]{2,1,0:T(8,128)(2,1)S(1)}, bf16[72,16,1024]{2,1,0:T(8,128)(2,1)}, u32[]{:S(2)}) copy-start(bf16[72,16,1024]{2,1,0:T(8,128)(2,1)} %copy-done.7) | copy-start | bytes 7077892
  56.0 3.6 %copy-start = (bf16[8,1024,128]{2,1,0:T(8,128)(2,1)S(1)}, bf16[8,1024,128]{2,1,0:T(8,128)(2,1)}, u32[]{:S(2)}) copy-start(bf16[8,1024,128]{2,1,0:T(8,128)(2,1)} %basis.1) | copy-start | bytes 6291460
  56.0 3.7 %copy-start.10 = (bf16[8,16,1024]{2,1,0:T(8,128)(2,1)S(1)}, bf16[8,16,1024]{2,1,0:T(8,128)(2,1)}, u32[]{:S(2)}) copy-start(bf16[8,16,1024]{2,1,0:T(8,128)(2,1)} %copy-done.9) | copy-start | bytes 786436

commit v4 on v3

--- a/solution.py
+++ b/solution.py
@@ -22,7 +22,8 @@
 VM = pl.BlockSpec(memory_space=pltpu.VMEM)
 SM = pl.BlockSpec(memory_space=pltpu.SMEM)
 SLOT_OFFSETS = (0, 1, -1, -2, 2, 3, -3, -4, 4)
-SELF = (2, 5, 8)
+SELF = (1, 2, 8)
+BITS = (0, 3, 4, 1, 2)
 BUDGET = 11
 
 
@@ -61,7 +62,7 @@
     return pl.pallas_call(
         pack_kernel,
         out_shape=jax.ShapeDtypeStruct(PAYLOAD, bf16),
-        in_specs=[anywhere, anywhere],
+        in_specs=[anywhere] * 2,
         out_specs=VM,
         scratch_shapes=[
             pltpu.VMEM(charges.shape, bf16),
@@ -69,7 +70,7 @@
             pltpu.VMEM((48, HALF), f32),
             pltpu.SemaphoreType.DMA((2,)),
         ],
-        compiler_params=params(4),
+        compiler_params=params(60),
         cost_estimate=pl.CostEstimate(flops=10**6, bytes_accessed=10**6, transcendentals=0),
     )(charges, points)
 
@@ -93,25 +94,29 @@
 
 
 def store_features(dst, base, rows, tmp):
-    for f, row in enumerate(rows):
+    for f, row in rows:
         tmp[:, f, :] = row
-    for f in range(len(rows), FEATS):
-        tmp[:, f, :] = jnp.zeros((LEAVES_DEV, LEAF), f32)
     for l in range(LEAVES_DEV):
         dst[base + l] = tmp[l].astype(bf16)
 
 
+def constant_rows(tmp, ones):
+    for f in range(FEATS):
+        if f in ones:
+            tmp[:, f, :] = jnp.ones((LEAVES_DEV, LEAF), f32)
+        elif f >= 12:
+            tmp[:, f, :] = jnp.zeros((LEAVES_DEV, LEAF), f32)
+
+
 def source_features(block, first_leaf, dst, base, tmp):
     x, a, y, z, high, middle, low = squared_norm_parts(block, first_leaf, 0.0)
-    one = jnp.ones_like(x)
-    store_features(dst, base, [x, x, a, a, y, z, high, middle, low, one, one, one], tmp)
+    store_features(dst, base, list(enumerate([x, x, a, a, y, z, high, middle, low])), tmp)
 
 
 def target_features(block, dst, tmp):
     x, a, y, z, high, middle, low = squared_norm_parts(block, 0, smoothing_sq)
-    one = jnp.ones_like(x)
-    rows = [-2 * x, -2 * a, -2 * x, -2 * a, -2 * y, -2 * z, one, one, one, high, middle, low]
-    store_features(dst, 0, rows, tmp)
+    rows = list(enumerate([-2 * x, -2 * a, -2 * x, -2 * a, -2 * y, -2 * z]))
+    store_features(dst, 0, rows + [(9, high), (10, middle), (11, low)], tmp)
 
 
 def load_cluster(block, slot, sign, vals, feats, tmp):
@@ -145,77 +150,103 @@
     lax.fori_loop(0, LEAVES_DEV * (NB - 1), item, jnp.int32(0))
 
 
+def own_blocks(first, last, tgt, vals, feats, acc):
+    def one(i, carry):
+        add_block(i, i, tgt, vals, feats, acc)
+        return carry
+
+    lax.fori_loop(first, last, one, 0)
+
+
 def join(mine, theirs, joined):
     n = mine.shape[0]
     joined[:n] = mine[...]
     joined[n:] = theirs[...]
 
 
-def first_kernel(place, pair, mine, theirs, acc, tgt, vals, feats, joined, tmp):
+def first_kernel(place, own, mine, theirs, acc, tgt, vals, feats, joined, tmp):
     join(mine, theirs, joined)
     acc[...] = jnp.zeros_like(acc)
-    target_features(pair.at[0], tgt, tmp)
-    for slot in range(2):
-        load_cluster(pair.at[slot], slot, place[1], vals, feats, tmp)
+    constant_rows(tmp, (6, 7, 8))
+    target_features(own, tgt, tmp)
+    constant_rows(tmp, (9, 10, 11))
+    load_cluster(own, 0, place[1], vals, feats, tmp)
     own_blocks(0, SELF[0], tgt, vals, feats, acc)
 
 
-def own_blocks(first, last, tgt, vals, feats, acc):
-    def one(i, carry):
-        add_block(i, i, tgt, vals, feats, acc)
-        return carry
-
-    lax.fori_loop(first, last, one, 0)
-
-
-def own_kernel(step, acc_in, tgt, vals, feats, mine, theirs, acc, joined):
+def own_kernel(step, tgt, vals, feats, mine, theirs, acc_in, acc, joined):
     join(mine, theirs, joined)
     own_blocks(SELF[step - 1], SELF[step], tgt, vals, feats, acc)
 
 
-def near_kernel(place, work, near1, near2, tgt, mine, theirs, a_, v_, f_, acc, vals, feats, joined, tmp):
+def load_clusters(pieces, sign, vals, feats, tmp):
+    constant_rows(tmp, (9, 10, 11))
+    slot = 0
+    for piece in pieces:
+        for part in range(piece.shape[0]):
+            load_cluster(piece.at[part], slot, sign, vals, feats, tmp)
+            slot += 1
+
+
+def near_kernel(
+    place, work, pair, near1, near2, mine, theirs, acc_in, acc, joined, vals, feats, tmp, tgt
+):
     join(mine, theirs, joined)
-    for slot in range(2, 6):
-        piece = near1 if slot < 4 else near2
-        load_cluster(piece.at[slot % 2], slot, place[1], vals, feats, tmp)
+    constant_rows(tmp, (6, 7, 8))
+    target_features(pair.at[0], tgt, tmp)
+    load_clusters([pair, near1, near2], place[1], vals, feats, tmp)
     add_listed(1, work, tgt, vals, feats, acc)
 
 
-def tree_kernel(
-    place, flags, far1, mine, theirs, transfer, coupling, v_, f_, vals, feats, down, tmp
-):
-    for slot in range(6, 8):
-        load_cluster(far1.at[slot - 6], slot, place[1], vals, feats, tmp)
-    n = mine.shape[0]
-    coefs = [mine[m] for m in range(n)] + [theirs[m] for m in range(n)]
-    down[...] = tree(place[0], flags, coefs, transfer, coupling)
-
-
-def last_kernel(place, work, far2, tgt, down, basis, a_, v_, f_, acc, vals, feats, out, tmp):
-    load_cluster(far2.at[0], 8, place[1], vals, feats, tmp)
+def last_kernel(place, work, pair, near1, near2, far1, far2, acc_in, acc, vals, feats, tmp, tgt):
+    constant_rows(tmp, (6, 7, 8))
+    target_features(pair.at[0], tgt, tmp)
+    load_clusters([pair, near1, near2, far1, far2], place[1], vals, feats, tmp)
     add_listed(2, work, tgt, vals, feats, acc)
+
+
+def tree_kernel(place, flags, acc, *refs):
+    groups, (transfer, coupling, basis, out) = refs[:2], refs[2:]
+    coefs = []
+    for m in range(32):
+        where = sum(((m >> bit) & 1) << at for at, bit in enumerate(BITS))
+        coefs.append(groups[where // 16][where % 16])
+    down = tree(place[0], flags, coefs, transfer, coupling)
     scale = 1.0 / math.sqrt(NB * LEAF)
     for l in range(LEAVES_DEV):
         far = lax.dot_general(
-            down[...], basis[l], (((1,), (1,)), ((), ())), preferred_element_type=f32
+            down, basis[l], (((1,), (1,)), ((), ())), preferred_element_type=f32
         )
         out[:, l * LEAF : (l + 1) * LEAF] = (acc[l] * scale + far).astype(bf16)
 
 
 ACC = jax.ShapeDtypeStruct((LEAVES_DEV, RHS, LEAF), f32)
+TMP = pltpu.VMEM((LEAVES_DEV, FEATS, LEAF), f32)
+
+
+def window_scratch(slots):
+    return (
+        pltpu.VMEM((slots * LEAVES_DEV, RHS, LEAF), bf16),
+        pltpu.VMEM((slots * LEAVES_DEV, FEATS, LEAF), bf16),
+        TMP,
+        pltpu.VMEM((LEAVES_DEV, FEATS, LEAF), bf16),
+    )
+
+
 TGT = jax.ShapeDtypeStruct((LEAVES_DEV, FEATS, LEAF), bf16)
-VALS = jax.ShapeDtypeStruct((9 * LEAVES_DEV, RHS, LEAF), bf16)
-FEAT = jax.ShapeDtypeStruct((9 * LEAVES_DEV, FEATS, LEAF), bf16)
-TMP = pltpu.VMEM((LEAVES_DEV, FEATS, LEAF), f32)
-
-
-def staged(kernel, smem, inputs, state, outs, blocks, scratch=(TMP,)):
+VALS = jax.ShapeDtypeStruct((LEAVES_DEV, RHS, LEAF), bf16)
+
+
+def staged(kernel, smem, inputs, state, outs, blocks, scratch=(), unplaced=0):
     ins = len(smem) + len(inputs)
     state_shapes = [jax.ShapeDtypeStruct(s.shape, s.dtype) for s in state]
     return pl.pallas_call(
         kernel,
         out_shape=tuple(state_shapes) + tuple(outs),
-        in_specs=[SM] * len(smem) + [VM] * (len(inputs) + len(state)),
+        in_specs=[SM] * len(smem)
+        + [VM] * (len(inputs) - unplaced)
+        + [pl.BlockSpec(memory_space=pl.ANY)] * unplaced
+        + [VM] * len(state),
         out_specs=(VM,) * (len(state) + len(outs)),
         scratch_shapes=list(scratch),
         input_output_aliases={ins + n: n for n in range(len(state))},
@@ -234,18 +265,18 @@
     cur = coefs
     coupled = []
     for t in range(levels):
-        total = jnp.zeros((RHS, RANK), f32)
-        for m in range(3):
-            flag = flags[t, m].astype(f32)
-            total = total + flag * dot(cur[m + 1], coupling[t, m])
-        coupled.append(total)
+        chosen = [flags[t, m].astype(f32) * cur[m + 1] for m in range(3)]
+        coupled.append(
+            dot(jnp.concatenate(chosen, axis=1), coupling[t].reshape(3 * RANK, RANK))
+        )
         if t + 1 < levels:
             right = ((me >> t) & 1) == 1
             even = jnp.concatenate(cur[0::2], axis=0)
             odd = jnp.concatenate(cur[1::2], axis=0)
-            merged = dot(jnp.where(right, odd, even), transfer[t, 0]) + dot(
-                jnp.where(right, even, odd), transfer[t, 1]
+            both = jnp.concatenate(
+                [jnp.where(right, odd, even), jnp.where(right, even, odd)], axis=1
             )
+            merged = dot(both, transfer[t].reshape(2 * RANK, RANK))
             cur = [merged[m * RHS : (m + 1) * RHS] for m in range(len(cur) // 2)]
     local = coupled[-1]
     for t in range(levels - 1, 0, -1):
@@ -273,37 +304,37 @@
     pass
 
 
-def gate(array, after):
+def gate(array, *after):
     return pl.pallas_call(
         gate_kernel,
         out_shape=jax.ShapeDtypeStruct(array.shape, array.dtype),
-        in_specs=[VM, VM],
+        in_specs=[VM] * (1 + len(after)),
         out_specs=VM,
         input_output_aliases={0: 0},
         compiler_params=params(2),
-    )(array, after)
-
-
-def gate_copy_kernel(array, after, out):
-    out[0] = array[0]
-
-
-def gate_first(array, after):
+    )(array, *after)
+
+
+def gate_copy_kernel(array, *refs):
+    refs[-1][0] = array[0]
+
+
+def gate_first(array, *after):
     return pl.pallas_call(
         gate_copy_kernel,
         out_shape=jax.ShapeDtypeStruct((1,) + array.shape[1:], array.dtype),
-        in_specs=[VM, VM],
+        in_specs=[VM] * (1 + len(after)),
         out_specs=VM,
         compiler_params=params(2),
-    )(array, after)
+    )(array, *after)
+
+
+def partner(coefs, step):
+    return permuted(coefs, lambda i: i ^ (1 << BITS[step]))
 
 
 def joined_shape(n):
     return jax.ShapeDtypeStruct((n, RHS, RANK), f32)
-
-
-def partner(coefs, step):
-    return permuted(coefs, lambda i: i ^ (1 << step))
 
 
 def local(charges, points, leaf_basis, transfer, coupling, near_list, couple_flags):
@@ -315,8 +346,6 @@
     own = pack(charges, points)
     sib = permuted(own, lambda i: i ^ 1)
     pair = jnp.stack([own, sib])
-    near1 = permuted(pair, lambda i: i - 1 if i % 2 == 0 else i + 1)
-
     coefs = jnp.dot(
         charges,
         leaf_basis.reshape(LEAVES_DEV * LEAF, RANK),
@@ -325,54 +354,59 @@
     recv = partner(coefs, 0)
     following = partner(jnp.concatenate([coefs, recv]), 1)
     acc, tgt, vals, feats, coefs = staged(
-        first_kernel, [place], [pair, coefs, recv], [], [ACC, TGT, VALS, FEAT, joined_shape(2)], 2
+        first_kernel,
+        [place],
+        [own, coefs, recv],
+        [],
+        [ACC, TGT, VALS, TGT, joined_shape(2)],
+        2,
+        (TMP,),
     )
-    for step in range(1, 3):
+    for step in (1, 2):
         recv = following
         following = partner(jnp.concatenate([coefs, recv]), step + 1)
-
-        def own_step(t, v, f, c, r, a, acc, joined, step=step):
-            own_kernel(step, a, t, v, f, c, r, acc, joined)
-
+        if step == 2:
+            pair = gate(pair, recv)
+            near1 = permuted(pair, lambda i: i - 1 if i % 2 == 0 else i + 1)
         acc, coefs = staged(
-            own_step,
+            functools.partial(own_kernel, step),
             [],
             [tgt, vals, feats, coefs, recv],
             [acc],
             [joined_shape(2 ** (step + 1))],
-            3,
-            (),
+            SELF[step] - SELF[step - 1],
         )
-        if step == 1:
-            near1 = gate(near1, coefs)
-            near2 = permuted(near1, lambda i: i ^ 1)
-            far1 = permuted(near1, lambda i: i - 2 if i % 2 == 0 else i + 2)
     recv = following
+    near1 = gate(near1, acc, recv)
+    near2 = permuted(near1, lambda i: i ^ 1)
+    far1 = permuted(near1, lambda i: i - 2 if i % 2 == 0 else i + 2)
     following = partner(jnp.concatenate([coefs, recv]), 4)
-    acc, vals, feats, coefs = staged(
+    acc, coefs = staged(
         near_kernel,
         [place, work],
-        [near1, near2, tgt, coefs, recv],
-        [acc, vals, feats],
+        [pair, near1, near2, coefs, recv],
+        [acc],
         [joined_shape(16)],
         BUDGET,
+        window_scratch(6),
     )
-    far2 = permuted(gate_first(far1, coefs), lambda i: i ^ 1)
-    vals, feats, down = staged(
+    far2 = permuted(gate_first(far1, acc, following), lambda i: i ^ 1)
+    (acc,) = staged(
+        last_kernel,
+        [place, work],
+        [pair, near1, near2, far1, far2],
+        [acc],
+        [],
+        21,
+        window_scratch(9),
+    )
+    return staged(
         tree_kernel,
         [place, couple_flags[0]],
-        [far1, coefs, following, transfer, coupling],
-        [vals, feats],
-        [jax.ShapeDtypeStruct((RHS, RANK), bf16)],
+        [acc, coefs, following, transfer, coupling, leaf_basis],
+        [],
+        [jax.ShapeDtypeStruct((RHS, LEAVES_DEV * LEAF), bf16)],
         3,
-    )
-    return staged(
-        last_kernel,
-        [place, work],
-        [far2, tgt, down, leaf_basis],
-        [acc, vals, feats],
-        [jax.ShapeDtypeStruct((RHS, LEAVES_DEV * LEAF), bf16)],
-        21,
     )[-1]
 
 

time: 84 us -> 81.1 us (0.965)
  local copies, waits for them, and re-layouts: 8.12 us -> 1.74 us
  Pallas kernels: 50 us -> 52.5 us
  waiting for transfers between devices: 5.7 us -> 8.08 us
  starting transfers between devices: 17.4 us -> 16.1 us
    unnamed x27 -> x19, local copies, waits for them, and re-layouts: 8.12 us -> 1.74 us
    ppermute x10, waiting for transfers between devices: 5.7 us -> 8.08 us  [permuted(): return lax.ppermute(array, 'leaf', route)]
    pallas_call x1, Pallas kernels: 0.14 us -> 1.74 us  [pack(): pl.pallas_call(pack_kernel, out_shape=jax.ShapeDtypeStruct(PAYLOAD, bf16)...]
    ppermute x10, starting transfers between devices: 17.4 us -> 16.1 us  [permuted(): return lax.ppermute(array, 'leaf', route)]
    pallas_call x6, Pallas kernels: 49.9 us -> 50.8 us  [staged(): pl.pallas_call(kernel, out_shape=tuple(state_shapes) + tuple(outs), in_sp...]
  transfers between devices with their start and end apart: 10 -> 10, of which waited for: 2 -> 5; matrix products, arithmetic and copies ran while one was open for 3% -> 0% of each run, Pallas kernels for 31% -> 30%
where the time goes in v4:
time: 81.1 us; the launch traced here: 80.9 us
  Pallas kernels  52.5 us (65%)
  starting transfers between devices  16.1 us (20%)
  waiting for transfers between devices  8.08 us (10%)
  matrix products  2.07 us (3%)
  local copies, waits for them, and re-layouts  1.74 us (2%)
    pallas_call x6, Pallas kernels, staged(): pl.pallas_call(kernel, out_shape=tuple(state_shapes) + tuple(outs), in_sp...  50.8 us
    ppermute x10, starting transfers between devices, permuted(): return lax.ppermute(array, 'leaf', route)  16.1 us
    ppermute x10, waiting for transfers between devices, permuted(): return lax.ppermute(array, 'leaf', route)  8.08 us
    dot_general x1, matrix products, local(): jnp.dot(charges, leaf_basis.reshape(LEAVES_DEV * LEAF, RANK), preferred_e...  2.07 us
    pallas_call x1, Pallas kernels, pack(): pl.pallas_call(pack_kernel, out_shape=jax.ShapeDtypeStruct(PAYLOAD, bf16)...  1.74 us
    unnamed x19, local copies, waits for them, and re-layouts  1.74 us
  transfers between devices with their start and end apart: 10, of which 5 were waited for; matrix products, arithmetic and copies ran while one was open for 0% of the time, Pallas kernels for 30%

profile of v4, /device:TPU:127, one launch (start us, length us, event | category | flops | bytes accessed | tf_op | source)
XLA Modules:
  0.0 80.9 jit_solution(7853889564437409399)
XLA Ops:
  0.0 2.1 %convolution_bitcast_fusion.mine = f32[1,16,128]{2,1,0:T(8,128)S(1)} fusion(bf16[16,8192]{1,0:T(8,128)(2,1)} %charges_hbm.1, bf16[8192,128]{1,0:T(8,128)(2,1)} %bitcast.10), kind=kOutput, calls=%fused_computation | convolution fusion | flops 33554432 | bytes 2367488 | tf_op jit(solution)/shard_map/dot_general | solution.py:349
  2.1 0.8 collective-permute-start.1
  2.8 1.7 %shard_map.73.own = bf16[19,16,512]{2,1,0:T(8,128)(2,1)} custom-call(bf16[16,8192]{1,0:T(8,128)(2,1)} %charges_hbm.1, bf16[3,8192]{1,0:T(4,128)(2,1)} %points_hbm.1), custom_call_target="tpu_custom_call" | custom-call | flops 1000000 | bytes 1000000 | tf_op jit(solution)/shard_map/pallas_call | solution.py:62
  4.6 0.1 collective-permute-start
  4.7 0.1 pad_add_fusion.place
  4.8 0.0 collective-permute-done.1.theirs
  4.8 0.6 collective-permute-start.2
  5.4 1.0 %copy-done.1 = bf16[19,16,512]{2,1,0:T(8,128)(2,1)S(1)} copy-done((bf16[19,16,512]{2,1,0:T(8,128)(2,1)S(1)}, bf16[19,16,512]{2,1,0:T(8,128)(2,1)}, u32[]{:S(2)}) %copy-start.1) | copy-done | bytes 311320
  6.3 1.9 %shard_map.74 = (f32[8,16,1024]{2,1,0:T(8,128)S(1)}, bf16[8,16,1024]{2,1,0:T(8,128)(2,1)S(1)}, bf16[8,16,1024]{2,1,0:T(8,128)(2,1)S(1)}, bf16[8,16,1024]{2,1,0:T(8,128)(2,1)S(1)}, f32[2,16,128]{2,1,0:T(8,128)S(1)}) custom-call(s32[2]{0:T(128)S(1)} %pad_add_fusion.place, bf16[19,16,512]{2,1,0:T(8,128)(2,1)S(1)} %copy-done.1, ...), custom_call_target="tpu_custom_call" | custom-call | flops 2000000000 | bytes 1000000 | tf_op jit(solution)/shard_map/pallas_call | solution.py:243
  8.2 0.9 %collective-permute-start.3 = (f32[4,16,128]{2,1,0:T(8,128)S(1)}, f32[4,16,128]{2,1,0:T(8,128)S(1)}, u32[]{:S(2)}, u32[]{:S(2)}) collective-permute-start(f32[4,16,128]{2,1,0:T(8,128)S(1)} %pad_maximum_fusion.3), channel_id=1, source_target_pairs={{16,0},{17,1},{18,2},{19,3},{20,4},{21,5},{22,6},{23,7},{24,8},{25... | collective-permute-start | bytes 98312 | tf_op jit(solution)/shard_map/ppermute | solution.py:37
  9.1 1.0 %shard_map.76 = (f32[8,16,1024]{2,1,0:T(8,128)S(1)}, f32[4,16,128]{2,1,0:T(8,128)S(1)}) custom-call(bf16[8,16,1024]{2,1,0:T(8,128)(2,1)S(1)} %get-tuple-element.17.tgt, bf16[8,16,1024]{2,1,0:T(8,128)(2,1)S(1)} %get-tuple-element.18.vals, bf16[8,16,1024]{2,1,0:T(8,128)(2,1)S(1)} %get-tuple-element.19.feats, ...), custom_call_target="tpu_custom_call", output_to_operand_aliasing={{0}: (5, {})} | custom-call | flops 1000000000 | bytes 1000000 | tf_op jit(solution)/shard_map/pallas_call | solution.py:243
  10.2 0.0 collective-permute-done
  10.2 0.1 pad_maximum_fusion.refs_0_
  10.3 2.3 %collective-permute-done.3.refs_1_.theirs = f32[4,16,128]{2,1,0:T(8,128)S(1)} collective-permute-done((f32[4,16,128]{2,1,0:T(8,128)S(1)}, f32[4,16,128]{2,1,0:T(8,128)S(1)}, u32[]{:S(2)}, u32[]{:S(2)}) %collective-permute-start.3) | collective-permute-done | bytes 32800 | tf_op jit(solution)/shard_map/ppermute | solution.py:37
  12.6 6.8 %collective-permute-start.4 = (bf16[2,19,16,512]{3,2,1,0:T(8,128)(2,1)S(1)}, bf16[2,19,16,512]{3,2,1,0:T(8,128)(2,1)S(1)}, u32[]{:S(2)}, u32[]{:S(2)}) collective-permute-start(bf16[2,19,16,512]{3,2,1,0:T(8,128)(2,1)S(1)} %shard_map.75.pair), channel_id=1, source_target_pairs={{2,1},{1,2},{4,3},{3,4},{6,5},{5,6},{8,7},{7,8},{10,9},{9,10},{12,... | collective-permute-start | bytes 1867784 | tf_op jit(solution)/shard_map/ppermute | solution.py:37
  19.4 0.1 collective-permute-start.5
  19.5 0.0 copy-start.7
  19.5 6.3 %shard_map.77 = (f32[8,16,1024]{2,1,0:T(8,128)S(1)}, f32[8,16,128]{2,1,0:T(8,128)S(1)}) custom-call(bf16[8,16,1024]{2,1,0:T(8,128)(2,1)S(1)} %get-tuple-element.17.tgt, bf16[8,16,1024]{2,1,0:T(8,128)(2,1)S(1)} %get-tuple-element.18.vals, bf16[8,16,1024]{2,1,0:T(8,128)(2,1)S(1)} %get-tuple-element.19.feats, ...), custom_call_target="tpu_custom_call", output_to_operand_aliasing={{0}: (5, {})} | custom-call | flops 6000000000 | bytes 1000000 | tf_op jit(solution)/shard_map/pallas_call | solution.py:243
  25.7 1.0 %collective-permute-done.5.refs_2_.theirs = f32[8,16,128]{2,1,0:T(8,128)S(1)} collective-permute-done((f32[8,16,128]{2,1,0:T(8,128)S(1)}, f32[8,16,128]{2,1,0:T(8,128)S(1)}, u32[]{:S(2)}, u32[]{:S(2)}) %collective-permute-start.5) | collective-permute-done | bytes 65568 | tf_op jit(solution)/shard_map/ppermute | solution.py:37
  26.7 2.8 %collective-permute-done.4.refs_0_ = bf16[2,19,16,512]{3,2,1,0:T(8,128)(2,1)S(1)} collective-permute-done((bf16[2,19,16,512]{3,2,1,0:T(8,128)(2,1)S(1)}, bf16[2,19,16,512]{3,2,1,0:T(8,128)(2,1)S(1)}, u32[]{:S(2)}, u32[]{:S(2)}) %collective-permute-start.4) | collective-permute-done | bytes 622624 | tf_op jit(solution)/shard_map/ppermute | solution.py:37
  29.6 0.0 copy-start.8
  29.6 0.1 collective-permute-start.8
  29.7 1.9 %collective-permute-start.7 = (bf16[2,19,16,512]{3,2,1,0:T(8,128)(2,1)S(1)}, bf16[2,19,16,512]{3,2,1,0:T(8,128)(2,1)S(1)}, u32[]{:S(2)}, u32[]{:S(2)}) collective-permute-start(bf16[2,19,16,512]{3,2,1,0:T(8,128)(2,1)S(1)} %shard_map.78.near1), channel_id=1, source_target_pairs={{3,1},{0,2},{5,3},{2,4},{7,5},{4,6},{9,7},{6,8},{11,9},{8,10},{13,... | collective-permute-start | bytes 1867784 | tf_op jit(solution)/shard_map/ppermute | solution.py:37
  31.6 13.1 %shard_map.79 = (f32[8,16,1024]{2,1,0:T(8,128)S(1)}, f32[16,16,128]{2,1,0:T(8,128)S(1)}) custom-call(s32[2]{0:T(128)S(1)} %pad_add_fusion.place, s32[8,5]{1,0:T(8,128)S(1)} %fusion.2.work, bf16[2,19,16,512]{3,2,1,0:T(8,128)(2,1)S(1)} %shard_map.75.pair, bf16[2,19,16,512]{3,2,1,0:T(8,128)(2,1)S(1)} %shard_map.78.near1, ...), custom_call_target="tpu_custom_call", output_to_operand_aliasing={{0}: (7, {})} | custom-call | flops 11000000512 | bytes 1000000 | tf_op jit(solution)/shard_map/pallas_call | solution.py:243
  44.8 0.0 copy-start.5
  44.8 0.6 copy-done.5
  45.4 0.7 collective-permute-done.7.array.far1
  46.1 4.8 %collective-permute-start.9 = (bf16[1,19,16,512]{3,2,1,0:T(8,128)(2,1)S(1)}, bf16[1,19,16,512]{3,2,1,0:T(8,128)(2,1)}, u32[]{:S(2)}, u32[]{:S(2)}) collective-permute-start(bf16[1,19,16,512]{3,2,1,0:T(8,128)(2,1)S(1)} %shard_map.80), channel_id=1, source_target_pairs={{1,0},{0,1},{3,2},{2,3},{5,4},{4,5},{7,6},{6,7},{9,8},{8,9},{11,10... | collective-permute-start | bytes 933896 | tf_op jit(solution)/shard_map/ppermute | solution.py:37
  51.0 0.1 copy.14
  51.1 1.3 %collective-permute-done.9.far2 = bf16[1,19,16,512]{3,2,1,0:T(8,128)(2,1)} collective-permute-done((bf16[1,19,16,512]{3,2,1,0:T(8,128)(2,1)S(1)}, bf16[1,19,16,512]{3,2,1,0:T(8,128)(2,1)}, u32[]{:S(2)}, u32[]{:S(2)}) %collective-permute-start.9) | collective-permute-done | bytes 311328 | tf_op jit(solution)/shard_map/ppermute | solution.py:37
  52.3 24.1 %shard_map.81.acc = f32[8,16,1024]{2,1,0:T(8,128)S(1)} custom-call(s32[2]{0:T(128)S(1)} %pad_add_fusion.place, s32[8,5]{1,0:T(8,128)S(1)} %fusion.2.work, bf16[2,19,16,512]{3,2,1,0:T(8,128)(2,1)S(1)} %shard_map.75.pair, bf16[2,19,16,512]{3,2,1,0:T(8,128)(2,1)S(1)} %shard_map.78.near1, ...), custom_call_target="tpu_custom_call", output_to_operand_aliasing={{}: (7, {})} | custom-call | flops 20999999488 | bytes 1000000 | tf_op jit(solution)/shard_map/pallas_call | solution.py:243
  76.4 4.4 %shard_map.82 = bf16[16,8192]{1,0:T(8,128)(2,1)} custom-call(s32[2]{0:T(128)S(1)} %pad_add_fusion.place, s32[4,3]{1,0:T(4,128)S(1)} %bitcast.12, f32[8,16,1024]{2,1,0:T(8,128)S(1)} %shard_map.81.acc, f32[16,16,128]{2,1,0:T(8,128)S(1)} %copy-done.6, f32[16,16,128]{2,1,0:T(8,128)S(1)} %collective-permute-done.8.refs_1_, f32[4,2,128,128]{3,2,1,0:T(8,128)S(1)} %copy-done.4, ...), custom_call_target="tpu_custom_call" | custom-call | flops 3000000000 | bytes 1000000 | tf_op jit(solution)/shard_map/pallas_call | solution.py:243
  (25 shorter events, 0.1 us)
Async XLA Ops:
  2.1 2.7 %collective-permute-start.1 = (f32[1,16,128]{2,1,0:T(8,128)S(1)}, f32[1,16,128]{2,1,0:T(8,128)S(1)}, u32[]{:S(2)}, u32[]{:S(2)}) collective-permute-start(f32[1,16,128]{2,1,0:T(8,128)S(1)} %convolution_bitcast_fusion.mine), channel_id=1, source_target_pairs={{1,0},{0,1},{3,2},{2,3},{5,4},{4,5},{7,6},{6,7},{9,8},{8,9},{11,10... | collective-permute-start | bytes 24584 | tf_op jit(solution)/shard_map/ppermute | solution.py:37
  4.6 5.6 %collective-permute-start = (bf16[19,16,512]{2,1,0:T(8,128)(2,1)}, bf16[19,16,512]{2,1,0:T(8,128)(2,1)S(1)}, u32[]{:S(2)}, u32[]{:S(2)}) collective-permute-start(bf16[19,16,512]{2,1,0:T(8,128)(2,1)} %shard_map.73.own), channel_id=1, source_target_pairs={{1,0},{0,1},{3,2},{2,3},{5,4},{4,5},{7,6},{6,7},{9,8},{8,9},{11,10... | collective-permute-start | bytes 933896 | tf_op jit(solution)/shard_map/ppermute | solution.py:37
  4.8 3.4 %collective-permute-start.2 = (f32[2,16,128]{2,1,0:T(8,128)S(1)}, f32[2,16,128]{2,1,0:T(8,128)S(1)}, u32[]{:S(2)}, u32[]{:S(2)}) collective-permute-start(f32[2,16,128]{2,1,0:T(8,128)S(1)} %pad_maximum_fusion.4), channel_id=1, source_target_pairs={{8,0},{9,1},{10,2},{11,3},{12,4},{13,5},{14,6},{15,7},{0,8},{1,9},... | collective-permute-start | bytes 49160 | tf_op jit(solution)/shard_map/ppermute | solution.py:37
  5.4 1.0 %copy-start.1 = (bf16[19,16,512]{2,1,0:T(8,128)(2,1)S(1)}, bf16[19,16,512]{2,1,0:T(8,128)(2,1)}, u32[]{:S(2)}) copy-start(bf16[19,16,512]{2,1,0:T(8,128)(2,1)} %shard_map.73.own) | copy-start | bytes 933892
  8.2 2.0 %copy-start.2 = (bf16[19,16,512]{2,1,0:T(8,128)(2,1)S(1)}, bf16[19,16,512]{2,1,0:T(8,128)(2,1)}, u32[]{:S(2)}) copy-start(bf16[19,16,512]{2,1,0:T(8,128)(2,1)} %shard_map.73.own) | copy-start | bytes 933892
  8.2 4.4 %collective-permute-start.3 = (f32[4,16,128]{2,1,0:T(8,128)S(1)}, f32[4,16,128]{2,1,0:T(8,128)S(1)}, u32[]{:S(2)}, u32[]{:S(2)}) collective-permute-start(f32[4,16,128]{2,1,0:T(8,128)S(1)} %pad_maximum_fusion.3), channel_id=1, source_target_pairs={{16,0},{17,1},{18,2},{19,3},{20,4},{21,5},{22,6},{23,7},{24,8},{25... | collective-permute-start | bytes 98312 | tf_op jit(solution)/shard_map/ppermute | solution.py:37
  12.6 17.0 %collective-permute-start.4 = (bf16[2,19,16,512]{3,2,1,0:T(8,128)(2,1)S(1)}, bf16[2,19,16,512]{3,2,1,0:T(8,128)(2,1)S(1)}, u32[]{:S(2)}, u32[]{:S(2)}) collective-permute-start(bf16[2,19,16,512]{3,2,1,0:T(8,128)(2,1)S(1)} %shard_map.75.pair), channel_id=1, source_target_pairs={{2,1},{1,2},{4,3},{3,4},{6,5},{5,6},{8,7},{7,8},{10,9},{9,10},{12,... | collective-permute-start | bytes 1867784 | tf_op jit(solution)/shard_map/ppermute | solution.py:37
  19.4 7.4 %collective-permute-start.5 = (f32[8,16,128]{2,1,0:T(8,128)S(1)}, f32[8,16,128]{2,1,0:T(8,128)S(1)}, u32[]{:S(2)}, u32[]{:S(2)}) collective-permute-start(f32[8,16,128]{2,1,0:T(8,128)S(1)} %pad_maximum_fusion.2), channel_id=1, source_target_pairs={{2,0},{3,1},{0,2},{1,3},{6,4},{7,5},{4,6},{5,7},{10,8},{11,9},{8,1... | collective-permute-start | bytes 196616 | tf_op jit(solution)/shard_map/ppermute | solution.py:37
  19.5 10.1 %copy-start.7 = (s32[8,5]{1,0:T(8,128)S(1)}, s32[8,5]{1,0:T(8,128)}, u32[]{:S(2)}) copy-start(s32[8,5]{1,0:T(8,128)} %param.12) | copy-start | bytes 484
  29.5 2.1 %collective-permute-start.6 = (bf16[2,19,16,512]{3,2,1,0:T(8,128)(2,1)S(1)}, bf16[2,19,16,512]{3,2,1,0:T(8,128)(2,1)S(1)}, u32[]{:S(2)}, u32[]{:S(2)}) collective-permute-start(bf16[2,19,16,512]{3,2,1,0:T(8,128)(2,1)S(1)} %shard_map.78.near1), channel_id=1, source_target_pairs={{1,0},{0,1},{3,2},{2,3},{5,4},{4,5},{7,6},{6,7},{9,8},{8,9},{11,10... | collective-permute-start | bytes 1867784 | tf_op jit(solution)/shard_map/ppermute | solution.py:37
  29.6 21.4 %copy-start.8 = (s32[1,4,3]{1,0,2:T(1,128)S(1)}, s32[1,4,3]{1,0,2:T(1,128)}, u32[]{:S(2)}) copy-start(s32[1,4,3]{1,0,2:T(1,128)} %param.13) | copy-start | bytes 148
  29.6 15.8 %collective-permute-start.8 = (f32[16,16,128]{2,1,0:T(8,128)S(1)}, f32[16,16,128]{2,1,0:T(8,128)S(1)}, u32[]{:S(2)}, u32[]{:S(2)}) collective-permute-start(f32[16,16,128]{2,1,0:T(8,128)S(1)} %pad_maximum_fusion.1), channel_id=1, source_target_pairs={{4,0},{5,1},{6,2},{7,3},{0,4},{1,5},{2,6},{3,7},{12,8},{13,9},{14,... | collective-permute-start | bytes 393224 | tf_op jit(solution)/shard_map/ppermute | solution.py:37
  29.7 16.4 %collective-permute-start.7 = (bf16[2,19,16,512]{3,2,1,0:T(8,128)(2,1)S(1)}, bf16[2,19,16,512]{3,2,1,0:T(8,128)(2,1)S(1)}, u32[]{:S(2)}, u32[]{:S(2)}) collective-permute-start(bf16[2,19,16,512]{3,2,1,0:T(8,128)(2,1)S(1)} %shard_map.78.near1), channel_id=1, source_target_pairs={{3,1},{0,2},{5,3},{2,4},{7,5},{4,6},{9,7},{6,8},{11,9},{8,10},{13,... | collective-permute-start | bytes 1867784 | tf_op jit(solution)/shard_map/ppermute | solution.py:37
  44.8 0.7 copy-start.5
  46.1 6.2 %collective-permute-start.9 = (bf16[1,19,16,512]{3,2,1,0:T(8,128)(2,1)S(1)}, bf16[1,19,16,512]{3,2,1,0:T(8,128)(2,1)}, u32[]{:S(2)}, u32[]{:S(2)}) collective-permute-start(bf16[1,19,16,512]{3,2,1,0:T(8,128)(2,1)S(1)} %shard_map.80), channel_id=1, source_target_pairs={{1,0},{0,1},{3,2},{2,3},{5,4},{4,5},{7,6},{6,7},{9,8},{8,9},{11,10... | collective-permute-start | bytes 933896 | tf_op jit(solution)/shard_map/ppermute | solution.py:37
  51.1 25.3 %copy-start = (bf16[8,1024,128]{2,1,0:T(8,128)(2,1)S(1)}, bf16[8,1024,128]{2,1,0:T(8,128)(2,1)}, u32[]{:S(2)}) copy-start(bf16[8,1024,128]{2,1,0:T(8,128)(2,1)} %refs_4_.1) | copy-start | bytes 6291460
  51.1 25.3 %copy-start.3 = (f32[4,3,128,128]{3,2,1,0:T(8,128)S(1)}, f32[4,3,128,128]{3,2,1,0:T(8,128)}, u32[]{:S(2)}) copy-start(f32[4,3,128,128]{3,2,1,0:T(8,128)} %refs_3_.1) | copy-start | bytes 2359300
  51.1 25.3 %copy-start.4 = (f32[4,2,128,128]{3,2,1,0:T(8,128)S(1)}, f32[4,2,128,128]{3,2,1,0:T(8,128)}, u32[]{:S(2)}) copy-start(f32[4,2,128,128]{3,2,1,0:T(8,128)} %refs_2_.1) | copy-start | bytes 1572868
  51.1 25.3 %copy-start.6 = (f32[16,16,128]{2,1,0:T(8,128)S(1)}, f32[16,16,128]{2,1,0:T(8,128)}, u32[]{:S(2)}) copy-start(f32[16,16,128]{2,1,0:T(8,128)} %copy-done.5) | copy-start | bytes 393220

commit v5 on v4

--- a/solution.py
+++ b/solution.py
@@ -24,7 +24,7 @@
 SLOT_OFFSETS = (0, 1, -1, -2, 2, 3, -3, -4, 4)
 SELF = (1, 2, 8)
 BITS = (0, 3, 4, 1, 2)
-BUDGET = 11
+BUDGET = 12
 
 
 def params(mib):
@@ -119,11 +119,12 @@
     store_features(dst, 0, rows + [(9, high), (10, middle), (11, low)], tmp)
 
 
-def load_cluster(block, slot, sign, vals, feats, tmp):
+def load_cluster(block, slot, sign, vals, feats, tmp, window_slot=None):
     for l in range(LEAVES_DEV):
         vals[slot * LEAVES_DEV + l, :, :HALF] = block[2 * l]
         vals[slot * LEAVES_DEV + l, :, HALF:] = block[2 * l + 1]
-    first_leaf = SLOT_OFFSETS[slot] * LEAVES_DEV * sign
+    offset = SLOT_OFFSETS[slot if window_slot is None else window_slot]
+    first_leaf = offset * LEAVES_DEV * sign
     source_features(block, first_leaf, feats, slot * LEAVES_DEV, tmp)
 
 
@@ -135,27 +136,50 @@
         acc[i, :, t : t + 512] += jnp.dot(vals[w], kernel_vals, preferred_element_type=f32)
 
 
-def add_listed(part, work, tgt, vals, feats, acc):
-    def item(it, count):
+def add_listed(part, work, items, tgt, vals, feats, acc):
+    def select(it, counts):
+        first, chosen = counts
         i, k = it // (NB - 1), it % (NB - 1) + 1
         w = work[i, k]
-        in_first = (w < 6 * LEAVES_DEV) & (count < BUDGET)
-
-        @pl.when(in_first if part == 1 else jnp.logical_not(in_first))
-        def _():
-            add_block(i, w, tgt, vals, feats, acc)
-
-        return count + in_first.astype(jnp.int32)
-
-    lax.fori_loop(0, LEAVES_DEV * (NB - 1), item, jnp.int32(0))
+        in_first = (w < 6 * LEAVES_DEV) & (first < BUDGET)
+        in_last = w >= 8 * LEAVES_DEV
+        in_part = (
+            in_first,
+            jnp.logical_not(in_first | in_last),
+            in_last,
+        )[part - 1]
+        items[chosen] = i * 128 + w
+        return first + in_first.astype(jnp.int32), chosen + in_part.astype(jnp.int32)
+
+    _, count = lax.fori_loop(
+        0, LEAVES_DEV * (NB - 1), select, (jnp.int32(0), jnp.int32(0))
+    )
+    base = 8 * LEAVES_DEV if part == 3 else 0
+
+    def several(group):
+        def some(g, carry):
+            for u in range(group):
+                item = items[g * group + u]
+                add_block(item // 128, item % 128 - base, tgt, vals, feats, acc)
+            return carry
+
+        return some
+
+    whole = count // 4
+    lax.fori_loop(0, whole, several(4), 0)
+    lax.fori_loop(whole * 4, count, several(1), 0)
 
 
 def own_blocks(first, last, tgt, vals, feats, acc):
-    def one(i, carry):
-        add_block(i, i, tgt, vals, feats, acc)
+    group = 2 if (last - first) % 2 == 0 else 1
+
+    def some(n, carry):
+        for u in range(group):
+            i = first + n * group + u
+            add_block(i, i, tgt, vals, feats, acc)
         return carry
 
-    lax.fori_loop(first, last, one, 0)
+    lax.fori_loop(0, (last - first) // group, some, 0)
 
 
 def join(mine, theirs, joined):
@@ -189,28 +213,36 @@
 
 
 def near_kernel(
-    place, work, pair, near1, near2, mine, theirs, acc_in, acc, joined, vals, feats, tmp, tgt
+    place, work, pair, near1, near2, mine, theirs, acc_in, acc, joined, vals, feats, tmp, tgt, items
 ):
     join(mine, theirs, joined)
     constant_rows(tmp, (6, 7, 8))
     target_features(pair.at[0], tgt, tmp)
     load_clusters([pair, near1, near2], place[1], vals, feats, tmp)
-    add_listed(1, work, tgt, vals, feats, acc)
-
-
-def last_kernel(place, work, pair, near1, near2, far1, far2, acc_in, acc, vals, feats, tmp, tgt):
+    add_listed(1, work, items, tgt, vals, feats, acc)
+
+
+def last_kernel(place, work, pair, near1, near2, far1, acc_in, acc, vals, feats, tmp, tgt, items):
     constant_rows(tmp, (6, 7, 8))
     target_features(pair.at[0], tgt, tmp)
-    load_clusters([pair, near1, near2, far1, far2], place[1], vals, feats, tmp)
-    add_listed(2, work, tgt, vals, feats, acc)
-
-
-def tree_kernel(place, flags, acc, *refs):
-    groups, (transfer, coupling, basis, out) = refs[:2], refs[2:]
+    load_clusters([pair, near1, near2, far1], place[1], vals, feats, tmp)
+    add_listed(2, work, items, tgt, vals, feats, acc)
+
+
+def tree_kernel(
+    place, work, flags, pair, far2, mine, theirs, transfer, coupling, basis, acc_in,
+    acc, out, vals, feats, tmp, tgt, items,
+):
+    constant_rows(tmp, (6, 7, 8))
+    target_features(pair.at[0], tgt, tmp)
+    constant_rows(tmp, (9, 10, 11))
+    load_cluster(far2.at[0], 0, place[1], vals, feats, tmp, 8)
+    add_listed(3, work, items, tgt, vals, feats, acc)
+    n = mine.shape[0]
     coefs = []
-    for m in range(32):
+    for m in range(2 * n):
         where = sum(((m >> bit) & 1) << at for at, bit in enumerate(BITS))
-        coefs.append(groups[where // 16][where % 16])
+        coefs.append(mine[where] if where < n else theirs[where - n])
     down = tree(place[0], flags, coefs, transfer, coupling)
     scale = 1.0 / math.sqrt(NB * LEAF)
     for l in range(LEAVES_DEV):
@@ -230,6 +262,7 @@
         pltpu.VMEM((slots * LEAVES_DEV, FEATS, LEAF), bf16),
         TMP,
         pltpu.VMEM((LEAVES_DEV, FEATS, LEAF), bf16),
+        pltpu.SMEM((LEAVES_DEV * NB,), jnp.int32),
     )
 
 
@@ -394,19 +427,20 @@
     (acc,) = staged(
         last_kernel,
         [place, work],
-        [pair, near1, near2, far1, far2],
+        [pair, near1, near2, far1],
         [acc],
         [],
-        21,
-        window_scratch(9),
+        20,
+        window_scratch(8),
     )
     return staged(
         tree_kernel,
-        [place, couple_flags[0]],
-        [acc, coefs, following, transfer, coupling, leaf_basis],
-        [],
+        [place, work, couple_flags[0]],
+        [pair, far2, coefs, following, transfer, coupling, leaf_basis],
+        [acc],
         [jax.ShapeDtypeStruct((RHS, LEAVES_DEV * LEAF), bf16)],
         3,
+        window_scratch(1),
     )[-1]
 
 

time: 81.1 us -> 76.3 us (0.941)
  Pallas kernels: 52.5 us -> 49.1 us
  starting transfers between devices: 16.1 us -> 14.9 us
    pallas_call x6, Pallas kernels: 50.8 us -> 47.4 us  [staged(): pl.pallas_call(kernel, out_shape=tuple(state_shapes) + tuple(outs), in_sp...]
    ppermute x10, starting transfers between devices: 16.1 us -> 14.9 us  [permuted(): return lax.ppermute(array, 'leaf', route)]
    unnamed x19 -> x15, local copies, waits for them, and re-layouts: 1.74 us -> 1.09 us
  transfers between devices with their start and end apart: 10 -> 10, of which waited for: 5 -> 4; matrix products, arithmetic and copies ran while one was open for 0% -> 0% of each run, Pallas kernels for 30% -> 54%
where the time goes in v5:
time: 76.3 us; the launch traced here: 76 us
  Pallas kernels  49.1 us (64%)
  starting transfers between devices  14.9 us (20%)
  waiting for transfers between devices  8.4 us (11%)
  matrix products  2.07 us (3%)
  local copies, waits for them, and re-layouts  1.09 us (1%)
    pallas_call x6, Pallas kernels, staged(): pl.pallas_call(kernel, out_shape=tuple(state_shapes) + tuple(outs), in_sp...  47.4 us
    ppermute x10, starting transfers between devices, permuted(): return lax.ppermute(array, 'leaf', route)  14.9 us
    ppermute x10, waiting for transfers between devices, permuted(): return lax.ppermute(array, 'leaf', route)  8.4 us
    dot_general x1, matrix products, local(): jnp.dot(charges, leaf_basis.reshape(LEAVES_DEV * LEAF, RANK), preferred_e...  2.07 us
    pallas_call x1, Pallas kernels, pack(): pl.pallas_call(pack_kernel, out_shape=jax.ShapeDtypeStruct(PAYLOAD, bf16)...  1.75 us
  transfers between devices with their start and end apart: 10, of which 4 were waited for; matrix products, arithmetic and copies ran while one was open for 0% of the time, Pallas kernels for 54%

profile of v5, /device:TPU:127, one launch (start us, length us, event | category | flops | bytes accessed | tf_op | source)
XLA Modules:
  0.0 76.0 jit_solution(15975298898062152567)
XLA Ops:
  0.0 2.1 %convolution_bitcast_fusion.mine = f32[1,16,128]{2,1,0:T(8,128)S(1)} fusion(bf16[16,8192]{1,0:T(8,128)(2,1)} %charges_hbm.1, bf16[8192,128]{1,0:T(8,128)(2,1)} %bitcast.10), kind=kOutput, calls=%fused_computation | convolution fusion | flops 33554432 | bytes 2367488 | tf_op jit(solution)/shard_map/dot_general | solution.py:382
  2.1 0.8 %collective-permute-start.1 = (f32[1,16,128]{2,1,0:T(8,128)S(1)}, f32[1,16,128]{2,1,0:T(8,128)S(1)}, u32[]{:S(2)}, u32[]{:S(2)}) collective-permute-start(f32[1,16,128]{2,1,0:T(8,128)S(1)} %convolution_bitcast_fusion.mine), channel_id=1, source_target_pairs={{1,0},{0,1},{3,2},{2,3},{5,4},{4,5},{7,6},{6,7},{9,8},{8,9},{11,10... | collective-permute-start | bytes 24584 | tf_op jit(solution)/shard_map/ppermute | solution.py:37
  2.8 1.8 %shard_map.73.own = bf16[19,16,512]{2,1,0:T(8,128)(2,1)} custom-call(bf16[16,8192]{1,0:T(8,128)(2,1)} %charges_hbm.1, bf16[3,8192]{1,0:T(4,128)(2,1)} %points_hbm.1), custom_call_target="tpu_custom_call" | custom-call | flops 1000000 | bytes 1000000 | tf_op jit(solution)/shard_map/pallas_call | solution.py:62
  4.6 0.1 collective-permute-start
  4.7 0.1 pad_add_fusion.place
  4.8 0.6 collective-permute-start.2
  5.4 1.0 %copy-done.1 = bf16[19,16,512]{2,1,0:T(8,128)(2,1)S(1)} copy-done((bf16[19,16,512]{2,1,0:T(8,128)(2,1)S(1)}, bf16[19,16,512]{2,1,0:T(8,128)(2,1)}, u32[]{:S(2)}) %copy-start.1) | copy-done | bytes 311320
  6.4 1.9 %shard_map.74 = (f32[8,16,1024]{2,1,0:T(8,128)S(1)}, bf16[8,16,1024]{2,1,0:T(8,128)(2,1)S(1)}, bf16[8,16,1024]{2,1,0:T(8,128)(2,1)S(1)}, bf16[8,16,1024]{2,1,0:T(8,128)(2,1)S(1)}, f32[2,16,128]{2,1,0:T(8,128)S(1)}) custom-call(s32[2]{0:T(128)S(1)} %pad_add_fusion.place, bf16[19,16,512]{2,1,0:T(8,128)(2,1)S(1)} %copy-done.1, ...), custom_call_target="tpu_custom_call" | custom-call | flops 2000000000 | bytes 1000000 | tf_op jit(solution)/shard_map/pallas_call | solution.py:276
  8.2 0.9 %collective-permute-start.3 = (f32[4,16,128]{2,1,0:T(8,128)S(1)}, f32[4,16,128]{2,1,0:T(8,128)S(1)}, u32[]{:S(2)}, u32[]{:S(2)}) collective-permute-start(f32[4,16,128]{2,1,0:T(8,128)S(1)} %pad_maximum_fusion.3), channel_id=1, source_target_pairs={{16,0},{17,1},{18,2},{19,3},{20,4},{21,5},{22,6},{23,7},{24,8},{25... | collective-permute-start | bytes 98312 | tf_op jit(solution)/shard_map/ppermute | solution.py:37
  9.1 1.0 %shard_map.76 = (f32[8,16,1024]{2,1,0:T(8,128)S(1)}, f32[4,16,128]{2,1,0:T(8,128)S(1)}) custom-call(bf16[8,16,1024]{2,1,0:T(8,128)(2,1)S(1)} %get-tuple-element.18.tgt, bf16[8,16,1024]{2,1,0:T(8,128)(2,1)S(1)} %get-tuple-element.19.vals, bf16[8,16,1024]{2,1,0:T(8,128)(2,1)S(1)} %get-tuple-element.20.feats, ...), custom_call_target="tpu_custom_call", output_to_operand_aliasing={{0}: (5, {})} | custom-call | flops 1000000000 | bytes 1000000 | tf_op jit(solution)/shard_map/pallas_call | solution.py:276
  10.2 0.0 collective-permute-done
  10.2 0.1 pad_maximum_fusion.refs_0_
  10.3 2.3 %collective-permute-done.3.refs_1_.theirs = f32[4,16,128]{2,1,0:T(8,128)S(1)} collective-permute-done((f32[4,16,128]{2,1,0:T(8,128)S(1)}, f32[4,16,128]{2,1,0:T(8,128)S(1)}, u32[]{:S(2)}, u32[]{:S(2)}) %collective-permute-start.3) | collective-permute-done | bytes 32800 | tf_op jit(solution)/shard_map/ppermute | solution.py:37
  12.6 6.8 %collective-permute-start.4 = (bf16[2,19,16,512]{3,2,1,0:T(8,128)(2,1)S(1)}, bf16[2,19,16,512]{3,2,1,0:T(8,128)(2,1)S(1)}, u32[]{:S(2)}, u32[]{:S(2)}) collective-permute-start(bf16[2,19,16,512]{3,2,1,0:T(8,128)(2,1)S(1)} %shard_map.75.pair), channel_id=1, source_target_pairs={{2,1},{1,2},{4,3},{3,4},{6,5},{5,6},{8,7},{7,8},{10,9},{9,10},{12,... | collective-permute-start | bytes 1867784 | tf_op jit(solution)/shard_map/ppermute | solution.py:37
  19.4 0.1 collective-permute-start.5
  19.5 0.0 copy-start.6
  19.5 0.0 copy-start.5
  19.5 5.6 %shard_map.77 = (f32[8,16,1024]{2,1,0:T(8,128)S(1)}, f32[8,16,128]{2,1,0:T(8,128)S(1)}) custom-call(bf16[8,16,1024]{2,1,0:T(8,128)(2,1)S(1)} %get-tuple-element.18.tgt, bf16[8,16,1024]{2,1,0:T(8,128)(2,1)S(1)} %get-tuple-element.19.vals, bf16[8,16,1024]{2,1,0:T(8,128)(2,1)S(1)} %get-tuple-element.20.feats, ...), custom_call_target="tpu_custom_call", output_to_operand_aliasing={{0}: (5, {})} | custom-call | flops 6000000000 | bytes 1000000 | tf_op jit(solution)/shard_map/pallas_call | solution.py:276
  25.1 1.6 %collective-permute-done.5.refs_2_.theirs = f32[8,16,128]{2,1,0:T(8,128)S(1)} collective-permute-done((f32[8,16,128]{2,1,0:T(8,128)S(1)}, f32[8,16,128]{2,1,0:T(8,128)S(1)}, u32[]{:S(2)}, u32[]{:S(2)}) %collective-permute-start.5) | collective-permute-done | bytes 65568 | tf_op jit(solution)/shard_map/ppermute | solution.py:37
  26.7 2.8 %collective-permute-done.4.refs_0_ = bf16[2,19,16,512]{3,2,1,0:T(8,128)(2,1)S(1)} collective-permute-done((bf16[2,19,16,512]{3,2,1,0:T(8,128)(2,1)S(1)}, bf16[2,19,16,512]{3,2,1,0:T(8,128)(2,1)S(1)}, u32[]{:S(2)}, u32[]{:S(2)}) %collective-permute-start.4) | collective-permute-done | bytes 622624 | tf_op jit(solution)/shard_map/ppermute | solution.py:37
  29.6 0.0 collective-permute-start.7
  29.6 0.1 copy.15
  29.7 0.1 collective-permute-start.8
  29.8 1.9 %collective-permute-start.6 = (bf16[2,19,16,512]{3,2,1,0:T(8,128)(2,1)S(1)}, bf16[2,19,16,512]{3,2,1,0:T(8,128)(2,1)S(1)}, u32[]{:S(2)}, u32[]{:S(2)}) collective-permute-start(bf16[2,19,16,512]{3,2,1,0:T(8,128)(2,1)S(1)} %shard_map.78.near1), channel_id=1, source_target_pairs={{3,1},{0,2},{5,3},{2,4},{7,5},{4,6},{9,7},{6,8},{11,9},{8,10},{13,... | collective-permute-start | bytes 1867784 | tf_op jit(solution)/shard_map/ppermute | solution.py:37
  31.7 12.8 %shard_map.79 = (f32[8,16,1024]{2,1,0:T(8,128)S(1)}, f32[16,16,128]{2,1,0:T(8,128)S(1)}) custom-call(s32[2]{0:T(128)S(1)} %pad_add_fusion.place, s32[8,5]{1,0:T(8,128)S(1)} %fusion.2.work, bf16[2,19,16,512]{3,2,1,0:T(8,128)(2,1)S(1)} %shard_map.75.pair, bf16[2,19,16,512]{3,2,1,0:T(8,128)(2,1)S(1)} %shard_map.78.near1, ...), custom_call_target="tpu_custom_call", output_to_operand_aliasing={{0}: (7, {})} | custom-call | flops 12000000000 | bytes 1000000 | tf_op jit(solution)/shard_map/pallas_call | solution.py:276
  44.6 1.7 %collective-permute-done.6.array.far1 = bf16[2,19,16,512]{3,2,1,0:T(8,128)(2,1)S(1)} collective-permute-done((bf16[2,19,16,512]{3,2,1,0:T(8,128)(2,1)S(1)}, bf16[2,19,16,512]{3,2,1,0:T(8,128)(2,1)S(1)}, u32[]{:S(2)}, u32[]{:S(2)}) %collective-permute-start.6) | collective-permute-done | bytes 622624 | tf_op jit(solution)/shard_map/ppermute | solution.py:37
  46.2 0.0 copy-start
  46.2 0.0 copy-start.3
  46.3 0.0 copy-start.4
  46.3 3.7 %collective-permute-start.9 = (bf16[1,19,16,512]{3,2,1,0:T(8,128)(2,1)S(1)}, bf16[1,19,16,512]{3,2,1,0:T(8,128)(2,1)S(1)}, u32[]{:S(2)}, u32[]{:S(2)}) collective-permute-start(bf16[1,19,16,512]{3,2,1,0:T(8,128)(2,1)S(1)} %shard_map.80), channel_id=1, source_target_pairs={{1,0},{0,1},{3,2},{2,3},{5,4},{4,5},{7,6},{6,7},{9,8},{8,9},{11,10... | collective-permute-start | bytes 933896 | tf_op jit(solution)/shard_map/ppermute | solution.py:37
  50.0 17.6 %shard_map.81.acc_in = f32[8,16,1024]{2,1,0:T(8,128)S(1)} custom-call(s32[2]{0:T(128)S(1)} %pad_add_fusion.place, s32[8,5]{1,0:T(8,128)S(1)} %fusion.2.work, bf16[2,19,16,512]{3,2,1,0:T(8,128)(2,1)S(1)} %shard_map.75.pair, bf16[2,19,16,512]{3,2,1,0:T(8,128)(2,1)S(1)} %shard_map.78.near1, ...), custom_call_target="tpu_custom_call", output_to_operand_aliasing={{}: (6, {})} | custom-call | flops 20000000000 | bytes 1000000 | tf_op jit(solution)/shard_map/pallas_call | solution.py:276
  67.6 8.4 %shard_map.82 = (f32[8,16,1024]{2,1,0:T(8,128)S(1)}, bf16[16,8192]{1,0:T(8,128)(2,1)}) custom-call(s32[2]{0:T(128)S(1)} %pad_add_fusion.place, s32[8,5]{1,0:T(8,128)S(1)} %fusion.2.work, s32[4,3]{1,0:T(4,128)S(1)} %bitcast.12, bf16[2,19,16,512]{3,2,1,0:T(8,128)(2,1)S(1)} %shard_map.75.pair, ...), custom_call_target="tpu_custom_call", output_to_operand_aliasing={{0}: (10, {})} | custom-call | flops 3000000000 | bytes 1000000 | tf_op jit(solution)/shard_map/pallas_call | solution.py:276
  (21 shorter events, 0.1 us)
Async XLA Ops:
  2.1 2.7 %collective-permute-start.1 = (f32[1,16,128]{2,1,0:T(8,128)S(1)}, f32[1,16,128]{2,1,0:T(8,128)S(1)}, u32[]{:S(2)}, u32[]{:S(2)}) collective-permute-start(f32[1,16,128]{2,1,0:T(8,128)S(1)} %convolution_bitcast_fusion.mine), channel_id=1, source_target_pairs={{1,0},{0,1},{3,2},{2,3},{5,4},{4,5},{7,6},{6,7},{9,8},{8,9},{11,10... | collective-permute-start | bytes 24584 | tf_op jit(solution)/shard_map/ppermute | solution.py:37
  4.6 5.6 %collective-permute-start = (bf16[19,16,512]{2,1,0:T(8,128)(2,1)}, bf16[19,16,512]{2,1,0:T(8,128)(2,1)S(1)}, u32[]{:S(2)}, u32[]{:S(2)}) collective-permute-start(bf16[19,16,512]{2,1,0:T(8,128)(2,1)} %shard_map.73.own), channel_id=1, source_target_pairs={{1,0},{0,1},{3,2},{2,3},{5,4},{4,5},{7,6},{6,7},{9,8},{8,9},{11,10... | collective-permute-start | bytes 933896 | tf_op jit(solution)/shard_map/ppermute | solution.py:37
  4.8 3.4 %collective-permute-start.2 = (f32[2,16,128]{2,1,0:T(8,128)S(1)}, f32[2,16,128]{2,1,0:T(8,128)S(1)}, u32[]{:S(2)}, u32[]{:S(2)}) collective-permute-start(f32[2,16,128]{2,1,0:T(8,128)S(1)} %pad_maximum_fusion.4), channel_id=1, source_target_pairs={{8,0},{9,1},{10,2},{11,3},{12,4},{13,5},{14,6},{15,7},{0,8},{1,9},... | collective-permute-start | bytes 49160 | tf_op jit(solution)/shard_map/ppermute | solution.py:37
  5.4 1.0 %copy-start.1 = (bf16[19,16,512]{2,1,0:T(8,128)(2,1)S(1)}, bf16[19,16,512]{2,1,0:T(8,128)(2,1)}, u32[]{:S(2)}) copy-start(bf16[19,16,512]{2,1,0:T(8,128)(2,1)} %shard_map.73.own) | copy-start | bytes 933892
  8.2 2.0 %copy-start.2 = (bf16[19,16,512]{2,1,0:T(8,128)(2,1)S(1)}, bf16[19,16,512]{2,1,0:T(8,128)(2,1)}, u32[]{:S(2)}) copy-start(bf16[19,16,512]{2,1,0:T(8,128)(2,1)} %shard_map.73.own) | copy-start | bytes 933892
  8.2 4.4 %collective-permute-start.3 = (f32[4,16,128]{2,1,0:T(8,128)S(1)}, f32[4,16,128]{2,1,0:T(8,128)S(1)}, u32[]{:S(2)}, u32[]{:S(2)}) collective-permute-start(f32[4,16,128]{2,1,0:T(8,128)S(1)} %pad_maximum_fusion.3), channel_id=1, source_target_pairs={{16,0},{17,1},{18,2},{19,3},{20,4},{21,5},{22,6},{23,7},{24,8},{25... | collective-permute-start | bytes 98312 | tf_op jit(solution)/shard_map/ppermute | solution.py:37
  12.6 17.0 %collective-permute-start.4 = (bf16[2,19,16,512]{3,2,1,0:T(8,128)(2,1)S(1)}, bf16[2,19,16,512]{3,2,1,0:T(8,128)(2,1)S(1)}, u32[]{:S(2)}, u32[]{:S(2)}) collective-permute-start(bf16[2,19,16,512]{3,2,1,0:T(8,128)(2,1)S(1)} %shard_map.75.pair), channel_id=1, source_target_pairs={{2,1},{1,2},{4,3},{3,4},{6,5},{5,6},{8,7},{7,8},{10,9},{9,10},{12,... | collective-permute-start | bytes 1867784 | tf_op jit(solution)/shard_map/ppermute | solution.py:37
  19.4 7.4 %collective-permute-start.5 = (f32[8,16,128]{2,1,0:T(8,128)S(1)}, f32[8,16,128]{2,1,0:T(8,128)S(1)}, u32[]{:S(2)}, u32[]{:S(2)}) collective-permute-start(f32[8,16,128]{2,1,0:T(8,128)S(1)} %pad_maximum_fusion.2), channel_id=1, source_target_pairs={{2,0},{3,1},{0,2},{1,3},{6,4},{7,5},{4,6},{5,7},{10,8},{11,9},{8,1... | collective-permute-start | bytes 196616 | tf_op jit(solution)/shard_map/ppermute | solution.py:37
  19.5 10.1 %copy-start.6 = (s32[1,4,3]{1,0,2:T(1,128)S(1)}, s32[1,4,3]{1,0,2:T(1,128)}, u32[]{:S(2)}) copy-start(s32[1,4,3]{1,0,2:T(1,128)} %param.13) | copy-start | bytes 148
  19.5 10.2 %copy-start.5 = (s32[8,5]{1,0:T(8,128)S(1)}, s32[8,5]{1,0:T(8,128)}, u32[]{:S(2)}) copy-start(s32[8,5]{1,0:T(8,128)} %param.12) | copy-start | bytes 484
  29.6 2.2 %collective-permute-start.7 = (bf16[2,19,16,512]{3,2,1,0:T(8,128)(2,1)S(1)}, bf16[2,19,16,512]{3,2,1,0:T(8,128)(2,1)S(1)}, u32[]{:S(2)}, u32[]{:S(2)}) collective-permute-start(bf16[2,19,16,512]{3,2,1,0:T(8,128)(2,1)S(1)} %shard_map.78.near1), channel_id=1, source_target_pairs={{1,0},{0,1},{3,2},{2,3},{5,4},{4,5},{7,6},{6,7},{9,8},{8,9},{11,10... | collective-permute-start | bytes 1867784 | tf_op jit(solution)/shard_map/ppermute | solution.py:37
  29.7 14.8 %collective-permute-start.8 = (f32[16,16,128]{2,1,0:T(8,128)S(1)}, f32[16,16,128]{2,1,0:T(8,128)S(1)}, u32[]{:S(2)}, u32[]{:S(2)}) collective-permute-start(f32[16,16,128]{2,1,0:T(8,128)S(1)} %pad_maximum_fusion.1), channel_id=1, source_target_pairs={{4,0},{5,1},{6,2},{7,3},{0,4},{1,5},{2,6},{3,7},{12,8},{13,9},{14,... | collective-permute-start | bytes 393224 | tf_op jit(solution)/shard_map/ppermute | solution.py:37
  29.8 16.4 %collective-permute-start.6 = (bf16[2,19,16,512]{3,2,1,0:T(8,128)(2,1)S(1)}, bf16[2,19,16,512]{3,2,1,0:T(8,128)(2,1)S(1)}, u32[]{:S(2)}, u32[]{:S(2)}) collective-permute-start(bf16[2,19,16,512]{3,2,1,0:T(8,128)(2,1)S(1)} %shard_map.78.near1), channel_id=1, source_target_pairs={{3,1},{0,2},{5,3},{2,4},{7,5},{4,6},{9,7},{6,8},{11,9},{8,10},{13,... | collective-permute-start | bytes 1867784 | tf_op jit(solution)/shard_map/ppermute | solution.py:37
  46.2 21.3 %copy-start = (bf16[8,1024,128]{2,1,0:T(8,128)(2,1)S(1)}, bf16[8,1024,128]{2,1,0:T(8,128)(2,1)}, u32[]{:S(2)}) copy-start(bf16[8,1024,128]{2,1,0:T(8,128)(2,1)} %basis.1) | copy-start | bytes 6291460
  46.2 21.3 %copy-start.3 = (f32[4,3,128,128]{3,2,1,0:T(8,128)S(1)}, f32[4,3,128,128]{3,2,1,0:T(8,128)}, u32[]{:S(2)}) copy-start(f32[4,3,128,128]{3,2,1,0:T(8,128)} %coupling.1) | copy-start | bytes 2359300
  46.3 21.3 %copy-start.4 = (f32[4,2,128,128]{3,2,1,0:T(8,128)S(1)}, f32[4,2,128,128]{3,2,1,0:T(8,128)}, u32[]{:S(2)}) copy-start(f32[4,2,128,128]{3,2,1,0:T(8,128)} %transfer.1) | copy-start | bytes 1572868
  46.3 21.3 %collective-permute-start.9 = (bf16[1,19,16,512]{3,2,1,0:T(8,128)(2,1)S(1)}, bf16[1,19,16,512]{3,2,1,0:T(8,128)(2,1)S(1)}, u32[]{:S(2)}, u32[]{:S(2)}) collective-permute-start(bf16[1,19,16,512]{3,2,1,0:T(8,128)(2,1)S(1)} %shard_map.80), channel_id=1, source_target_pairs={{1,0},{0,1},{3,2},{2,3},{5,4},{4,5},{7,6},{6,7},{9,8},{8,9},{11,10... | collective-permute-start | bytes 933896 | tf_op jit(solution)/shard_map/ppermute | solution.py:37

commit v6 on v5

--- a/solution.py
+++ b/solution.py
@@ -22,8 +22,9 @@
 VM = pl.BlockSpec(memory_space=pltpu.VMEM)
 SM = pl.BlockSpec(memory_space=pltpu.SMEM)
 SLOT_OFFSETS = (0, 1, -1, -2, 2, 3, -3, -4, 4)
-SELF = (1, 2, 8)
+SELF = (1, 3, 8)
 BITS = (0, 3, 4, 1, 2)
+EARLY = 3
 BUDGET = 12
 
 
@@ -130,30 +131,33 @@
 
 def add_block(i, w, tgt, vals, feats, acc):
     src = feats[w].astype(f32).T.astype(bf16)
-    for t in range(0, LEAF, 512):
-        dist_sq = jnp.dot(src, tgt[i, :, t : t + 512], preferred_element_type=f32)
-        kernel_vals = lax.rsqrt(dist_sq).astype(bf16)
-        acc[i, :, t : t + 512] += jnp.dot(vals[w], kernel_vals, preferred_element_type=f32)
+    dist_sq = jnp.dot(src, tgt[i], preferred_element_type=f32)
+    kernel_vals = lax.rsqrt(dist_sq).astype(bf16)
+    acc[i] += jnp.dot(vals[w], kernel_vals, preferred_element_type=f32)
 
 
 def add_listed(part, work, items, tgt, vals, feats, acc):
     def select(it, counts):
-        first, chosen = counts
+        early, first, chosen = counts
         i, k = it // (NB - 1), it % (NB - 1) + 1
         w = work[i, k]
-        in_first = (w < 6 * LEAVES_DEV) & (first < BUDGET)
+        in_early = (w < 2 * LEAVES_DEV) & (early < EARLY)
+        in_first = jnp.logical_not(in_early) & (w < 6 * LEAVES_DEV) & (first < BUDGET)
         in_last = w >= 8 * LEAVES_DEV
         in_part = (
+            in_early,
             in_first,
-            jnp.logical_not(in_first | in_last),
+            jnp.logical_not(in_early | in_first | in_last),
             in_last,
-        )[part - 1]
+        )[part]
         items[chosen] = i * 128 + w
-        return first + in_first.astype(jnp.int32), chosen + in_part.astype(jnp.int32)
-
-    _, count = lax.fori_loop(
-        0, LEAVES_DEV * (NB - 1), select, (jnp.int32(0), jnp.int32(0))
-    )
+        return (
+            early + in_early.astype(jnp.int32),
+            first + in_first.astype(jnp.int32),
+            chosen + in_part.astype(jnp.int32),
+        )
+
+    _, _, count = lax.fori_loop(0, LEAVES_DEV * (NB - 1), select, (jnp.int32(0),) * 3)
     base = 8 * LEAVES_DEV if part == 3 else 0
 
     def several(group):
@@ -171,15 +175,15 @@
 
 
 def own_blocks(first, last, tgt, vals, feats, acc):
-    group = 2 if (last - first) % 2 == 0 else 1
-
-    def some(n, carry):
-        for u in range(group):
-            i = first + n * group + u
+    def pair_of_blocks(n, carry):
+        for u in range(2):
+            i = first + n * 2 + u
             add_block(i, i, tgt, vals, feats, acc)
         return carry
 
-    lax.fori_loop(0, (last - first) // group, some, 0)
+    lax.fori_loop(0, (last - first) // 2, pair_of_blocks, 0)
+    if (last - first) % 2 == 1:
+        add_block(last - 1, last - 1, tgt, vals, feats, acc)
 
 
 def join(mine, theirs, joined):
@@ -201,6 +205,17 @@
 def own_kernel(step, tgt, vals, feats, mine, theirs, acc_in, acc, joined):
     join(mine, theirs, joined)
     own_blocks(SELF[step - 1], SELF[step], tgt, vals, feats, acc)
+
+
+def early_kernel(
+    place, work, pair, mine, theirs, acc_in, acc, joined, vals, feats, tmp, tgt, items
+):
+    join(mine, theirs, joined)
+    constant_rows(tmp, (6, 7, 8))
+    target_features(pair.at[0], tgt, tmp)
+    load_clusters([pair], place[1], vals, feats, tmp)
+    own_blocks(SELF[1], SELF[2], tgt, vals, feats, acc)
+    add_listed(0, work, items, tgt, vals, feats, acc)
 
 
 def load_clusters(pieces, sign, vals, feats, tmp):
@@ -401,14 +416,25 @@
         if step == 2:
             pair = gate(pair, recv)
             near1 = permuted(pair, lambda i: i - 1 if i % 2 == 0 else i + 1)
-        acc, coefs = staged(
-            functools.partial(own_kernel, step),
-            [],
-            [tgt, vals, feats, coefs, recv],
-            [acc],
-            [joined_shape(2 ** (step + 1))],
-            SELF[step] - SELF[step - 1],
-        )
+        if step == 1:
+            acc, coefs = staged(
+                functools.partial(own_kernel, step),
+                [],
+                [tgt, vals, feats, coefs, recv],
+                [acc],
+                [joined_shape(4)],
+                SELF[1] - SELF[0],
+            )
+        else:
+            acc, coefs = staged(
+                early_kernel,
+                [place, work],
+                [pair, coefs, recv],
+                [acc],
+                [joined_shape(8)],
+                SELF[2] - SELF[1] + EARLY,
+                window_scratch(2),
+            )
     recv = following
     near1 = gate(near1, acc, recv)
     near2 = permuted(near1, lambda i: i ^ 1)

time: 76.3 us -> 76.2 us (level)
  the two profiles are of different devices: /device:TPU:127 before, /device:TPU:129 now
where the time goes in v6:
time: 76.2 us; the launch traced here: 76.7 us
  Pallas kernels  50.7 us (67%)
  starting transfers between devices  22.4 us (29%)
  matrix products  2.08 us (3%)
  local copies, waits for them, and re-layouts  1.09 us (1%)
    pallas_call x6, Pallas kernels, staged(): pl.pallas_call(kernel, out_shape=tuple(state_shapes) + tuple(outs), in_sp...  49 us
    ppermute x10, starting transfers between devices, permuted(): return lax.ppermute(array, 'leaf', route)  22.4 us
    dot_general x1, matrix products, local(): jnp.dot(charges, leaf_basis.reshape(LEAVES_DEV * LEAF, RANK), preferred_e...  2.08 us
    pallas_call x1, Pallas kernels, pack(): pl.pallas_call(pack_kernel, out_shape=jax.ShapeDtypeStruct(PAYLOAD, bf16)...  1.75 us
  transfers between devices with their start and end apart: 10, of which 0 were waited for; matrix products, arithmetic and copies ran while one was open for 0% of the time, Pallas kernels for 57%

profile of v6, /device:TPU:129, one launch (start us, length us, event | category | flops | bytes accessed | tf_op | source)
XLA Modules:
  0.0 76.7 jit_solution(14566767423562352286)
XLA Ops:
  0.0 2.1 %convolution_bitcast_fusion.mine = f32[1,16,128]{2,1,0:T(8,128)S(1)} fusion(bf16[16,8192]{1,0:T(8,128)(2,1)} %charges_hbm.1, bf16[8192,128]{1,0:T(8,128)(2,1)} %bitcast.10), kind=kOutput, calls=%fused_computation | convolution fusion | flops 33554432 | bytes 2367488 | tf_op jit(solution)/shard_map/dot_general | solution.py:397
  2.1 0.8 collective-permute-start.1
  2.9 1.8 %shard_map.73.own = bf16[19,16,512]{2,1,0:T(8,128)(2,1)} custom-call(bf16[16,8192]{1,0:T(8,128)(2,1)} %charges_hbm.1, bf16[3,8192]{1,0:T(4,128)(2,1)} %points_hbm.1), custom_call_target="tpu_custom_call" | custom-call | flops 1000000 | bytes 1000000 | tf_op jit(solution)/shard_map/pallas_call | solution.py:63
  4.6 0.1 collective-permute-start
  4.8 0.1 pad_add_fusion.place
  4.8 0.0 collective-permute-done.1.theirs
  4.8 1.3 %collective-permute-start.2 = (f32[2,16,128]{2,1,0:T(8,128)S(1)}, f32[2,16,128]{2,1,0:T(8,128)S(1)}, u32[]{:S(2)}, u32[]{:S(2)}) collective-permute-start(f32[2,16,128]{2,1,0:T(8,128)S(1)} %pad_maximum_fusion.4), channel_id=1, source_target_pairs={{8,0},{9,1},{10,2},{11,3},{12,4},{13,5},{14,6},{15,7},{0,8},{1,9},... | collective-permute-start | bytes 49160 | tf_op jit(solution)/shard_map/ppermute | solution.py:38
  6.1 1.0 %copy-done.1 = bf16[19,16,512]{2,1,0:T(8,128)(2,1)S(1)} copy-done((bf16[19,16,512]{2,1,0:T(8,128)(2,1)S(1)}, bf16[19,16,512]{2,1,0:T(8,128)(2,1)}, u32[]{:S(2)}) %copy-start.1) | copy-done | bytes 311320
  7.1 1.8 %shard_map.74 = (f32[8,16,1024]{2,1,0:T(8,128)S(1)}, bf16[8,16,1024]{2,1,0:T(8,128)(2,1)S(1)}, bf16[8,16,1024]{2,1,0:T(8,128)(2,1)S(1)}, bf16[8,16,1024]{2,1,0:T(8,128)(2,1)S(1)}, f32[2,16,128]{2,1,0:T(8,128)S(1)}) custom-call(s32[2]{0:T(128)S(1)} %pad_add_fusion.place, bf16[19,16,512]{2,1,0:T(8,128)(2,1)S(1)} %copy-done.1, ...), custom_call_target="tpu_custom_call" | custom-call | flops 2000000000 | bytes 1000000 | tf_op jit(solution)/shard_map/pallas_call | solution.py:291
  8.9 0.0 collective-permute-done.2.theirs
  8.9 2.5 %collective-permute-start.3 = (f32[4,16,128]{2,1,0:T(8,128)S(1)}, f32[4,16,128]{2,1,0:T(8,128)S(1)}, u32[]{:S(2)}, u32[]{:S(2)}) collective-permute-start(f32[4,16,128]{2,1,0:T(8,128)S(1)} %pad_maximum_fusion.3), channel_id=1, source_target_pairs={{16,0},{17,1},{18,2},{19,3},{20,4},{21,5},{22,6},{23,7},{24,8},{25... | collective-permute-start | bytes 98312 | tf_op jit(solution)/shard_map/ppermute | solution.py:38
  11.5 1.8 %shard_map.76 = (f32[8,16,1024]{2,1,0:T(8,128)S(1)}, f32[4,16,128]{2,1,0:T(8,128)S(1)}) custom-call(bf16[8,16,1024]{2,1,0:T(8,128)(2,1)S(1)} %get-tuple-element.18.tgt, bf16[8,16,1024]{2,1,0:T(8,128)(2,1)S(1)} %get-tuple-element.19.vals, bf16[8,16,1024]{2,1,0:T(8,128)(2,1)S(1)} %get-tuple-element.20.feats, ...), custom_call_target="tpu_custom_call", output_to_operand_aliasing={{0}: (5, {})} | custom-call | flops 2000000000 | bytes 1000000 | tf_op jit(solution)/shard_map/pallas_call | solution.py:291
  13.3 0.0 collective-permute-done.3.refs_1_.theirs
  13.3 1.4 %collective-permute-start.5 = (f32[8,16,128]{2,1,0:T(8,128)S(1)}, f32[8,16,128]{2,1,0:T(8,128)S(1)}, u32[]{:S(2)}, u32[]{:S(2)}) collective-permute-start(f32[8,16,128]{2,1,0:T(8,128)S(1)} %pad_maximum_fusion.2), channel_id=1, source_target_pairs={{2,0},{3,1},{0,2},{1,3},{6,4},{7,5},{4,6},{5,7},{10,8},{11,9},{8,1... | collective-permute-start | bytes 196616 | tf_op jit(solution)/shard_map/ppermute | solution.py:38
  14.7 0.1 pad_maximum_fusion.refs_0_
  14.8 4.0 %collective-permute-start.4 = (bf16[2,19,16,512]{3,2,1,0:T(8,128)(2,1)S(1)}, bf16[2,19,16,512]{3,2,1,0:T(8,128)(2,1)S(1)}, u32[]{:S(2)}, u32[]{:S(2)}) collective-permute-start(bf16[2,19,16,512]{3,2,1,0:T(8,128)(2,1)S(1)} %shard_map.75.pair), channel_id=1, source_target_pairs={{2,1},{1,2},{4,3},{3,4},{6,5},{5,6},{8,7},{7,8},{10,9},{9,10},{12,... | collective-permute-start | bytes 1867784 | tf_op jit(solution)/shard_map/ppermute | solution.py:38
  18.8 0.0 copy-start.6
  18.8 9.3 %shard_map.77 = (f32[8,16,1024]{2,1,0:T(8,128)S(1)}, f32[8,16,128]{2,1,0:T(8,128)S(1)}) custom-call(s32[2]{0:T(128)S(1)} %pad_add_fusion.place, s32[8,5]{1,0:T(8,128)S(1)} %fusion.2.work, bf16[2,19,16,512]{3,2,1,0:T(8,128)(2,1)S(1)} %shard_map.75.pair, f32[4,16,128]{2,1,0:T(8,128)S(1)} %get-tuple-element.22.mine, ...), custom_call_target="tpu_custom_call", output_to_operand_aliasing={{0}: (5, {})} | custom-call | flops 8000000000 | bytes 1000000 | tf_op jit(solution)/shard_map/pallas_call | solution.py:291
  28.1 0.0 collective-permute-done.4.refs_0_
  28.1 5.7 %collective-permute-start.7 = (bf16[2,19,16,512]{3,2,1,0:T(8,128)(2,1)S(1)}, bf16[2,19,16,512]{3,2,1,0:T(8,128)(2,1)S(1)}, u32[]{:S(2)}, u32[]{:S(2)}) collective-permute-start(bf16[2,19,16,512]{3,2,1,0:T(8,128)(2,1)S(1)} %shard_map.78.near1), channel_id=1, source_target_pairs={{1,0},{0,1},{3,2},{2,3},{5,4},{4,5},{7,6},{6,7},{9,8},{8,9},{11,10... | collective-permute-start | bytes 1867784 | tf_op jit(solution)/shard_map/ppermute | solution.py:38
  33.8 0.1 copy.15
  33.9 0.1 collective-permute-start.8
  34.0 3.0 %collective-permute-start.6 = (bf16[2,19,16,512]{3,2,1,0:T(8,128)(2,1)S(1)}, bf16[2,19,16,512]{3,2,1,0:T(8,128)(2,1)S(1)}, u32[]{:S(2)}, u32[]{:S(2)}) collective-permute-start(bf16[2,19,16,512]{3,2,1,0:T(8,128)(2,1)S(1)} %shard_map.78.near1), channel_id=1, source_target_pairs={{3,1},{0,2},{5,3},{2,4},{7,5},{4,6},{9,7},{6,8},{11,9},{8,10},{13,... | collective-permute-start | bytes 1867784 | tf_op jit(solution)/shard_map/ppermute | solution.py:38
  37.1 11.1 %shard_map.79 = (f32[8,16,1024]{2,1,0:T(8,128)S(1)}, f32[16,16,128]{2,1,0:T(8,128)S(1)}) custom-call(s32[2]{0:T(128)S(1)} %pad_add_fusion.place, s32[8,5]{1,0:T(8,128)S(1)} %fusion.2.work, bf16[2,19,16,512]{3,2,1,0:T(8,128)(2,1)S(1)} %shard_map.75.pair, bf16[2,19,16,512]{3,2,1,0:T(8,128)(2,1)S(1)} %shard_map.78.near1, ...), custom_call_target="tpu_custom_call", output_to_operand_aliasing={{0}: (7, {})} | custom-call | flops 12000000000 | bytes 1000000 | tf_op jit(solution)/shard_map/pallas_call | solution.py:291
  48.2 0.0 collective-permute-done.6.array.far1
  48.2 0.0 copy-start
  48.2 0.0 copy-start.3
  48.2 0.0 copy-start.4
  48.3 3.5 %collective-permute-start.9 = (bf16[1,19,16,512]{3,2,1,0:T(8,128)(2,1)S(1)}, bf16[1,19,16,512]{3,2,1,0:T(8,128)(2,1)S(1)}, u32[]{:S(2)}, u32[]{:S(2)}) collective-permute-start(bf16[1,19,16,512]{3,2,1,0:T(8,128)(2,1)S(1)} %shard_map.80), channel_id=1, source_target_pairs={{1,0},{0,1},{3,2},{2,3},{5,4},{4,5},{7,6},{6,7},{9,8},{8,9},{11,10... | collective-permute-start | bytes 933896 | tf_op jit(solution)/shard_map/ppermute | solution.py:38
  51.7 17.6 %shard_map.81.acc_in = f32[8,16,1024]{2,1,0:T(8,128)S(1)} custom-call(s32[2]{0:T(128)S(1)} %pad_add_fusion.place, s32[8,5]{1,0:T(8,128)S(1)} %fusion.2.work, bf16[2,19,16,512]{3,2,1,0:T(8,128)(2,1)S(1)} %shard_map.75.pair, bf16[2,19,16,512]{3,2,1,0:T(8,128)(2,1)S(1)} %shard_map.78.near1, ...), custom_call_target="tpu_custom_call", output_to_operand_aliasing={{}: (6, {})} | custom-call | flops 20000000000 | bytes 1000000 | tf_op jit(solution)/shard_map/pallas_call | solution.py:291
  69.3 0.0 copy-done
  69.4 7.3 %shard_map.82 = (f32[8,16,1024]{2,1,0:T(8,128)S(1)}, bf16[16,8192]{1,0:T(8,128)(2,1)}) custom-call(s32[2]{0:T(128)S(1)} %pad_add_fusion.place, s32[8,5]{1,0:T(8,128)S(1)} %fusion.2.work, s32[4,3]{1,0:T(4,128)S(1)} %bitcast.12, bf16[2,19,16,512]{3,2,1,0:T(8,128)(2,1)S(1)} %shard_map.75.pair, ...), custom_call_target="tpu_custom_call", output_to_operand_aliasing={{0}: (10, {})} | custom-call | flops 3000000000 | bytes 1000000 | tf_op jit(solution)/shard_map/pallas_call | solution.py:291
  (21 shorter events, 0.1 us)
Async XLA Ops:
  0.0 4.7 %copy-start.5 = (s32[8,5]{1,0:T(8,128)S(1)}, s32[8,5]{1,0:T(8,128)}, u32[]{:S(2)}) copy-start(s32[8,5]{1,0:T(8,128)} %param.12) | copy-start | bytes 484
  2.1 2.8 %collective-permute-start.1 = (f32[1,16,128]{2,1,0:T(8,128)S(1)}, f32[1,16,128]{2,1,0:T(8,128)S(1)}, u32[]{:S(2)}, u32[]{:S(2)}) collective-permute-start(f32[1,16,128]{2,1,0:T(8,128)S(1)} %convolution_bitcast_fusion.mine), channel_id=1, source_target_pairs={{1,0},{0,1},{3,2},{2,3},{5,4},{4,5},{7,6},{6,7},{9,8},{8,9},{11,10... | collective-permute-start | bytes 24584 | tf_op jit(solution)/shard_map/ppermute | solution.py:38
  4.6 10.1 %collective-permute-start = (bf16[19,16,512]{2,1,0:T(8,128)(2,1)}, bf16[19,16,512]{2,1,0:T(8,128)(2,1)S(1)}, u32[]{:S(2)}, u32[]{:S(2)}) collective-permute-start(bf16[19,16,512]{2,1,0:T(8,128)(2,1)} %shard_map.73.own), channel_id=1, source_target_pairs={{1,0},{0,1},{3,2},{2,3},{5,4},{4,5},{7,6},{6,7},{9,8},{8,9},{11,10... | collective-permute-start | bytes 933896 | tf_op jit(solution)/shard_map/ppermute | solution.py:38
  4.8 4.1 %collective-permute-start.2 = (f32[2,16,128]{2,1,0:T(8,128)S(1)}, f32[2,16,128]{2,1,0:T(8,128)S(1)}, u32[]{:S(2)}, u32[]{:S(2)}) collective-permute-start(f32[2,16,128]{2,1,0:T(8,128)S(1)} %pad_maximum_fusion.4), channel_id=1, source_target_pairs={{8,0},{9,1},{10,2},{11,3},{12,4},{13,5},{14,6},{15,7},{0,8},{1,9},... | collective-permute-start | bytes 49160 | tf_op jit(solution)/shard_map/ppermute | solution.py:38
  6.1 1.0 %copy-start.1 = (bf16[19,16,512]{2,1,0:T(8,128)(2,1)S(1)}, bf16[19,16,512]{2,1,0:T(8,128)(2,1)}, u32[]{:S(2)}) copy-start(bf16[19,16,512]{2,1,0:T(8,128)(2,1)} %shard_map.73.own) | copy-start | bytes 933892
  8.9 4.4 %collective-permute-start.3 = (f32[4,16,128]{2,1,0:T(8,128)S(1)}, f32[4,16,128]{2,1,0:T(8,128)S(1)}, u32[]{:S(2)}, u32[]{:S(2)}) collective-permute-start(f32[4,16,128]{2,1,0:T(8,128)S(1)} %pad_maximum_fusion.3), channel_id=1, source_target_pairs={{16,0},{17,1},{18,2},{19,3},{20,4},{21,5},{22,6},{23,7},{24,8},{25... | collective-permute-start | bytes 98312 | tf_op jit(solution)/shard_map/ppermute | solution.py:38
  11.4 3.3 %copy-start.2 = (bf16[19,16,512]{2,1,0:T(8,128)(2,1)S(1)}, bf16[19,16,512]{2,1,0:T(8,128)(2,1)}, u32[]{:S(2)}) copy-start(bf16[19,16,512]{2,1,0:T(8,128)(2,1)} %shard_map.73.own) | copy-start | bytes 933892
  13.3 14.8 %collective-permute-start.5 = (f32[8,16,128]{2,1,0:T(8,128)S(1)}, f32[8,16,128]{2,1,0:T(8,128)S(1)}, u32[]{:S(2)}, u32[]{:S(2)}) collective-permute-start(f32[8,16,128]{2,1,0:T(8,128)S(1)} %pad_maximum_fusion.2), channel_id=1, source_target_pairs={{2,0},{3,1},{0,2},{1,3},{6,4},{7,5},{4,6},{5,7},{10,8},{11,9},{8,1... | collective-permute-start | bytes 196616 | tf_op jit(solution)/shard_map/ppermute | solution.py:38
  14.8 13.3 %collective-permute-start.4 = (bf16[2,19,16,512]{3,2,1,0:T(8,128)(2,1)S(1)}, bf16[2,19,16,512]{3,2,1,0:T(8,128)(2,1)S(1)}, u32[]{:S(2)}, u32[]{:S(2)}) collective-permute-start(bf16[2,19,16,512]{3,2,1,0:T(8,128)(2,1)S(1)} %shard_map.75.pair), channel_id=1, source_target_pairs={{2,1},{1,2},{4,3},{3,4},{6,5},{5,6},{8,7},{7,8},{10,9},{9,10},{12,... | collective-permute-start | bytes 1867784 | tf_op jit(solution)/shard_map/ppermute | solution.py:38
  18.8 15.0 %copy-start.6 = (s32[1,4,3]{1,0,2:T(1,128)S(1)}, s32[1,4,3]{1,0,2:T(1,128)}, u32[]{:S(2)}) copy-start(s32[1,4,3]{1,0,2:T(1,128)} %param.13) | copy-start | bytes 148
  28.1 9.0 %collective-permute-start.7 = (bf16[2,19,16,512]{3,2,1,0:T(8,128)(2,1)S(1)}, bf16[2,19,16,512]{3,2,1,0:T(8,128)(2,1)S(1)}, u32[]{:S(2)}, u32[]{:S(2)}) collective-permute-start(bf16[2,19,16,512]{3,2,1,0:T(8,128)(2,1)S(1)} %shard_map.78.near1), channel_id=1, source_target_pairs={{1,0},{0,1},{3,2},{2,3},{5,4},{4,5},{7,6},{6,7},{9,8},{8,9},{11,10... | collective-permute-start | bytes 1867784 | tf_op jit(solution)/shard_map/ppermute | solution.py:38
  33.9 14.2 %collective-permute-start.8 = (f32[16,16,128]{2,1,0:T(8,128)S(1)}, f32[16,16,128]{2,1,0:T(8,128)S(1)}, u32[]{:S(2)}, u32[]{:S(2)}) collective-permute-start(f32[16,16,128]{2,1,0:T(8,128)S(1)} %pad_maximum_fusion.1), channel_id=1, source_target_pairs={{4,0},{5,1},{6,2},{7,3},{0,4},{1,5},{2,6},{3,7},{12,8},{13,9},{14,... | collective-permute-start | bytes 393224 | tf_op jit(solution)/shard_map/ppermute | solution.py:38
  34.0 14.2 %collective-permute-start.6 = (bf16[2,19,16,512]{3,2,1,0:T(8,128)(2,1)S(1)}, bf16[2,19,16,512]{3,2,1,0:T(8,128)(2,1)S(1)}, u32[]{:S(2)}, u32[]{:S(2)}) collective-permute-start(bf16[2,19,16,512]{3,2,1,0:T(8,128)(2,1)S(1)} %shard_map.78.near1), channel_id=1, source_target_pairs={{3,1},{0,2},{5,3},{2,4},{7,5},{4,6},{9,7},{6,8},{11,9},{8,10},{13,... | collective-permute-start | bytes 1867784 | tf_op jit(solution)/shard_map/ppermute | solution.py:38
  48.2 21.1 %copy-start = (bf16[8,1024,128]{2,1,0:T(8,128)(2,1)S(1)}, bf16[8,1024,128]{2,1,0:T(8,128)(2,1)}, u32[]{:S(2)}) copy-start(bf16[8,1024,128]{2,1,0:T(8,128)(2,1)} %basis.1) | copy-start | bytes 6291460
  48.2 21.1 %copy-start.3 = (f32[4,3,128,128]{3,2,1,0:T(8,128)S(1)}, f32[4,3,128,128]{3,2,1,0:T(8,128)}, u32[]{:S(2)}) copy-start(f32[4,3,128,128]{3,2,1,0:T(8,128)} %coupling.1) | copy-start | bytes 2359300
  48.2 21.1 %copy-start.4 = (f32[4,2,128,128]{3,2,1,0:T(8,128)S(1)}, f32[4,2,128,128]{3,2,1,0:T(8,128)}, u32[]{:S(2)}) copy-start(f32[4,2,128,128]{3,2,1,0:T(8,128)} %transfer.1) | copy-start | bytes 1572868
  48.3 21.1 %collective-permute-start.9 = (bf16[1,19,16,512]{3,2,1,0:T(8,128)(2,1)S(1)}, bf16[1,19,16,512]{3,2,1,0:T(8,128)(2,1)S(1)}, u32[]{:S(2)}, u32[]{:S(2)}) collective-permute-start(bf16[1,19,16,512]{3,2,1,0:T(8,128)(2,1)S(1)} %shard_map.80), channel_id=1, source_target_pairs={{1,0},{0,1},{3,2},{2,3},{5,4},{4,5},{7,6},{6,7},{9,8},{8,9},{11,10... | collective-permute-start | bytes 933896 | tf_op jit(solution)/shard_map/ppermute | solution.py:38

commit v7 on v6

--- a/solution.py
+++ b/solution.py
@@ -38,12 +38,9 @@
     return lax.ppermute(array, "leaf", route)
 
 
-def pack_kernel(charges_hbm, points_hbm, out, charges, points, rows, sems):
-    get_points = pltpu.make_async_copy(points_hbm, points, sems.at[0])
-    get_charges = pltpu.make_async_copy(charges_hbm, charges, sems.at[1])
-    get_points.start()
-    get_charges.start()
-    get_points.wait()
+def pack_kernel(charges, points, out, rows):
+    for k in range(16):
+        out[k] = charges[:, k * HALF : (k + 1) * HALF]
     for l in range(LEAVES_DEV):
         for h in range(2):
             start = l * LEAF + h * HALF
@@ -53,25 +50,16 @@
                 rows[row : row + 1, :] = part[c : c + 1]
     for k in range(3):
         out[16 + k] = rows[k * 16 : (k + 1) * 16, :].astype(bf16)
-    get_charges.wait()
-    for k in range(16):
-        out[k] = charges[:, k * HALF : (k + 1) * HALF]
 
 
 def pack(charges, points):
-    anywhere = pl.BlockSpec(memory_space=pl.ANY)
     return pl.pallas_call(
         pack_kernel,
         out_shape=jax.ShapeDtypeStruct(PAYLOAD, bf16),
-        in_specs=[anywhere] * 2,
+        in_specs=[VM, VM],
         out_specs=VM,
-        scratch_shapes=[
-            pltpu.VMEM(charges.shape, bf16),
-            pltpu.VMEM(points.shape, bf16),
-            pltpu.VMEM((48, HALF), f32),
-            pltpu.SemaphoreType.DMA((2,)),
-        ],
-        compiler_params=params(60),
+        scratch_shapes=[pltpu.VMEM((48, HALF), f32)],
+        compiler_params=params(4),
         cost_estimate=pl.CostEstimate(flops=10**6, bytes_accessed=10**6, transcendentals=0),
     )(charges, points)
 

time: 76.2 us -> 73.3 us (0.962)
  the two profiles are of different devices: /device:TPU:129 before, /device:TPU:127 now
where the time goes in v7:
time: 73.3 us; the launch traced here: 72.9 us
  Pallas kernels  49.1 us (67%)
  starting transfers between devices  17.8 us (24%)
  waiting for transfers between devices  3.49 us (5%)
  matrix products  2.1 us (3%)
    pallas_call x6, Pallas kernels, staged(): pl.pallas_call(kernel, out_shape=tuple(state_shapes) + tuple(outs), in_sp...  49 us
    ppermute x10, starting transfers between devices, permuted(): return lax.ppermute(array, 'leaf', route)  17.8 us
    ppermute x10, waiting for transfers between devices, permuted(): return lax.ppermute(array, 'leaf', route)  3.49 us
    dot_general x1, matrix products, local(): jnp.dot(charges, leaf_basis.reshape(LEAVES_DEV * LEAF, RANK), preferred_e...  2.1 us
  transfers between devices with their start and end apart: 10, of which 4 were waited for; matrix products, arithmetic and copies ran while one was open for 0% of the time, Pallas kernels for 57%

profile of v7, /device:TPU:127, one launch (start us, length us, event | category | flops | bytes accessed | tf_op | source)
XLA Modules:
  0.0 72.9 jit_solution(6949899237267196773)
XLA Ops:
  0.0 2.1 %convolution_bitcast_fusion.mine = f32[1,16,128]{2,1,0:T(8,128)S(1)} fusion(bf16[16,8192]{1,0:T(8,128)(2,1)} %charges.1, bf16[8192,128]{1,0:T(8,128)(2,1)} %bitcast.10), kind=kOutput, calls=%fused_computation | convolution fusion | flops 33554432 | bytes 2367488 | tf_op jit(solution)/shard_map/dot_general | solution.py:385
  2.1 0.8 %collective-permute-start.1 = (f32[1,16,128]{2,1,0:T(8,128)S(1)}, f32[1,16,128]{2,1,0:T(8,128)S(1)}, u32[]{:S(2)}, u32[]{:S(2)}) collective-permute-start(f32[1,16,128]{2,1,0:T(8,128)S(1)} %convolution_bitcast_fusion.mine), channel_id=1, source_target_pairs={{1,0},{0,1},{3,2},{2,3},{5,4},{4,5},{7,6},{6,7},{9,8},{8,9},{11,10... | collective-permute-start | bytes 24584 | tf_op jit(solution)/shard_map/ppermute | solution.py:38
  2.9 0.1 collective-permute-start
  3.1 0.1 pad_add_fusion.place
  3.2 0.5 collective-permute-done.1.theirs
  3.7 0.5 collective-permute-start.2
  4.3 1.8 %shard_map.74 = (f32[8,16,1024]{2,1,0:T(8,128)S(1)}, bf16[8,16,1024]{2,1,0:T(8,128)(2,1)S(1)}, bf16[8,16,1024]{2,1,0:T(8,128)(2,1)S(1)}, bf16[8,16,1024]{2,1,0:T(8,128)(2,1)S(1)}, f32[2,16,128]{2,1,0:T(8,128)S(1)}) custom-call(s32[2]{0:T(128)S(1)} %pad_add_fusion.place, bf16[19,16,512]{2,1,0:T(8,128)(2,1)S(1)} %shard_map.73.own, ...), custom_call_target="tpu_custom_call" | custom-call | flops 2000000000 | bytes 1000000 | tf_op jit(solution)/shard_map/pallas_call | solution.py:279
  6.1 0.2 collective-permute-done.2.theirs
  6.3 1.1 %collective-permute-start.3 = (f32[4,16,128]{2,1,0:T(8,128)S(1)}, f32[4,16,128]{2,1,0:T(8,128)S(1)}, u32[]{:S(2)}, u32[]{:S(2)}) collective-permute-start(f32[4,16,128]{2,1,0:T(8,128)S(1)} %pad_maximum_fusion.3), channel_id=1, source_target_pairs={{16,0},{17,1},{18,2},{19,3},{20,4},{21,5},{22,6},{23,7},{24,8},{25... | collective-permute-start | bytes 98312 | tf_op jit(solution)/shard_map/ppermute | solution.py:38
  7.4 1.8 %shard_map.76 = (f32[8,16,1024]{2,1,0:T(8,128)S(1)}, f32[4,16,128]{2,1,0:T(8,128)S(1)}) custom-call(bf16[8,16,1024]{2,1,0:T(8,128)(2,1)S(1)} %get-tuple-element.18.tgt, bf16[8,16,1024]{2,1,0:T(8,128)(2,1)S(1)} %get-tuple-element.19.vals, bf16[8,16,1024]{2,1,0:T(8,128)(2,1)S(1)} %get-tuple-element.20.feats, ...), custom_call_target="tpu_custom_call", output_to_operand_aliasing={{0}: (5, {})} | custom-call | flops 2000000000 | bytes 1000000 | tf_op jit(solution)/shard_map/pallas_call | solution.py:279
  9.3 1.3 %collective-permute-done.3.refs_1_.theirs = f32[4,16,128]{2,1,0:T(8,128)S(1)} collective-permute-done((f32[4,16,128]{2,1,0:T(8,128)S(1)}, f32[4,16,128]{2,1,0:T(8,128)S(1)}, u32[]{:S(2)}, u32[]{:S(2)}) %collective-permute-start.3) | collective-permute-done | bytes 32800 | tf_op jit(solution)/shard_map/ppermute | solution.py:38
  10.6 0.5 collective-permute-start.5
  11.0 0.0 collective-permute-done
  11.1 0.1 pad_maximum_fusion.refs_0_
  11.1 8.0 %collective-permute-start.4 = (bf16[2,19,16,512]{3,2,1,0:T(8,128)(2,1)S(1)}, bf16[2,19,16,512]{3,2,1,0:T(8,128)(2,1)S(1)}, u32[]{:S(2)}, u32[]{:S(2)}) collective-permute-start(bf16[2,19,16,512]{3,2,1,0:T(8,128)(2,1)S(1)} %shard_map.75.pair), channel_id=1, source_target_pairs={{2,1},{1,2},{4,3},{3,4},{6,5},{5,6},{8,7},{7,8},{10,9},{9,10},{12,... | collective-permute-start | bytes 1867784 | tf_op jit(solution)/shard_map/ppermute | solution.py:38
  19.1 0.0 copy-start.6
  19.1 9.3 %shard_map.77 = (f32[8,16,1024]{2,1,0:T(8,128)S(1)}, f32[8,16,128]{2,1,0:T(8,128)S(1)}) custom-call(s32[2]{0:T(128)S(1)} %pad_add_fusion.place, s32[8,5]{1,0:T(8,128)S(1)} %fusion.2.work, bf16[2,19,16,512]{3,2,1,0:T(8,128)(2,1)S(1)} %shard_map.75.pair, f32[4,16,128]{2,1,0:T(8,128)S(1)} %get-tuple-element.22.mine, ...), custom_call_target="tpu_custom_call", output_to_operand_aliasing={{0}: (5, {})} | custom-call | flops 8000000000 | bytes 1000000 | tf_op jit(solution)/shard_map/pallas_call | solution.py:279
  28.4 0.0 collective-permute-done.5.refs_2_.theirs
  28.4 0.0 collective-permute-done.4.refs_0_
  28.4 0.1 collective-permute-start.7
  28.5 0.1 copy.15
  28.6 0.1 collective-permute-start.8
  28.7 2.4 %collective-permute-start.6 = (bf16[2,19,16,512]{3,2,1,0:T(8,128)(2,1)S(1)}, bf16[2,19,16,512]{3,2,1,0:T(8,128)(2,1)S(1)}, u32[]{:S(2)}, u32[]{:S(2)}) collective-permute-start(bf16[2,19,16,512]{3,2,1,0:T(8,128)(2,1)S(1)} %shard_map.78.near1), channel_id=1, source_target_pairs={{3,1},{0,2},{5,3},{2,4},{7,5},{4,6},{9,7},{6,8},{11,9},{8,10},{13,... | collective-permute-start | bytes 1867784 | tf_op jit(solution)/shard_map/ppermute | solution.py:38
  31.2 12.6 %shard_map.79 = (f32[8,16,1024]{2,1,0:T(8,128)S(1)}, f32[16,16,128]{2,1,0:T(8,128)S(1)}) custom-call(s32[2]{0:T(128)S(1)} %pad_add_fusion.place, s32[8,5]{1,0:T(8,128)S(1)} %fusion.2.work, bf16[2,19,16,512]{3,2,1,0:T(8,128)(2,1)S(1)} %shard_map.75.pair, bf16[2,19,16,512]{3,2,1,0:T(8,128)(2,1)S(1)} %shard_map.78.near1, ...), custom_call_target="tpu_custom_call", output_to_operand_aliasing={{0}: (7, {})} | custom-call | flops 12000000000 | bytes 1000000 | tf_op jit(solution)/shard_map/pallas_call | solution.py:279
  43.7 1.4 %collective-permute-done.6.array.far1 = bf16[2,19,16,512]{3,2,1,0:T(8,128)(2,1)S(1)} collective-permute-done((bf16[2,19,16,512]{3,2,1,0:T(8,128)(2,1)S(1)}, bf16[2,19,16,512]{3,2,1,0:T(8,128)(2,1)S(1)}, u32[]{:S(2)}, u32[]{:S(2)}) %collective-permute-start.6) | collective-permute-done | bytes 622624 | tf_op jit(solution)/shard_map/ppermute | solution.py:38
  45.2 0.0 copy-start
  45.2 0.0 copy-start.3
  45.2 0.0 copy-start.4
  45.2 4.2 %collective-permute-start.9 = (bf16[1,19,16,512]{3,2,1,0:T(8,128)(2,1)S(1)}, bf16[1,19,16,512]{3,2,1,0:T(8,128)(2,1)S(1)}, u32[]{:S(2)}, u32[]{:S(2)}) collective-permute-start(bf16[1,19,16,512]{3,2,1,0:T(8,128)(2,1)S(1)} %shard_map.80), channel_id=1, source_target_pairs={{1,0},{0,1},{3,2},{2,3},{5,4},{4,5},{7,6},{6,7},{9,8},{8,9},{11,10... | collective-permute-start | bytes 933896 | tf_op jit(solution)/shard_map/ppermute | solution.py:38
  49.4 16.1 %shard_map.81.acc_in = f32[8,16,1024]{2,1,0:T(8,128)S(1)} custom-call(s32[2]{0:T(128)S(1)} %pad_add_fusion.place, s32[8,5]{1,0:T(8,128)S(1)} %fusion.2.work, bf16[2,19,16,512]{3,2,1,0:T(8,128)(2,1)S(1)} %shard_map.75.pair, bf16[2,19,16,512]{3,2,1,0:T(8,128)(2,1)S(1)} %shard_map.78.near1, ...), custom_call_target="tpu_custom_call", output_to_operand_aliasing={{}: (6, {})} | custom-call | flops 20000000000 | bytes 1000000 | tf_op jit(solution)/shard_map/pallas_call | solution.py:279
  65.6 0.0 copy-done
  65.6 7.3 %shard_map.82 = (f32[8,16,1024]{2,1,0:T(8,128)S(1)}, bf16[16,8192]{1,0:T(8,128)(2,1)}) custom-call(s32[2]{0:T(128)S(1)} %pad_add_fusion.place, s32[8,5]{1,0:T(8,128)S(1)} %fusion.2.work, s32[4,3]{1,0:T(4,128)S(1)} %bitcast.12, bf16[2,19,16,512]{3,2,1,0:T(8,128)(2,1)S(1)} %shard_map.75.pair, ...), custom_call_target="tpu_custom_call", output_to_operand_aliasing={{0}: (10, {})} | custom-call | flops 3000000000 | bytes 1000000 | tf_op jit(solution)/shard_map/pallas_call | solution.py:279
  (21 shorter events, 0.1 us)
Async XLA Ops:
  0.0 2.9 %copy-start.1 = (bf16[16,8192]{1,0:T(8,128)(2,1)S(1)}, bf16[16,8192]{1,0:T(8,128)(2,1)}, u32[]{:S(2)}) copy-start(bf16[16,8192]{1,0:T(8,128)(2,1)} %charges.1) | copy-start | bytes 786436
  0.0 2.9 %copy-start.2 = (bf16[3,8192]{1,0:T(4,128)(2,1)S(1)}, bf16[3,8192]{1,0:T(4,128)(2,1)}, u32[]{:S(2)}) copy-start(bf16[3,8192]{1,0:T(4,128)(2,1)} %points.1) | copy-start | bytes 147460
  0.0 3.1 %copy-start.5 = (s32[8,5]{1,0:T(8,128)S(1)}, s32[8,5]{1,0:T(8,128)}, u32[]{:S(2)}) copy-start(s32[8,5]{1,0:T(8,128)} %param.12) | copy-start | bytes 484
  2.1 1.6 %collective-permute-start.1 = (f32[1,16,128]{2,1,0:T(8,128)S(1)}, f32[1,16,128]{2,1,0:T(8,128)S(1)}, u32[]{:S(2)}, u32[]{:S(2)}) collective-permute-start(f32[1,16,128]{2,1,0:T(8,128)S(1)} %convolution_bitcast_fusion.mine), channel_id=1, source_target_pairs={{1,0},{0,1},{3,2},{2,3},{5,4},{4,5},{7,6},{6,7},{9,8},{8,9},{11,10... | collective-permute-start | bytes 24584 | tf_op jit(solution)/shard_map/ppermute | solution.py:38
  2.9 8.1 %collective-permute-start = (bf16[19,16,512]{2,1,0:T(8,128)(2,1)S(1)}, bf16[19,16,512]{2,1,0:T(8,128)(2,1)S(1)}, u32[]{:S(2)}, u32[]{:S(2)}) collective-permute-start(bf16[19,16,512]{2,1,0:T(8,128)(2,1)S(1)} %shard_map.73.own), channel_id=1, source_target_pairs={{1,0},{0,1},{3,2},{2,3},{5,4},{4,5},{7,6},{6,7},{9,8},{8,9},{11,10... | collective-permute-start | bytes 933896 | tf_op jit(solution)/shard_map/ppermute | solution.py:38
  3.7 2.6 %collective-permute-start.2 = (f32[2,16,128]{2,1,0:T(8,128)S(1)}, f32[2,16,128]{2,1,0:T(8,128)S(1)}, u32[]{:S(2)}, u32[]{:S(2)}) collective-permute-start(f32[2,16,128]{2,1,0:T(8,128)S(1)} %pad_maximum_fusion.4), channel_id=1, source_target_pairs={{8,0},{9,1},{10,2},{11,3},{12,4},{13,5},{14,6},{15,7},{0,8},{1,9},... | collective-permute-start | bytes 49160 | tf_op jit(solution)/shard_map/ppermute | solution.py:38
  6.3 4.3 %collective-permute-start.3 = (f32[4,16,128]{2,1,0:T(8,128)S(1)}, f32[4,16,128]{2,1,0:T(8,128)S(1)}, u32[]{:S(2)}, u32[]{:S(2)}) collective-permute-start(f32[4,16,128]{2,1,0:T(8,128)S(1)} %pad_maximum_fusion.3), channel_id=1, source_target_pairs={{16,0},{17,1},{18,2},{19,3},{20,4},{21,5},{22,6},{23,7},{24,8},{25... | collective-permute-start | bytes 98312 | tf_op jit(solution)/shard_map/ppermute | solution.py:38
  10.6 17.8 %collective-permute-start.5 = (f32[8,16,128]{2,1,0:T(8,128)S(1)}, f32[8,16,128]{2,1,0:T(8,128)S(1)}, u32[]{:S(2)}, u32[]{:S(2)}) collective-permute-start(f32[8,16,128]{2,1,0:T(8,128)S(1)} %pad_maximum_fusion.2), channel_id=1, source_target_pairs={{2,0},{3,1},{0,2},{1,3},{6,4},{7,5},{4,6},{5,7},{10,8},{11,9},{8,1... | collective-permute-start | bytes 196616 | tf_op jit(solution)/shard_map/ppermute | solution.py:38
  11.1 17.3 %collective-permute-start.4 = (bf16[2,19,16,512]{3,2,1,0:T(8,128)(2,1)S(1)}, bf16[2,19,16,512]{3,2,1,0:T(8,128)(2,1)S(1)}, u32[]{:S(2)}, u32[]{:S(2)}) collective-permute-start(bf16[2,19,16,512]{3,2,1,0:T(8,128)(2,1)S(1)} %shard_map.75.pair), channel_id=1, source_target_pairs={{2,1},{1,2},{4,3},{3,4},{6,5},{5,6},{8,7},{7,8},{10,9},{9,10},{12,... | collective-permute-start | bytes 1867784 | tf_op jit(solution)/shard_map/ppermute | solution.py:38
  19.1 9.4 %copy-start.6 = (s32[1,4,3]{1,0,2:T(1,128)S(1)}, s32[1,4,3]{1,0,2:T(1,128)}, u32[]{:S(2)}) copy-start(s32[1,4,3]{1,0,2:T(1,128)} %param.13) | copy-start | bytes 148
  28.4 2.7 %collective-permute-start.7 = (bf16[2,19,16,512]{3,2,1,0:T(8,128)(2,1)S(1)}, bf16[2,19,16,512]{3,2,1,0:T(8,128)(2,1)S(1)}, u32[]{:S(2)}, u32[]{:S(2)}) collective-permute-start(bf16[2,19,16,512]{3,2,1,0:T(8,128)(2,1)S(1)} %shard_map.78.near1), channel_id=1, source_target_pairs={{1,0},{0,1},{3,2},{2,3},{5,4},{4,5},{7,6},{6,7},{9,8},{8,9},{11,10... | collective-permute-start | bytes 1867784 | tf_op jit(solution)/shard_map/ppermute | solution.py:38
  28.6 15.1 %collective-permute-start.8 = (f32[16,16,128]{2,1,0:T(8,128)S(1)}, f32[16,16,128]{2,1,0:T(8,128)S(1)}, u32[]{:S(2)}, u32[]{:S(2)}) collective-permute-start(f32[16,16,128]{2,1,0:T(8,128)S(1)} %pad_maximum_fusion.1), channel_id=1, source_target_pairs={{4,0},{5,1},{6,2},{7,3},{0,4},{1,5},{2,6},{3,7},{12,8},{13,9},{14,... | collective-permute-start | bytes 393224 | tf_op jit(solution)/shard_map/ppermute | solution.py:38
  28.7 16.4 %collective-permute-start.6 = (bf16[2,19,16,512]{3,2,1,0:T(8,128)(2,1)S(1)}, bf16[2,19,16,512]{3,2,1,0:T(8,128)(2,1)S(1)}, u32[]{:S(2)}, u32[]{:S(2)}) collective-permute-start(bf16[2,19,16,512]{3,2,1,0:T(8,128)(2,1)S(1)} %shard_map.78.near1), channel_id=1, source_target_pairs={{3,1},{0,2},{5,3},{2,4},{7,5},{4,6},{9,7},{6,8},{11,9},{8,10},{13,... | collective-permute-start | bytes 1867784 | tf_op jit(solution)/shard_map/ppermute | solution.py:38
  45.2 20.4 %copy-start = (bf16[8,1024,128]{2,1,0:T(8,128)(2,1)S(1)}, bf16[8,1024,128]{2,1,0:T(8,128)(2,1)}, u32[]{:S(2)}) copy-start(bf16[8,1024,128]{2,1,0:T(8,128)(2,1)} %basis.1) | copy-start | bytes 6291460
  45.2 20.4 %copy-start.3 = (f32[4,3,128,128]{3,2,1,0:T(8,128)S(1)}, f32[4,3,128,128]{3,2,1,0:T(8,128)}, u32[]{:S(2)}) copy-start(f32[4,3,128,128]{3,2,1,0:T(8,128)} %coupling.1) | copy-start | bytes 2359300
  45.2 20.4 %copy-start.4 = (f32[4,2,128,128]{3,2,1,0:T(8,128)S(1)}, f32[4,2,128,128]{3,2,1,0:T(8,128)}, u32[]{:S(2)}) copy-start(f32[4,2,128,128]{3,2,1,0:T(8,128)} %transfer.1) | copy-start | bytes 1572868
  45.2 20.4 %collective-permute-start.9 = (bf16[1,19,16,512]{3,2,1,0:T(8,128)(2,1)S(1)}, bf16[1,19,16,512]{3,2,1,0:T(8,128)(2,1)S(1)}, u32[]{:S(2)}, u32[]{:S(2)}) collective-permute-start(bf16[1,19,16,512]{3,2,1,0:T(8,128)(2,1)S(1)} %shard_map.80), channel_id=1, source_target_pairs={{1,0},{0,1},{3,2},{2,3},{5,4},{4,5},{7,6},{6,7},{9,8},{8,9},{11,10... | collective-permute-start | bytes 933896 | tf_op jit(solution)/shard_map/ppermute | solution.py:38
